TPU v7x, 32 devices: a whole 2x2x4 slice. The times are simulated.
32 devices in a mesh: dp: 8 (over z, x), fsdp: 4 (over y, core).
Axes of the slice: x: 2, y: 2, z: 4, core: 2. Of those that a mesh axis runs over, the one named last changes fastest.
Arguments:
- projection_input: bfloat16 [4096, 7168], P(('dp', 'fsdp')), may hold values from -6 to 6
- value_cotangent: bfloat16 [4096, 512], P(('dp', 'fsdp')), may hold values from -6 to 6
- value_weight: bfloat16 [7168, 512], P('fsdp'), may hold values from -0.0625 to 0.0625
- adapter_down_table: bfloat16 [40, 16, 7168], P('dp', None, 'fsdp'), may hold values from -0.0625 to 0.0625
- adapter_up_table: bfloat16 [40, 16, 512], P('dp', None, 'fsdp'), may hold values from -0.25 to 0.25
- adapter_per_block: int32 [32], replicated, may hold values from 0 to 39, as said below
- adapter_table_row: int32 [40], replicated, may hold values from 0 to 39, as said below
Outputs:
- grad_input: bfloat16 [4096, 7168], P(('dp', 'fsdp'))
- grad_down: float32 [40, 16, 7168], P('dp', None, 'fsdp')
- grad_up: float32 [40, 16, 512], P('dp', None, 'fsdp')
Inputs may be any that keep to these rules, and one draw needn't show every extreme that they name: adapter_table_row is a permutation: adapter a's factors are row adapter_table_row[a] of the tables, and row r lies on index r // 5 of dp. `adapter_per_block`: among the 4 blocks of one index of dp, all blocks whose adapters lie on the same index of dp name the same adapter.
All inputs are finite; a program needn't handle non-finite values.
Results may differ from a plain program's by a relative error of at most 0.0032.
Values may be sent and summed in bfloat16 or wider, within the bound.
No kernel may reach another device: no remote copies, remote signals or barrier semaphores. Data moves between devices by JAX's collectives and lax.ppermute only.
A program may use at most 64 MiB of HBM per device.

v0:
```python
import jax
import jax.numpy as jnp
from jax import lax
from jax.sharding import PartitionSpec as P

BLOCK = 128


adapter_scale = 2.0


def one_hot(indices, count, dtype):
    return (indices[:, None] == jnp.arange(count, dtype=jnp.int32)[None, :]).astype(dtype)


def per_device(
    projection_input,
    value_cotangent,
    value_weight,
    adapter_down_table,
    adapter_up_table,
    adapter_per_block,
    adapter_table_row,
):
    dp_count = lax.axis_size("dp")
    fsdp_count = lax.axis_size("fsdp")
    dp_index = lax.axis_index("dp")
    tok_rows = projection_input.shape[0]
    table_row_count = adapter_down_table.shape[0]
    rank_width = adapter_down_table.shape[1]
    input_feature_part = adapter_down_table.shape[2]
    value_feature_part = adapter_up_table.shape[2]
    blk_local = tok_rows // BLOCK
    group_blocks = blk_local * fsdp_count
    table_rows = adapter_table_row[adapter_per_block]
    owner_grid = (table_rows // table_row_count).reshape(dp_count, group_blocks)
    local_grid = (table_rows % table_row_count).reshape(dp_count, group_blocks)
    owner_ids = jnp.arange(dp_count, dtype=jnp.int32)
    matched = owner_grid[:, :, None] == owner_ids[None, None, :]
    need_slot = jnp.max(jnp.where(matched, local_grid[:, :, None], 0), axis=1)
    wanted = lax.dynamic_index_in_dim(need_slot, dp_index, 1, keepdims=False)
    slot_onehot = one_hot(wanted, table_row_count, jnp.bfloat16)
    send_down = jnp.dot(
        slot_onehot,
        adapter_down_table.reshape(table_row_count, rank_width * input_feature_part),
        preferred_element_type=jnp.float32,
    ).astype(jnp.bfloat16)
    send_up = jnp.dot(
        slot_onehot,
        adapter_up_table.reshape(table_row_count, rank_width * value_feature_part),
        preferred_element_type=jnp.float32,
    ).astype(jnp.bfloat16)
    owner_down, owner_up = (
        lax.all_to_all(send_down, "dp", split_axis=0, concat_axis=0, tiled=True),
        lax.all_to_all(send_up, "dp", split_axis=0, concat_axis=0, tiled=True),
    )
    my_owners = lax.dynamic_index_in_dim(owner_grid, dp_index, 0, keepdims=False)
    select = one_hot(my_owners, dp_count, jnp.bfloat16)
    share_down = jnp.dot(select, owner_down, preferred_element_type=jnp.float32).astype(
        jnp.bfloat16
    )
    share_up = jnp.dot(select, owner_up, preferred_element_type=jnp.float32).astype(jnp.bfloat16)
    full_down, full_up = (
        lax.all_to_all(share_down, "fsdp", split_axis=0, concat_axis=0, tiled=True),
        lax.all_to_all(share_up, "fsdp", split_axis=0, concat_axis=0, tiled=True),
    )
    down_four = full_down.reshape(fsdp_count, blk_local, rank_width, input_feature_part)
    up_four = full_up.reshape(fsdp_count, blk_local, rank_width, value_feature_part)
    x_blocks = projection_input.reshape(blk_local, BLOCK, fsdp_count, input_feature_part)
    dy_blocks = value_cotangent.reshape(blk_local, BLOCK, fsdp_count, value_feature_part)
    rank_activations = jnp.einsum(
        "ltkd,klrd->ltr", x_blocks, down_four, preferred_element_type=jnp.float32
    ).astype(jnp.bfloat16)
    rank_backward = (
        adapter_scale
        * jnp.einsum("ltkc,klrc->ltr", dy_blocks, up_four, preferred_element_type=jnp.float32)
    ).astype(jnp.bfloat16)
    adapter_term = jnp.einsum(
        "ltr,klrd->ltkd", rank_backward, down_four, preferred_element_type=jnp.float32
    ).reshape(tok_rows, fsdp_count * input_feature_part)
    frozen_term = jnp.einsum(
        "tc,dc->td",
        value_cotangent,
        lax.all_gather(value_weight, "fsdp", axis=0, tiled=True),
        preferred_element_type=jnp.float32,
    )
    grad_input = (frozen_term + adapter_term).astype(jnp.bfloat16)
    part_down = jnp.einsum(
        "ltr,ltkd->lkrd", rank_backward, x_blocks, preferred_element_type=jnp.float32
    ).reshape(blk_local, fsdp_count, rank_width * input_feature_part)
    part_up = (
        adapter_scale
        * jnp.einsum(
            "ltr,ltkc->lkrc", rank_activations, dy_blocks, preferred_element_type=jnp.float32
        )
    ).reshape(blk_local, fsdp_count, rank_width * value_feature_part)
    got_down, got_up = (
        lax.all_to_all(part_down, "fsdp", split_axis=1, concat_axis=0, tiled=True),
        lax.all_to_all(part_up, "fsdp", split_axis=1, concat_axis=0, tiled=True),
    )
    select_float = select.astype(jnp.float32)
    owner_sum_down = jnp.einsum(
        "bo,bx->ox",
        select_float,
        got_down.reshape(group_blocks, rank_width * input_feature_part),
        precision=lax.Precision.HIGHEST,
    )
    owner_sum_up = jnp.einsum(
        "bo,bx->ox",
        select_float,
        got_up.reshape(group_blocks, rank_width * value_feature_part),
        precision=lax.Precision.HIGHEST,
    )
    arrived_down, arrived_up = (
        lax.all_to_all(owner_sum_down, "dp", split_axis=0, concat_axis=0, tiled=True),
        lax.all_to_all(owner_sum_up, "dp", split_axis=0, concat_axis=0, tiled=True),
    )
    slot_float = slot_onehot.astype(jnp.float32)
    total_down = jnp.einsum("gs,gx->sx", slot_float, arrived_down, precision=lax.Precision.HIGHEST)
    total_up = jnp.einsum("gs,gx->sx", slot_float, arrived_up, precision=lax.Precision.HIGHEST)
    my_rows = dp_index * table_row_count + jnp.arange(table_row_count, dtype=jnp.int32)
    counts = jnp.sum((table_rows[None, :] == my_rows[:, None]).astype(jnp.int32), axis=1)
    divisor = jnp.maximum(counts, 1).astype(jnp.float32)
    grad_down = (total_down / divisor[:, None]).reshape(
        table_row_count, rank_width, input_feature_part
    )
    grad_up = (total_up / divisor[:, None]).reshape(table_row_count, rank_width, value_feature_part)
    return (grad_input, grad_down, grad_up)


def solution(mesh):
    return jax.shard_map(
        per_device,
        mesh=mesh,
        in_specs=(
            P(("dp", "fsdp"), None),
            P(("dp", "fsdp"), None),
            P("fsdp", None),
            P("dp", None, "fsdp"),
            P("dp", None, "fsdp"),
            P(),
            P(),
        ),
        out_specs=(P(("dp", "fsdp"), None), P("dp", None, "fsdp"), P("dp", None, "fsdp")),
        check_vma=False,
    )
```

profile of v0, /device:TPU:0, one launch (start us, length us, event | category | flops | bytes accessed | tf_op | source)
XLA Modules:
  0.0 139.8 jit_solution(4269094409666220113)
XLA Ops:
  7.2 0.0 copy-start
  7.2 0.0 copy-start.5
  7.2 0.0 copy-start.1
  7.2 0.0 all-gather.2.cloned.1.call-start
  7.3 0.7 all-gather.2.cloned.1.call-update
  8.0 0.0 copy-done.5
  8.0 0.7 gather_fusion
  8.7 0.1 div.31
  8.8 0.1 ne.42
  8.9 0.1 rem.27
  9.0 0.1 copy.59
  9.1 0.1 copy.58
  9.2 0.1 select_reduce_fusion
  9.3 0.2 dynamic-slice_reduce_fusion
  9.4 0.2 fusion.3
  9.6 0.5 broadcast.81
  10.2 0.7 reduce.4
  10.8 0.6 reshape.171
  11.4 7.3 %all-to-all-start = ((bf16[8,2,1024]{2,1,0:T(2,128)(2,1)}), bf16[8,2,1024]{2,1,0:T(2,128)(2,1)S(1)}, u32[]{:S(2)}, u32[]{:S(2)}) async-start(bf16[8,2,1024]{2,1,0:T(2,128)(2,1)} %reshape.171), calls=%async_computation | async-start | bytes 65536 | tf_op jit(solution)/shard_map/all_to_all | solution.py:55
  18.7 0.1 copy.84
  18.8 6.5 %all-to-all-done = bf16[8,2,1024]{2,1,0:T(2,128)(2,1)S(1)} async-done(((bf16[8,2,1024]{2,1,0:T(2,128)(2,1)}), bf16[8,2,1024]{2,1,0:T(2,128)(2,1)S(1)}, u32[]{:S(2)}, u32[]{:S(2)}) %all-to-all-start) | async-done | bytes 32800 | tf_op jit(solution)/shard_map/all_to_all | solution.py:55
  25.4 0.2 fusion.4
  25.6 0.7 reduce.5
  26.3 0.6 reshape.173
  26.9 3.3 %all-to-all-start.1 = ((bf16[4,2,1024]{2,1,0:T(2,128)(2,1)}), bf16[4,2,1024]{2,1,0:T(2,128)(2,1)S(1)}, u32[]{:S(2)}, u32[]{:S(2)}) async-start(bf16[4,2,1024]{2,1,0:T(2,128)(2,1)} %reshape.173), calls=%async_computation.1 | async-start | bytes 32768 | tf_op jit(solution)/shard_map/all_to_all | solution.py:65
  30.2 0.3 fusion
  30.5 1.0 reduce.6
  31.5 1.1 reshape.175
  32.6 1.6 %all-to-all-done.1 = bf16[4,2,1024]{2,1,0:T(2,128)(2,1)S(1)} async-done(((bf16[4,2,1024]{2,1,0:T(2,128)(2,1)}), bf16[4,2,1024]{2,1,0:T(2,128)(2,1)S(1)}, u32[]{:S(2)}, u32[]{:S(2)}) %all-to-all-start.1) | async-done | bytes 16416 | tf_op jit(solution)/shard_map/all_to_all | solution.py:65
  34.1 3.5 %all-to-all-start.2 = ((bf16[8,2,14336]{2,1,0:T(2,128)(2,1)}), bf16[8,2,14336]{2,1,0:T(2,128)(2,1)S(1)}, u32[]{:S(2)}, u32[]{:S(2)}) async-start(bf16[8,2,14336]{2,1,0:T(2,128)(2,1)} %reshape.175), calls=%async_computation.2 | async-start | bytes 917504 | tf_op jit(solution)/shard_map/all_to_all | solution.py:54
  37.6 0.1 reduce.1
  37.7 13.4 %all-to-all-done.2 = bf16[8,2,14336]{2,1,0:T(2,128)(2,1)S(1)} async-done(((bf16[8,2,14336]{2,1,0:T(2,128)(2,1)}), bf16[8,2,14336]{2,1,0:T(2,128)(2,1)S(1)}, u32[]{:S(2)}, u32[]{:S(2)}) %all-to-all-start.2) | async-done | bytes 458784 | tf_op jit(solution)/shard_map/all_to_all | solution.py:54
  51.2 0.5 reshape.176
  51.6 0.0 copy-start.2
  51.6 0.6 fusion.1
  52.2 0.9 reduce.7
  53.2 1.0 reshape.177
  54.1 3.4 %all-to-all-start.3 = ((bf16[4,2,14336]{2,1,0:T(2,128)(2,1)}), bf16[4,2,14336]{2,1,0:T(2,128)(2,1)S(1)}, u32[]{:S(2)}, u32[]{:S(2)}) async-start(bf16[4,2,14336]{2,1,0:T(2,128)(2,1)} %reshape.177), calls=%async_computation.3 | async-start | bytes 458752 | tf_op jit(solution)/shard_map/all_to_all | solution.py:64
  57.5 0.1 fusion.15
  57.7 7.9 %all-to-all-done.3 = bf16[4,2,14336]{2,1,0:T(2,128)(2,1)S(1)} async-done(((bf16[4,2,14336]{2,1,0:T(2,128)(2,1)}), bf16[4,2,14336]{2,1,0:T(2,128)(2,1)S(1)}, u32[]{:S(2)}, u32[]{:S(2)}) %all-to-all-start.3) | async-done | bytes 229408 | tf_op jit(solution)/shard_map/all_to_all | solution.py:64
  65.6 0.2 reshape.178
  65.8 1.5 %reduce.2 = bf16[4,28672]{1,0:T(4,128)(2,1)S(1)} reduce(bf16[4,1,28672]{2,1,0:T(2,128)(2,1)S(1)} %reshape.178, bf16[]{:T(256)} %constant.48), dimensions={1}, to_apply=%all_to_all.67.reduce_sub_computation | reduce | bytes 458754 | tf_op jit(solution)/shard_map/all_to_all | solution.py:64
  67.3 1.4 convolution_multiply_fusion
  68.7 3.3 %all-to-all-start.6 = ((f32[1,4,2048]{2,0,1:T(1,128)}), f32[1,4,2048]{2,0,1:T(1,128)S(1)}, u32[]{:S(2)}, u32[]{:S(2)}) async-start(f32[1,4,2048]{2,0,1:T(1,128)} %bitcast.17), calls=%async_computation.6 | async-start | bytes 65536 | tf_op jit(solution)/shard_map/all_to_all | solution.py:99
  71.9 0.4 convolution_bitcast_fusion.1
  72.3 1.2 reshape.167
  73.5 2.3 %all-to-all-done.6 = f32[1,4,2048]{2,0,1:T(1,128)S(1)} async-done(((f32[1,4,2048]{2,0,1:T(1,128)}), f32[1,4,2048]{2,0,1:T(1,128)S(1)}, u32[]{:S(2)}, u32[]{:S(2)}) %all-to-all-start.6) | async-done | bytes 32800 | tf_op jit(solution)/shard_map/all_to_all | solution.py:99
  75.9 3.5 %all-to-all-start.4 = ((f32[1,4,28672]{2,0,1:T(1,128)}), f32[1,4,28672]{2,0,1:T(1,128)S(1)}, u32[]{:S(2)}, u32[]{:S(2)}) async-start(f32[1,4,28672]{2,0,1:T(1,128)} %reshape.167), calls=%async_computation.4 | async-start | bytes 917504 | tf_op jit(solution)/shard_map/all_to_all | solution.py:98
  79.3 0.3 convolution_bitcast_fusion.2
  79.6 0.7 copy.72
  80.3 7.1 %all-to-all-done.4 = f32[1,4,28672]{2,0,1:T(1,128)S(1)} async-done(((f32[1,4,28672]{2,0,1:T(1,128)}), f32[1,4,28672]{2,0,1:T(1,128)S(1)}, u32[]{:S(2)}, u32[]{:S(2)}) %all-to-all-start.4) | async-done | bytes 458784 | tf_op jit(solution)/shard_map/all_to_all | solution.py:98
  87.4 4.0 %all-to-all-start.7 = ((f32[8,1,2048]{2,1,0:T(1,128)}), f32[8,1,2048]{2,1,0:T(1,128)S(1)}, u32[]{:S(2)}, u32[]{:S(2)}) async-start(f32[8,1,2048]{2,1,0:T(1,128)} %copy.72), calls=%async_computation.7 | async-start | bytes 131072 | tf_op jit(solution)/shard_map/all_to_all | solution.py:116
  91.4 0.9 convolution_bitcast_fusion
  92.4 1.9 %copy.68 = f32[8,1,28672]{2,1,0:T(1,128)} copy(f32[8,1,28672]{2,0,1:T(8,128)S(1)} %convolution_bitcast_fusion) | data formatting | bytes 1835008 | tf_op jit(solution)/shard_map/all_to_all | solution.py:115
  94.2 4.1 %all-to-all-done.7 = f32[8,1,2048]{2,1,0:T(1,128)S(1)} async-done(((f32[8,1,2048]{2,1,0:T(1,128)}), f32[8,1,2048]{2,1,0:T(1,128)S(1)}, u32[]{:S(2)}, u32[]{:S(2)}) %all-to-all-start.7) | async-done | bytes 65568 | tf_op jit(solution)/shard_map/all_to_all | solution.py:116
  98.3 3.7 %all-to-all-start.5 = ((f32[8,1,28672]{2,1,0:T(1,128)}), f32[8,1,28672]{2,1,0:T(1,128)S(1)}, u32[]{:S(2)}, u32[]{:S(2)}) async-start(f32[8,1,28672]{2,1,0:T(1,128)} %copy.68), calls=%async_computation.5 | async-start | bytes 1835008 | tf_op jit(solution)/shard_map/all_to_all | solution.py:115
  102.1 0.2 convert_reduce_fusion
  102.3 0.3 fusion.10
  102.6 0.6 copy.154
  103.3 20.2 %all-to-all-done.5 = f32[8,1,28672]{2,1,0:T(1,128)S(1)} async-done(((f32[8,1,28672]{2,1,0:T(1,128)}), f32[8,1,28672]{2,1,0:T(1,128)S(1)}, u32[]{:S(2)}, u32[]{:S(2)}) %all-to-all-start.5) | async-done | bytes 917536 | tf_op jit(solution)/shard_map/all_to_all | solution.py:115
  123.4 1.1 convolution_divide_fusion
  124.6 1.0 copy.152
  125.6 5.6 %fusion.57 = f32[128,7168]{1,0:T(8,128)S(1)} fusion(bf16[128,512]{1,0:T(8,128)(2,1)S(1)} %copy-done, bf16[7168,512]{1,0:T(8,128)(2,1)} %all-gather.2.cloned.1.call-done), kind=kOutput, calls=%fused_computation.80 | convolution fusion | flops 939524096 | bytes 11141120 | tf_op jit(solution)/shard_map/tc,dc->td/dot_general | solution.py:81
  131.1 1.9 %fusion.2 = bf16[128,7168]{1,0:T(8,128)(2,1)} fusion(f32[128,7168]{1,0:T(8,128)S(1)} %fusion.57, bf16[16,128]{1,0:T(8,128)(2,1)S(1)} %fusion.15, bf16[7168,16]{0,1:T(8,128)(2,1)S(1)} %bitcast.137), kind=kOutput, calls=%fused_computation.8 | convolution fusion | flops 31195136 | bytes 5738496 | tf_op jit(solution)/shard_map/ltr,klrd->ltkd/dot_general | solution.py:78
  (20 shorter events, 0.2 us)
Async XLA Ops:
  7.2 50.4 %copy-start = (bf16[128,512]{1,0:T(8,128)(2,1)S(1)}, bf16[128,512]{1,0:T(8,128)(2,1)}, u32[]{:S(2)}) copy-start(bf16[128,512]{1,0:T(8,128)(2,1)} %param.8) | copy-start | bytes 393220
  7.2 0.8 copy-start.5
  7.2 0.8 copy-start.1
  7.2 2.2 %copy-start.4 = (bf16[5,16,128]{2,1,0:T(8,128)(2,1)S(1)}, bf16[5,16,128]{2,1,0:T(8,128)(2,1)}, u32[]{:S(2)}) copy-start(bf16[5,16,128]{2,1,0:T(8,128)(2,1)} %param.11) | copy-start | bytes 61444
  7.2 11.5 %copy-start.3 = (bf16[5,16,1792]{2,1,0:T(8,128)(2,1)S(1)}, bf16[5,16,1792]{2,1,0:T(8,128)(2,1)}, u32[]{:S(2)}) copy-start(bf16[5,16,1792]{2,1,0:T(8,128)(2,1)} %param.10) | copy-start | bytes 860164
  7.2 118.3 %all-gather.2.cloned.1.call-start = ((), (), s32[]{:S(2)}) async-start(), calls=%async_computation.8 | async-start | bytes 9175040 | tf_op jit(solution)/shard_map/all_gather | solution.py:84
  11.4 13.9 %all-to-all-start = ((bf16[8,2,1024]{2,1,0:T(2,128)(2,1)}), bf16[8,2,1024]{2,1,0:T(2,128)(2,1)S(1)}, u32[]{:S(2)}, u32[]{:S(2)}) async-start(bf16[8,2,1024]{2,1,0:T(2,128)(2,1)} %reshape.171), calls=%async_computation | async-start | bytes 65536 | tf_op jit(solution)/shard_map/all_to_all | solution.py:55
  26.9 7.2 %all-to-all-start.1 = ((bf16[4,2,1024]{2,1,0:T(2,128)(2,1)}), bf16[4,2,1024]{2,1,0:T(2,128)(2,1)S(1)}, u32[]{:S(2)}, u32[]{:S(2)}) async-start(bf16[4,2,1024]{2,1,0:T(2,128)(2,1)} %reshape.173), calls=%async_computation.1 | async-start | bytes 32768 | tf_op jit(solution)/shard_map/all_to_all | solution.py:65
  34.1 17.0 %all-to-all-start.2 = ((bf16[8,2,14336]{2,1,0:T(2,128)(2,1)}), bf16[8,2,14336]{2,1,0:T(2,128)(2,1)S(1)}, u32[]{:S(2)}, u32[]{:S(2)}) async-start(bf16[8,2,14336]{2,1,0:T(2,128)(2,1)} %reshape.175), calls=%async_computation.2 | async-start | bytes 917504 | tf_op jit(solution)/shard_map/all_to_all | solution.py:54
  51.6 15.7 %copy-start.2 = (bf16[128,7168]{1,0:T(8,128)(2,1)S(1)}, bf16[128,7168]{1,0:T(8,128)(2,1)}, u32[]{:S(2)}) copy-start(bf16[128,7168]{1,0:T(8,128)(2,1)} %param.7) | copy-start | bytes 5505028
  54.1 11.4 %all-to-all-start.3 = ((bf16[4,2,14336]{2,1,0:T(2,128)(2,1)}), bf16[4,2,14336]{2,1,0:T(2,128)(2,1)S(1)}, u32[]{:S(2)}, u32[]{:S(2)}) async-start(bf16[4,2,14336]{2,1,0:T(2,128)(2,1)} %reshape.177), calls=%async_computation.3 | async-start | bytes 458752 | tf_op jit(solution)/shard_map/all_to_all | solution.py:64
  68.7 7.2 %all-to-all-start.6 = ((f32[1,4,2048]{2,0,1:T(1,128)}), f32[1,4,2048]{2,0,1:T(1,128)S(1)}, u32[]{:S(2)}, u32[]{:S(2)}) async-start(f32[1,4,2048]{2,0,1:T(1,128)} %bitcast.17), calls=%async_computation.6 | async-start | bytes 65536 | tf_op jit(solution)/shard_map/all_to_all | solution.py:99
  75.9 11.6 %all-to-all-start.4 = ((f32[1,4,28672]{2,0,1:T(1,128)}), f32[1,4,28672]{2,0,1:T(1,128)S(1)}, u32[]{:S(2)}, u32[]{:S(2)}) async-start(f32[1,4,28672]{2,0,1:T(1,128)} %reshape.167), calls=%async_computation.4 | async-start | bytes 917504 | tf_op jit(solution)/shard_map/all_to_all | solution.py:98
  87.4 10.9 %all-to-all-start.7 = ((f32[8,1,2048]{2,1,0:T(1,128)}), f32[8,1,2048]{2,1,0:T(1,128)S(1)}, u32[]{:S(2)}, u32[]{:S(2)}) async-start(f32[8,1,2048]{2,1,0:T(1,128)} %copy.72), calls=%async_computation.7 | async-start | bytes 131072 | tf_op jit(solution)/shard_map/all_to_all | solution.py:116
  98.3 25.1 %all-to-all-start.5 = ((f32[8,1,28672]{2,1,0:T(1,128)}), f32[8,1,28672]{2,1,0:T(1,128)S(1)}, u32[]{:S(2)}, u32[]{:S(2)}) async-start(f32[8,1,28672]{2,1,0:T(1,128)} %copy.68), calls=%async_computation.5 | async-start | bytes 1835008 | tf_op jit(solution)/shard_map/all_to_all | solution.py:115
Sparse Core Ops, SparseCore 0:
  9.6 57.5 all-gather.1
where the time goes:
time: 141 us; the launch traced here: 140 us
  waiting for transfers between devices  63.8 us (45%)
  starting transfers between devices  31.9 us (23%)
  between operations  14.4 us (10%)
  matrix products  13.2 us (9%)
  local copies, waits for them, and re-layouts  11.5 us (8%)
  other arithmetic  5.09 us (4%)
    all_to_all x1, waiting for transfers between devices, per_device(): lax.all_to_all(owner_sum_down, 'dp', split_axis=0, concat_axis=0, tiled=T...  20.2 us
    all_to_all x1, waiting for transfers between devices, per_device(): lax.all_to_all(send_down, 'dp', split_axis=0, concat_axis=0, tiled=True)  13.4 us
    all_to_all x1, waiting for transfers between devices, per_device(): lax.all_to_all(share_down, 'fsdp', split_axis=0, concat_axis=0, tiled=True)  7.91 us
    all_to_all x1, starting transfers between devices, per_device(): lax.all_to_all(send_up, 'dp', split_axis=0, concat_axis=0, tiled=True)  7.25 us
    all_to_all x1, waiting for transfers between devices, per_device(): lax.all_to_all(part_down, 'fsdp', split_axis=1, concat_axis=0, tiled=True)  7.12 us
    all_to_all x1, waiting for transfers between devices, per_device(): lax.all_to_all(send_up, 'dp', split_axis=0, concat_axis=0, tiled=True)  6.55 us
    unnamed x24, local copies, waits for them, and re-layouts  5.83 us
    dot_general x1, matrix products, per_device(): jnp.einsum('tc,dc->td', value_cotangent, lax.all_gather(value_weight, 'fs...  5.55 us
  transfers between devices with their start and end apart: 9, of which 8 were waited for; matrix products, arithmetic and copies ran while one was open for 16% of the time, Pallas kernels for 0%

commit v1 on v0

v1 whole, which is shorter than its diff:
```python
import functools

import jax
import jax.numpy as jnp
from jax import lax
from jax.experimental import pallas as pl
from jax.experimental.pallas import tpu as pltpu
from jax.sharding import PartitionSpec as P

BLOCK = 128
LANES = 128
adapter_scale = 2.0

SMEM = pl.BlockSpec(memory_space=pltpu.SMEM)
VMEM = pl.BlockSpec(memory_space=pltpu.VMEM)
NT = (((1,), (1,)), ((), ()))


def round_up(n):
    return -(-n // LANES) * LANES


def dot(a, b, dims=(((1,), (0,)), ((), ()))):
    return lax.dot_general(a, b, dims, preferred_element_type=jnp.float32)


def pick_kernel(group_blocks, me_ref, apb_ref, row_ref, down_ref, up_ref, send_ref, want_ref, count_ref):
    slots, _, down_part = down_ref.shape
    up_part = up_ref.shape[2]
    up_at = round_up(down_part)
    groups = send_ref.shape[0]
    first = me_ref[0] * slots
    for s in range(slots):
        count_ref[s] = 0

    def group(g, carry):
        want_ref[g] = 0
        for j in range(group_blocks):
            local = row_ref[apb_ref[g * group_blocks + j]] - first

            @pl.when((local >= 0) & (local < slots))
            def _():
                want_ref[g] = local
                count_ref[local] = count_ref[local] + 1

        slot = want_ref[g]
        send_ref[g, :, :down_part] = down_ref[slot]
        send_ref[g, :, up_at : up_at + up_part] = up_ref[slot]
        return carry

    lax.fori_loop(0, groups, group, 0)


def share_kernel(slots, me_ref, apb_ref, row_ref, got_ref, out_ref):
    blocks = out_ref.shape[0]
    for j in range(blocks):
        owner = lax.div(row_ref[apb_ref[me_ref[0] * blocks + j]], slots)
        out_ref[j] = got_ref[owner]


def block_kernel(down_part, up_part, x_ref, dy_ref, fac_ref, grads_ref, back_ref):
    shares = fac_ref.shape[0]
    up_at = round_up(down_part)
    low_t = jnp.zeros((fac_ref.shape[1], BLOCK), jnp.float32)
    back_t = jnp.zeros((fac_ref.shape[1], BLOCK), jnp.float32)
    for k in range(shares):
        back_t += dot(
            fac_ref[k, :, up_at : up_at + up_part],
            dy_ref[:, k * up_part : (k + 1) * up_part],
            NT,
        )
        low_t += dot(
            fac_ref[k, :, :down_part], x_ref[:, k * down_part : (k + 1) * down_part], NT
        )
    low = low_t.astype(jnp.bfloat16)
    scaled = adapter_scale * back_t
    back = scaled.astype(jnp.bfloat16)
    back_ref[...] = scaled.T.astype(jnp.bfloat16)
    for k in range(shares):
        grads_ref[k, :, :down_part] = dot(
            back, x_ref[:, k * down_part : (k + 1) * down_part]
        ).astype(jnp.bfloat16)
        grads_ref[k, :, up_at : up_at + up_part] = (
            adapter_scale * dot(low, dy_ref[:, k * up_part : (k + 1) * up_part])
        ).astype(jnp.bfloat16)


def owner_kernel(slots, me_ref, apb_ref, row_ref, got_ref, out_ref, acc_ref):
    blocks = got_ref.shape[0]
    acc_ref[...] = jnp.zeros_like(acc_ref)
    for j in range(blocks):
        owner = lax.div(row_ref[apb_ref[me_ref[0] * blocks + j]], slots)
        acc_ref[owner] += got_ref[j].astype(jnp.float32)
    out_ref[...] = acc_ref[...].astype(jnp.bfloat16)


def total_kernel(want_ref, count_ref, got_ref, down_ref, up_ref):
    slots, _, down_part = down_ref.shape
    up_part = up_ref.shape[2]
    up_at = round_up(down_part)
    down_ref[...] = jnp.zeros_like(down_ref)
    up_ref[...] = jnp.zeros_like(up_ref)

    def group(g, carry):
        slot = want_ref[g]
        down_ref[slot] += got_ref[g, :, :down_part].astype(jnp.float32)
        up_ref[slot] += got_ref[g, :, up_at : up_at + up_part].astype(jnp.float32)
        return carry

    lax.fori_loop(0, got_ref.shape[0], group, 0)
    for s in range(slots):
        divisor = jnp.maximum(count_ref[s], 1).astype(jnp.float32)
        down_ref[s] = down_ref[s] / divisor
        up_ref[s] = up_ref[s] / divisor


def input_kernel(half, *refs):
    place_ref, dy_ref, back_ref, fac_ref = refs[:4]
    weights = refs[4:8]
    out_ref, buf, sems = refs[-3:]
    k = pl.program_id(0)
    rows = buf.shape[1]
    copies = [pltpu.make_async_copy(weights[i], buf.at[i], sems.at[i]) for i in range(4)]
    for i in range(4):

        @pl.when(k == 0)
        def _():
            copies[i].start()

    for i in range(4):

        @pl.when(k == i)
        def _():
            copies[i].wait()

    out_ref[...] = (
        dot(dy_ref[...], buf[k], NT)
        + dot(back_ref[...], fac_ref[place_ref[k], :, half * rows : (half + 1) * rows])
    ).astype(jnp.bfloat16)


def input_half(half, place, dy, back, factors, weights, out, width):
    rows, features = weights[0].shape
    operands = [dy, back, factors, *weights]
    whole = [
        pl.BlockSpec(a.shape, functools.partial(lambda n, *_: (0,) * n, a.ndim))
        for a in operands[:3]
    ]
    specs = whole + [pl.BlockSpec(memory_space=pl.ANY)] * 4
    aliases = {}
    if out is not None:
        operands.append(out)
        specs.append(pl.BlockSpec(memory_space=pl.ANY))
        aliases = {len(operands): 0}
    return pl.pallas_call(
        functools.partial(input_kernel, half),
        grid_spec=pltpu.PrefetchScalarGridSpec(
            num_scalar_prefetch=1,
            grid=(4,),
            in_specs=specs,
            out_specs=pl.BlockSpec((dy.shape[0], rows), lambda k, place: (0, 2 * place[k] + half)),
            scratch_shapes=[
                pltpu.VMEM((4, rows, features), jnp.bfloat16),
                pltpu.SemaphoreType.DMA((4,)),
            ],
        ),
        out_shape=jax.ShapeDtypeStruct((dy.shape[0], width), jnp.bfloat16),
        input_output_aliases=aliases,
        compiler_params=pltpu.CompilerParams(vmem_limit_bytes=32 << 20),
        cost_estimate=pl.CostEstimate(
            flops=8 * dy.shape[0] * rows * features,
            bytes_accessed=8 * rows * features + 8 * dy.shape[0] * rows,
            transcendentals=0,
        ),
    )(place, *operands)


def call(kernel, out_shape, out_specs, *operands, smem=0, scratch=()):
    return pl.pallas_call(
        kernel,
        out_shape=out_shape,
        in_specs=[SMEM] * smem + [VMEM] * (len(operands) - smem),
        out_specs=out_specs,
        scratch_shapes=scratch,
        compiler_params=pltpu.CompilerParams(vmem_limit_bytes=32 << 20),
    )(*operands)


def per_device(
    projection_input,
    value_cotangent,
    value_weight,
    adapter_down_table,
    adapter_up_table,
    adapter_per_block,
    adapter_table_row,
):
    dp_count = lax.axis_size("dp")
    fsdp_count = lax.axis_size("fsdp")
    me = lax.axis_index("dp").reshape(1)
    at = lax.axis_index("fsdp")
    tok_rows, width = projection_input.shape
    slots, rank, down_part = adapter_down_table.shape
    up_part = adapter_up_table.shape[2]
    assert tok_rows == BLOCK
    wide = round_up(down_part) + round_up(up_part)
    bf16 = jnp.bfloat16

    def shaped(*shape, dtype=bf16):
        return jax.ShapeDtypeStruct(shape, dtype)

    by_permute = fsdp_count == 4 and value_weight.shape[0] % 256 == 0

    def cross(array, bit):
        return lax.ppermute(array, "fsdp", [(i, i ^ bit) for i in range(fsdp_count)])

    half_rows = value_weight.shape[0] // 2
    halves = [value_weight[:half_rows], value_weight[half_rows:]]

    def gather_half(own):
        far = cross(own, 2)
        return own, cross(own, 1), far, cross(far, 1)

    index = (me, adapter_per_block, adapter_table_row)
    send, want, count = call(
        functools.partial(pick_kernel, fsdp_count),
        (
            shaped(dp_count, rank, wide),
            shaped(dp_count, dtype=jnp.int32),
            shaped(slots, dtype=jnp.int32),
        ),
        (VMEM, SMEM, SMEM),
        *index,
        adapter_down_table,
        adapter_up_table,
        smem=3,
    )
    if by_permute:
        first = gather_half(halves[0])
    owned = lax.all_to_all(send, "dp", split_axis=0, concat_axis=0, tiled=True)
    share = call(
        functools.partial(share_kernel, slots),
        shaped(fsdp_count, rank, wide),
        VMEM,
        *index,
        owned,
        smem=3,
    )
    factors = lax.all_to_all(share, "fsdp", split_axis=0, concat_axis=0, tiled=True)
    grads, back = call(
        functools.partial(block_kernel, down_part, up_part),
        (shaped(fsdp_count, rank, wide), shaped(BLOCK, rank)),
        (VMEM, VMEM),
        projection_input,
        value_cotangent,
        factors,
    )
    got = lax.all_to_all(grads, "fsdp", split_axis=0, concat_axis=0, tiled=True)
    if by_permute:
        second_own, got = lax.optimization_barrier((halves[1], got))
        second = gather_half(second_own)
    sums = call(
        functools.partial(owner_kernel, slots),
        shaped(dp_count, rank, wide),
        VMEM,
        *index,
        got,
        smem=3,
        scratch=[pltpu.VMEM((dp_count, rank, wide), jnp.float32)],
    )
    arrived = lax.all_to_all(sums, "dp", split_axis=0, concat_axis=0, tiled=True)
    grad_down, grad_up = call(
        total_kernel,
        (
            shaped(slots, rank, down_part, dtype=jnp.float32),
            shaped(slots, rank, up_part, dtype=jnp.float32),
        ),
        (VMEM, VMEM),
        want,
        count,
        arrived,
        smem=2,
    )
    if by_permute:
        place = at ^ jnp.arange(4, dtype=jnp.int32)
        grad_input = None
        for half, weights in enumerate((first, second)):
            grad_input = input_half(
                half, place, value_cotangent, back, factors, weights, grad_input, width
            )
    else:
        weight = lax.all_gather(value_weight, "fsdp", axis=0, tiled=True)
        adapter_term = jnp.einsum(
            "tr,krd->tkd", back, factors[:, :, :down_part], preferred_element_type=jnp.float32
        )
        frozen_term = jnp.einsum(
            "tc,dc->td", value_cotangent, weight, preferred_element_type=jnp.float32
        )
        grad_input = (frozen_term + adapter_term.reshape(tok_rows, width)).astype(bf16)
    return (grad_input, grad_down, grad_up)


def solution(mesh):
    return jax.shard_map(
        per_device,
        mesh=mesh,
        in_specs=(
            P(("dp", "fsdp"), None),
            P(("dp", "fsdp"), None),
            P("fsdp", None),
            P("dp", None, "fsdp"),
            P("dp", None, "fsdp"),
            P(),
            P(),
        ),
        out_specs=(P(("dp", "fsdp"), None), P("dp", None, "fsdp"), P("dp", None, "fsdp")),
        check_vma=False,
    )
```

time: 141 us -> 112 us (0.79)
  blocking collectives: 0 us -> 29.3 us
  starting transfers between devices: 31.9 us -> 9.55 us
  Pallas kernels: 0 us -> 15.8 us
  between operations: 14.4 us -> 0.75 us
  matrix products: 13.2 us -> 0 us
  waiting for transfers between devices: 63.8 us -> 51.3 us
  local copies, waits for them, and re-layouts: 11.5 us -> 4.73 us
  other arithmetic: 5.09 us -> 0.01 us
    all_to_all x8 -> x2, waiting for transfers between devices: 63.1 us -> 12.8 us  [the longest x1 10.2 us: per_device(): lax.all_to_all(sums, 'dp', split_axis=0, concat_axis=0, tiled=True)]
    ppermute x0 -> x6, waiting for transfers between devices: none -> 38.4 us  [cross(): lax.ppermute(array, 'fsdp', [(i, i ^ bit) for i in range(fsdp_count)])]
    all_to_all x0 -> x2, blocking collectives: none -> 29.3 us  [the longest x1 20.9 us: per_device(): owned = lax.all_to_all(send, 'dp', split_axis=0, concat_axis=0, tiled=True)]
    all_to_all x8 -> x2, starting transfers between devices: 31.8 us -> 6.98 us  [the longest x1 3.59 us: per_device(): lax.all_to_all(sums, 'dp', split_axis=0, concat_axis=0, tiled=True)]
    pallas_call x0 -> x7, Pallas kernels: none -> 15.8 us  [the longest x2 8.67 us: input_half(): pl.pallas_call(functools.partial(input_kernel, half), grid_spec=pltpu.Pre...]
    dot_general x13 -> x0, matrix products: 13.2 us -> none  [the longest x1 5.55 us: per_device(): jnp.einsum('tc,dc->td', value_cotangent, lax.all_gather(value_weight, 'fs...]
    all_to_all x6 -> x0, other arithmetic: 4.76 us -> none  [the longest x2 2.38 us: per_device(): lax.all_to_all(share_down, 'fsdp', split_axis=0, concat_axis=0, tiled=True)]
    all_to_all x3 -> x0, local copies, waits for them, and re-layouts: 3.08 us -> none  [the longest x1 1.87 us: per_device(): lax.all_to_all(owner_sum_down, 'dp', split_axis=0, concat_axis=0, tiled=T...]
  transfers between devices with their start and end apart: 9 -> 8, of which waited for: 8 -> 4; matrix products, arithmetic and copies ran while one was open for 16% -> 1% of each run, Pallas kernels for 0% -> 7%
where the time goes in v1:
time: 112 us; the launch traced here: 111 us
  waiting for transfers between devices  51.3 us (46%)
  blocking collectives  29.3 us (26%)
  Pallas kernels  15.8 us (14%)
  starting transfers between devices  9.55 us (9%)
  local copies, waits for them, and re-layouts  4.73 us (4%)
    ppermute x6, waiting for transfers between devices, cross(): lax.ppermute(array, 'fsdp', [(i, i ^ bit) for i in range(fsdp_count)])  38.4 us
    all_to_all x1, blocking collectives, per_device(): owned = lax.all_to_all(send, 'dp', split_axis=0, concat_axis=0, tiled=True)  20.9 us
    all_to_all x1, waiting for transfers between devices, per_device(): lax.all_to_all(sums, 'dp', split_axis=0, concat_axis=0, tiled=True)  10.2 us
    pallas_call x2, Pallas kernels, input_half(): pl.pallas_call(functools.partial(input_kernel, half), grid_spec=pltpu.Pre...  8.67 us
    all_to_all x1, blocking collectives, per_device(): lax.all_to_all(share, 'fsdp', split_axis=0, concat_axis=0, tiled=True)  8.45 us
    pallas_call x5, Pallas kernels, call(): pl.pallas_call(kernel, out_shape=out_shape, in_specs=[SMEM] * smem + [VME...  7.14 us
    all_to_all x1, starting transfers between devices, per_device(): lax.all_to_all(sums, 'dp', split_axis=0, concat_axis=0, tiled=True)  3.59 us
    all_to_all x1, starting transfers between devices, per_device(): got = lax.all_to_all(grads, 'fsdp', split_axis=0, concat_axis=0, tiled=True)  3.4 us
  transfers between devices with their start and end apart: 8, of which 4 were waited for; matrix products, arithmetic and copies ran while one was open for 1% of the time, Pallas kernels for 7%

profile of v1, /device:TPU:0, one launch (start us, length us, event | category | flops | bytes accessed | tf_op | source)
XLA Modules:
  0.0 111.5 jit_solution(17247260911925148438)
XLA Ops:
  0.6 0.0 copy-start
  0.6 0.0 copy-start.1
  0.7 0.0 copy-start.2
  0.7 1.1 copy-done.2
  1.8 0.0 copy-start.3
  1.8 0.7 copy-done.3
  2.5 0.0 copy-start.4
  2.5 0.7 copy-done.4
  3.1 0.0 copy-start.6
  3.1 0.7 copy-done.6
  3.8 1.4 %shard_map.94 = (bf16[8,16,1920]{2,1,0:T(8,128)(2,1)S(1)}, s32[8]{0:T(128)S(1)}, s32[5]{0:T(128)S(1)}) custom-call(s32[1]{0:T(128)} %bitcast.me_ref, s32[32]{0:T(128)S(1)} %copy-done.4, s32[40]{0:T(128)S(1)} %copy-done.6, bf16[5,16,1792]{2,1,0:T(8,128)(2,1)S(1)} %copy-done.2, bf16[5,16,128]{2,1,0:T(8,128)(2,1)S(1)} %copy-done.3), custom_call_target="tpu_custom_call" | custom-call | tf_op jit(solution)/shard_map/pallas_call | solution.py:179
  5.2 20.9 %all_to_all.20.got_ref = bf16[8,16,1920]{2,1,0:T(8,128)(2,1)S(1)} all-to-all(bf16[8,16,1920]{2,1,0:T(8,128)(2,1)S(1)} %get-tuple-element.12), channel_id=1, replica_groups=mesh['dp'=8,'fsdp'=4] {'dp'}, dimensions={0} | all-to-all | bytes 983040 | tf_op jit(solution)/shard_map/all_to_all | solution.py:240
  26.1 0.6 shard_map.95
  26.6 8.5 %all_to_all.21.fac_ref.refs_3_ = bf16[4,16,1920]{2,1,0:T(8,128)(2,1)S(1)} all-to-all(bf16[4,16,1920]{2,1,0:T(8,128)(2,1)S(1)} %shard_map.95), channel_id=1, replica_groups=mesh['dp'=8,'fsdp'=4] {'fsdp'}, dimensions={0} | all-to-all | bytes 491520 | tf_op jit(solution)/shard_map/all_to_all | solution.py:249
  35.1 0.0 copy-done
  35.1 0.0 copy-done.1
  35.1 2.1 %shard_map.96 = (bf16[4,16,1920]{2,1,0:T(8,128)(2,1)}, bf16[128,16]{1,0:T(8,128)(2,1)S(1)}) custom-call(bf16[128,7168]{1,0:T(8,128)(2,1)S(1)} %copy-done, bf16[128,512]{1,0:T(8,128)(2,1)S(1)} %copy-done.1, bf16[4,16,1920]{2,1,0:T(8,128)(2,1)S(1)} %all_to_all.21.fac_ref.refs_3_), custom_call_target="tpu_custom_call" | custom-call | tf_op jit(solution)/shard_map/pallas_call | solution.py:179
  37.3 3.4 %all-to-all-start.2 = ((bf16[4,16,1920]{2,1,0:T(8,128)(2,1)}), bf16[4,16,1920]{2,1,0:T(8,128)(2,1)S(1)}, u32[]{:S(2)}, u32[]{:S(2)}) async-start(bf16[4,16,1920]{2,1,0:T(8,128)(2,1)} %get-tuple-element.14), calls=%async_computation.2 | async-start | bytes 491520 | tf_op jit(solution)/shard_map/all_to_all | solution.py:258
  40.7 0.0 copy-start.5
  40.7 0.0 copy-start.7
  40.7 1.6 %fusion = (bf16[896,512]{1,0:T(8,128)(2,1)S(1)}, bf16[896,512]{1,0:T(8,128)(2,1)S(1)}) fusion(bf16[1792,512]{1,0:T(8,128)(2,1)} %param.9), kind=kLoop, calls=%fused_computation.1 | loop fusion | bytes 3670016 | tf_op jit(solution)/shard_map/slice | solution.py:218
  42.3 2.0 %collective-permute-start.4 = (bf16[896,512]{1,0:T(8,128)(2,1)S(1)}, bf16[896,512]{1,0:T(8,128)(2,1)}, u32[]{:S(2)}, u32[]{:S(2)}) collective-permute-start(bf16[896,512]{1,0:T(8,128)(2,1)S(1)} %get-tuple-element.21.refs_4_), channel_id=1, source_target_pairs={{0,2},{1,3},{2,0},{3,1},{4,6},{5,7},{6,4},{7,5},{8,10},{9,11},{10,... | collective-permute-start | bytes 2752520 | tf_op jit(solution)/shard_map/ppermute | solution.py:215
  44.3 2.6 %all-to-all-done.2.got_ref = bf16[4,16,1920]{2,1,0:T(8,128)(2,1)S(1)} async-done(((bf16[4,16,1920]{2,1,0:T(8,128)(2,1)}), bf16[4,16,1920]{2,1,0:T(8,128)(2,1)S(1)}, u32[]{:S(2)}, u32[]{:S(2)}) %all-to-all-start.2) | async-done | bytes 245792 | tf_op jit(solution)/shard_map/all_to_all | solution.py:258
  47.0 0.0 collective-permute-start.1
  47.0 0.0 collective-permute-start.3
  47.0 19.8 %collective-permute-done.4.refs_6_ = bf16[896,512]{1,0:T(8,128)(2,1)} collective-permute-done((bf16[896,512]{1,0:T(8,128)(2,1)S(1)}, bf16[896,512]{1,0:T(8,128)(2,1)}, u32[]{:S(2)}, u32[]{:S(2)}) %collective-permute-start.4) | collective-permute-done | bytes 917536 | tf_op jit(solution)/shard_map/ppermute | solution.py:215
  66.7 0.0 collective-permute-start.5
  66.7 0.5 collective-permute-start
  67.2 18.7 %collective-permute-done.1.refs_6_ = bf16[896,512]{1,0:T(8,128)(2,1)} collective-permute-done((bf16[896,512]{1,0:T(8,128)(2,1)S(1)}, bf16[896,512]{1,0:T(8,128)(2,1)}, u32[]{:S(2)}, u32[]{:S(2)}) %collective-permute-start.1) | collective-permute-done | bytes 917536 | tf_op jit(solution)/shard_map/ppermute | solution.py:215
  85.9 0.0 collective-permute-start.2
  85.9 0.0 copy-done.5
  85.9 0.0 copy-done.7
  85.9 1.5 %shard_map.99 = bf16[8,16,1920]{2,1,0:T(8,128)(2,1)} custom-call(s32[1]{0:T(128)} %bitcast.me_ref, s32[32]{0:T(128)S(1)} %copy-done.5, s32[40]{0:T(128)S(1)} %copy-done.7, bf16[4,16,1920]{2,1,0:T(8,128)(2,1)S(1)} %all-to-all-done.2.got_ref), custom_call_target="tpu_custom_call" | custom-call | tf_op jit(solution)/shard_map/pallas_call | solution.py:179
  87.4 3.6 %all-to-all-start.3 = ((bf16[8,16,1920]{2,1,0:T(8,128)(2,1)}), bf16[8,16,1920]{2,1,0:T(8,128)(2,1)S(1)}, u32[]{:S(2)}, u32[]{:S(2)}) async-start(bf16[8,16,1920]{2,1,0:T(8,128)(2,1)} %shard_map.99), calls=%async_computation.3 | async-start | bytes 983040 | tf_op jit(solution)/shard_map/all_to_all | solution.py:271
  91.0 0.0 collective-permute-done.3.refs_5_
  91.0 0.0 collective-permute-done.5.refs_7_
  91.0 4.3 %shard_map.97.refs_8_ = bf16[128,7168]{1,0:T(8,128)(2,1)} custom-call(s32[4]{0:T(128)S(1)} %iota_xor_fusion.refs_0_, bf16[128,512]{1,0:T(8,128)(2,1)S(1)} %copy-done.1, bf16[128,16]{1,0:T(8,128)(2,1)S(1)} %get-tuple-element.13.refs_2_, bf16[4,16,1920]{2,1,0:T(8,128)(2,1)S(1)} %all_to_all.21.fac_ref.refs_3_, bf16[896,512]{1,0:T(8,128)(2,1)S(1)} %get-tuple-element.21.refs_4_, ...), custom_call_target="tpu_custom_call" | custom-call | flops 469762048 | bytes 4587520 | tf_op jit(solution)/shard_map/pallas_call | solution.py:155
  95.4 10.2 %all-to-all-done.3.got_ref = bf16[8,16,1920]{2,1,0:T(8,128)(2,1)S(1)} async-done(((bf16[8,16,1920]{2,1,0:T(8,128)(2,1)}), bf16[8,16,1920]{2,1,0:T(8,128)(2,1)S(1)}, u32[]{:S(2)}, u32[]{:S(2)}) %all-to-all-start.3) | async-done | bytes 491552 | tf_op jit(solution)/shard_map/all_to_all | solution.py:271
  105.5 1.6 %shard_map.100 = (f32[5,16,1792]{2,1,0:T(8,128)}, f32[5,16,128]{2,1,0:T(8,128)}) custom-call(s32[8]{0:T(128)S(1)} %get-tuple-element.16.want_ref, s32[5]{0:T(128)S(1)} %get-tuple-element.17.count_ref, bf16[8,16,1920]{2,1,0:T(8,128)(2,1)S(1)} %all-to-all-done.3.got_ref), custom_call_target="tpu_custom_call" | custom-call | tf_op jit(solution)/shard_map/pallas_call | solution.py:179
  107.1 0.0 collective-permute-done.refs_5_
  107.1 0.0 collective-permute-done.2.refs_7_
  107.1 4.3 %shard_map.98 = bf16[128,7168]{1,0:T(8,128)(2,1)} custom-call(s32[4]{0:T(128)S(1)} %iota_xor_fusion.refs_0_, bf16[128,512]{1,0:T(8,128)(2,1)S(1)} %copy-done.1, bf16[128,16]{1,0:T(8,128)(2,1)S(1)} %get-tuple-element.13.refs_2_, bf16[4,16,1920]{2,1,0:T(8,128)(2,1)S(1)} %all_to_all.21.fac_ref.refs_3_, ...), custom_call_target="tpu_custom_call", output_to_operand_aliasing={{}: (8, {})} | custom-call | flops 469762048 | bytes 4587520 | tf_op jit(solution)/shard_map/pallas_call | solution.py:155
  (1 shorter events, 0.0 us)
Async XLA Ops:
  0.6 34.5 %copy-start = (bf16[128,7168]{1,0:T(8,128)(2,1)S(1)}, bf16[128,7168]{1,0:T(8,128)(2,1)}, u32[]{:S(2)}) copy-start(bf16[128,7168]{1,0:T(8,128)(2,1)} %x_ref.1) | copy-start | bytes 5505028
  0.6 34.5 %copy-start.1 = (bf16[128,512]{1,0:T(8,128)(2,1)S(1)}, bf16[128,512]{1,0:T(8,128)(2,1)}, u32[]{:S(2)}) copy-start(bf16[128,512]{1,0:T(8,128)(2,1)} %refs_1_.3) | copy-start | bytes 393220
  0.7 1.1 copy-start.2
  1.8 0.7 copy-start.3
  2.5 0.7 copy-start.4
  3.1 0.7 copy-start.6
  37.3 9.7 %all-to-all-start.2 = ((bf16[4,16,1920]{2,1,0:T(8,128)(2,1)}), bf16[4,16,1920]{2,1,0:T(8,128)(2,1)S(1)}, u32[]{:S(2)}, u32[]{:S(2)}) async-start(bf16[4,16,1920]{2,1,0:T(8,128)(2,1)} %get-tuple-element.14), calls=%async_computation.2 | async-start | bytes 491520 | tf_op jit(solution)/shard_map/all_to_all | solution.py:258
  40.7 45.3 %copy-start.5 = (s32[32]{0:T(128)S(1)}, s32[32]{0:T(128)}, u32[]{:S(2)}) copy-start(s32[32]{0:T(128)} %apb_ref.5) | copy-start | bytes 388
  40.7 45.3 %copy-start.7 = (s32[40]{0:T(128)S(1)}, s32[40]{0:T(128)}, u32[]{:S(2)}) copy-start(s32[40]{0:T(128)} %row_ref.5) | copy-start | bytes 484
  42.3 24.5 %collective-permute-start.4 = (bf16[896,512]{1,0:T(8,128)(2,1)S(1)}, bf16[896,512]{1,0:T(8,128)(2,1)}, u32[]{:S(2)}, u32[]{:S(2)}) collective-permute-start(bf16[896,512]{1,0:T(8,128)(2,1)S(1)} %get-tuple-element.21.refs_4_), channel_id=1, source_target_pairs={{0,2},{1,3},{2,0},{3,1},{4,6},{5,7},{6,4},{7,5},{8,10},{9,11},{10,... | collective-permute-start | bytes 2752520 | tf_op jit(solution)/shard_map/ppermute | solution.py:215
  47.0 39.0 %collective-permute-start.1 = (bf16[896,512]{1,0:T(8,128)(2,1)S(1)}, bf16[896,512]{1,0:T(8,128)(2,1)}, u32[]{:S(2)}, u32[]{:S(2)}) collective-permute-start(bf16[896,512]{1,0:T(8,128)(2,1)S(1)} %get-tuple-element.15.refs_4_), channel_id=1, source_target_pairs={{0,2},{1,3},{2,0},{3,1},{4,6},{5,7},{6,4},{7,5},{8,10},{9,11},{10,... | collective-permute-start | bytes 2752520 | tf_op jit(solution)/shard_map/ppermute | solution.py:215
  47.0 44.0 %collective-permute-start.3 = (bf16[896,512]{1,0:T(8,128)(2,1)S(1)}, bf16[896,512]{1,0:T(8,128)(2,1)}, u32[]{:S(2)}, u32[]{:S(2)}) collective-permute-start(bf16[896,512]{1,0:T(8,128)(2,1)S(1)} %get-tuple-element.21.refs_4_), channel_id=1, source_target_pairs={{0,1},{1,0},{2,3},{3,2},{4,5},{5,4},{6,7},{7,6},{8,9},{9,8},{10,11... | collective-permute-start | bytes 2752520 | tf_op jit(solution)/shard_map/ppermute | solution.py:215
  66.7 24.3 %collective-permute-start.5 = (bf16[896,512]{1,0:T(8,128)(2,1)}, bf16[896,512]{1,0:T(8,128)(2,1)}, u32[]{:S(2)}, u32[]{:S(2)}) collective-permute-start(bf16[896,512]{1,0:T(8,128)(2,1)} %collective-permute-done.4.refs_6_), channel_id=1, source_target_pairs={{0,1},{1,0},{2,3},{3,2},{4,5},{5,4},{6,7},{7,6},{8,9},{9,8},{10,11... | collective-permute-start | bytes 2752520 | tf_op jit(solution)/shard_map/ppermute | solution.py:215
  66.7 40.4 %collective-permute-start = (bf16[896,512]{1,0:T(8,128)(2,1)S(1)}, bf16[896,512]{1,0:T(8,128)(2,1)}, u32[]{:S(2)}, u32[]{:S(2)}) collective-permute-start(bf16[896,512]{1,0:T(8,128)(2,1)S(1)} %get-tuple-element.15.refs_4_), channel_id=1, source_target_pairs={{0,1},{1,0},{2,3},{3,2},{4,5},{5,4},{6,7},{7,6},{8,9},{9,8},{10,11... | collective-permute-start | bytes 2752520 | tf_op jit(solution)/shard_map/ppermute | solution.py:215
  85.9 21.2 %collective-permute-start.2 = (bf16[896,512]{1,0:T(8,128)(2,1)}, bf16[896,512]{1,0:T(8,128)(2,1)}, u32[]{:S(2)}, u32[]{:S(2)}) collective-permute-start(bf16[896,512]{1,0:T(8,128)(2,1)} %collective-permute-done.1.refs_6_), channel_id=1, source_target_pairs={{0,1},{1,0},{2,3},{3,2},{4,5},{5,4},{6,7},{7,6},{8,9},{9,8},{10,11... | collective-permute-start | bytes 2752520 | tf_op jit(solution)/shard_map/ppermute | solution.py:215
  87.4 18.1 %all-to-all-start.3 = ((bf16[8,16,1920]{2,1,0:T(8,128)(2,1)}), bf16[8,16,1920]{2,1,0:T(8,128)(2,1)S(1)}, u32[]{:S(2)}, u32[]{:S(2)}) async-start(bf16[8,16,1920]{2,1,0:T(8,128)(2,1)} %shard_map.99), calls=%async_computation.3 | async-start | bytes 983040 | tf_op jit(solution)/shard_map/all_to_all | solution.py:271

commit v2 on v1

--- a/solution.py
+++ b/solution.py
@@ -58,7 +58,7 @@
         out_ref[j] = got_ref[owner]
 
 
-def block_kernel(down_part, up_part, x_ref, dy_ref, fac_ref, grads_ref, back_ref):
+def block_kernel(down_part, up_part, x_ref, dy_ref, fac_ref, grads_ref, back_ref, dy_t_ref):
     shares = fac_ref.shape[0]
     up_at = round_up(down_part)
     low_t = jnp.zeros((fac_ref.shape[1], BLOCK), jnp.float32)
@@ -76,6 +76,7 @@
     scaled = adapter_scale * back_t
     back = scaled.astype(jnp.bfloat16)
     back_ref[...] = scaled.T.astype(jnp.bfloat16)
+    dy_t_ref[...] = dy_ref[...].astype(jnp.float32).T.astype(jnp.bfloat16)
     for k in range(shares):
         grads_ref[k, :, :down_part] = dot(
             back, x_ref[:, k * down_part : (k + 1) * down_part]
@@ -133,15 +134,17 @@
         def _():
             copies[i].wait()
 
+    frozen_t = dot(buf[k], dy_ref[...])
     out_ref[...] = (
-        dot(dy_ref[...], buf[k], NT)
+        frozen_t.T
         + dot(back_ref[...], fac_ref[place_ref[k], :, half * rows : (half + 1) * rows])
     ).astype(jnp.bfloat16)
 
 
-def input_half(half, place, dy, back, factors, weights, out, width):
+def input_half(half, place, dy_t, back, factors, weights, out, width):
     rows, features = weights[0].shape
-    operands = [dy, back, factors, *weights]
+    tokens = dy_t.shape[1]
+    operands = [dy_t, back, factors, *weights]
     whole = [
         pl.BlockSpec(a.shape, functools.partial(lambda n, *_: (0,) * n, a.ndim))
         for a in operands[:3]
@@ -158,31 +161,31 @@
             num_scalar_prefetch=1,
             grid=(4,),
             in_specs=specs,
-            out_specs=pl.BlockSpec((dy.shape[0], rows), lambda k, place: (0, 2 * place[k] + half)),
+            out_specs=pl.BlockSpec((tokens, rows), lambda k, place: (0, 2 * place[k] + half)),
             scratch_shapes=[
                 pltpu.VMEM((4, rows, features), jnp.bfloat16),
                 pltpu.SemaphoreType.DMA((4,)),
             ],
         ),
-        out_shape=jax.ShapeDtypeStruct((dy.shape[0], width), jnp.bfloat16),
+        out_shape=jax.ShapeDtypeStruct((tokens, width), jnp.bfloat16),
         input_output_aliases=aliases,
         compiler_params=pltpu.CompilerParams(vmem_limit_bytes=32 << 20),
         cost_estimate=pl.CostEstimate(
-            flops=8 * dy.shape[0] * rows * features,
-            bytes_accessed=8 * rows * features + 8 * dy.shape[0] * rows,
+            flops=8 * tokens * rows * features,
+            bytes_accessed=8 * rows * features + 8 * tokens * rows,
             transcendentals=0,
         ),
     )(place, *operands)
 
 
-def call(kernel, out_shape, out_specs, *operands, smem=0, scratch=()):
+def call(kernel, out_shape, out_specs, *operands, smem=0, scratch=(), vmem=32):
     return pl.pallas_call(
         kernel,
         out_shape=out_shape,
         in_specs=[SMEM] * smem + [VMEM] * (len(operands) - smem),
         out_specs=out_specs,
         scratch_shapes=scratch,
-        compiler_params=pltpu.CompilerParams(vmem_limit_bytes=32 << 20),
+        compiler_params=pltpu.CompilerParams(vmem_limit_bytes=vmem << 20),
     )(*operands)
 
 
@@ -215,11 +218,6 @@
         return lax.ppermute(array, "fsdp", [(i, i ^ bit) for i in range(fsdp_count)])
 
     half_rows = value_weight.shape[0] // 2
-    halves = [value_weight[:half_rows], value_weight[half_rows:]]
-
-    def gather_half(own):
-        far = cross(own, 2)
-        return own, cross(own, 1), far, cross(far, 1)
 
     index = (me, adapter_per_block, adapter_table_row)
     send, want, count = call(
@@ -234,10 +232,16 @@
         adapter_down_table,
         adapter_up_table,
         smem=3,
-    )
-    if by_permute:
-        first = gather_half(halves[0])
+        vmem=60,
+    )
+    if by_permute:
+        value_weight, send = lax.optimization_barrier((value_weight, send))
+    halves = [value_weight[:half_rows], value_weight[half_rows:]]
     owned = lax.all_to_all(send, "dp", split_axis=0, concat_axis=0, tiled=True)
+    if by_permute:
+        far = cross(halves[0], 2)
+        owned, far = lax.optimization_barrier((owned, far))
+        first = halves[0], cross(halves[0], 1), far, cross(far, 1)
     share = call(
         functools.partial(share_kernel, slots),
         shaped(fsdp_count, rank, wide),
@@ -247,18 +251,21 @@
         smem=3,
     )
     factors = lax.all_to_all(share, "fsdp", split_axis=0, concat_axis=0, tiled=True)
-    grads, back = call(
+    if by_permute:
+        factors, first = lax.optimization_barrier((factors, first))
+    grads, back, dy_t = call(
         functools.partial(block_kernel, down_part, up_part),
-        (shaped(fsdp_count, rank, wide), shaped(BLOCK, rank)),
-        (VMEM, VMEM),
+        (
+            shaped(fsdp_count, rank, wide),
+            shaped(BLOCK, rank),
+            shaped(value_cotangent.shape[1], BLOCK),
+        ),
+        (VMEM, VMEM, VMEM),
         projection_input,
         value_cotangent,
         factors,
     )
     got = lax.all_to_all(grads, "fsdp", split_axis=0, concat_axis=0, tiled=True)
-    if by_permute:
-        second_own, got = lax.optimization_barrier((halves[1], got))
-        second = gather_half(second_own)
     sums = call(
         functools.partial(owner_kernel, slots),
         shaped(dp_count, rank, wide),
@@ -268,7 +275,15 @@
         smem=3,
         scratch=[pltpu.VMEM((dp_count, rank, wide), jnp.float32)],
     )
+    if by_permute:
+        own, sums = lax.optimization_barrier((halves[1], sums))
+        far = cross(own, 2)
     arrived = lax.all_to_all(sums, "dp", split_axis=0, concat_axis=0, tiled=True)
+    if by_permute:
+        place = at ^ jnp.arange(4, dtype=jnp.int32)
+        grad_input = input_half(0, place, dy_t, back, factors, first, None, width)
+        arrived, far, grad_input = lax.optimization_barrier((arrived, far, grad_input))
+        second = own, cross(own, 1), far, cross(far, 1)
     grad_down, grad_up = call(
         total_kernel,
         (
@@ -282,12 +297,7 @@
         smem=2,
     )
     if by_permute:
-        place = at ^ jnp.arange(4, dtype=jnp.int32)
-        grad_input = None
-        for half, weights in enumerate((first, second)):
-            grad_input = input_half(
-                half, place, value_cotangent, back, factors, weights, grad_input, width
-            )
+        grad_input = input_half(1, place, dy_t, back, factors, second, grad_input, width)
     else:
         weight = lax.all_gather(value_weight, "fsdp", axis=0, tiled=True)
         adapter_term = jnp.einsum(

time: 112 us -> 82.1 us (0.73)
  blocking collectives: 29.3 us -> 8.24 us
  waiting for transfers between devices: 51.3 us -> 31.6 us
  starting transfers between devices: 9.55 us -> 18.6 us
    ppermute x6, waiting for transfers between devices: 38.4 us -> 4.05 us  [cross(): lax.ppermute(array, 'fsdp', [(i, i ^ bit) for i in range(fsdp_count)])]
    all_to_all x2 -> x1, blocking collectives: 29.3 us -> 8.24 us  [per_device(): got = lax.all_to_all(grads, 'fsdp', split_axis=0, concat_axis=0, tiled=True)]
    all_to_all x1 -> x2, waiting for transfers between devices: 2.64 us -> 19.4 us  [the longest x1 13.5 us: per_device(): owned = lax.all_to_all(send, 'dp', split_axis=0, concat_axis=0, tiled=True)]
    all_to_all x1 -> x2, starting transfers between devices: 3.4 us -> 9.2 us  [the longest x1 5.81 us: per_device(): owned = lax.all_to_all(send, 'dp', split_axis=0, concat_axis=0, tiled=True)]
    all_to_all x1, starting transfers between devices: 3.59 us -> 5.95 us  [per_device(): lax.all_to_all(sums, 'dp', split_axis=0, concat_axis=0, tiled=True)]
    all_to_all x1, waiting for transfers between devices: 10.2 us -> 8.13 us  [per_device(): lax.all_to_all(sums, 'dp', split_axis=0, concat_axis=0, tiled=True)]
    unnamed x16 -> x18, local copies, waits for them, and re-layouts: 3.15 us -> 4.23 us
  transfers between devices with their start and end apart: 8 -> 9, of which waited for: 4 -> 6; matrix products, arithmetic and copies ran while one was open for 1% -> 0% of each run, Pallas kernels for 7% -> 9%
where the time goes in v2:
time: 82.1 us; the launch traced here: 81.6 us
  waiting for transfers between devices  31.6 us (38%)
  starting transfers between devices  18.6 us (23%)
  Pallas kernels  16.5 us (20%)
  blocking collectives  8.24 us (10%)
  local copies, waits for them, and re-layouts  5.81 us (7%)
    all_to_all x1, waiting for transfers between devices, per_device(): owned = lax.all_to_all(send, 'dp', split_axis=0, concat_axis=0, tiled=True)  13.5 us
    pallas_call x2, Pallas kernels, input_half(): pl.pallas_call(functools.partial(input_kernel, half), grid_spec=pltpu.Pre...  8.79 us
    all_to_all x1, blocking collectives, per_device(): got = lax.all_to_all(grads, 'fsdp', split_axis=0, concat_axis=0, tiled=True)  8.24 us
    all_to_all x1, waiting for transfers between devices, per_device(): lax.all_to_all(sums, 'dp', split_axis=0, concat_axis=0, tiled=True)  8.13 us
    pallas_call x5, Pallas kernels, call(): pl.pallas_call(kernel, out_shape=out_shape, in_specs=[SMEM] * smem + [VME...  7.75 us
    all_to_all x1, starting transfers between devices, per_device(): lax.all_to_all(sums, 'dp', split_axis=0, concat_axis=0, tiled=True)  5.95 us
    all_to_all x1, waiting for transfers between devices, per_device(): lax.all_to_all(share, 'fsdp', split_axis=0, concat_axis=0, tiled=True)  5.89 us
    all_to_all x1, starting transfers between devices, per_device(): owned = lax.all_to_all(send, 'dp', split_axis=0, concat_axis=0, tiled=True)  5.81 us
  transfers between devices with their start and end apart: 9, of which 6 were waited for; matrix products, arithmetic and copies ran while one was open for 0% of the time, Pallas kernels for 9%

profile of v2, /device:TPU:0, one launch (start us, length us, event | category | flops | bytes accessed | tf_op | source)
XLA Modules:
  0.0 81.6 jit_solution(18119918786236489902)
XLA Ops:
  0.6 2.0 %shard_map.94 = (bf16[8,16,1920]{2,1,0:T(8,128)(2,1)}, s32[8]{0:T(128)}, s32[5]{0:T(128)}) custom-call(s32[1]{0:T(128)} %bitcast.me_ref, s32[32]{0:T(128)} %apb_ref.5, s32[40]{0:T(128)} %row_ref.5, bf16[5,16,1792]{2,1,0:T(8,128)(2,1)} %down_ref.1, bf16[5,16,128]{2,1,0:T(8,128)(2,1)} %up_ref.1), custom_call_target="tpu_custom_call" | custom-call | tf_op jit(solution)/shard_map/pallas_call | solution.py:182
  2.6 0.0 copy-start.5
  2.7 0.0 copy-start.6
  2.7 1.6 %fusion = (bf16[896,512]{1,0:T(8,128)(2,1)S(1)}, bf16[896,512]{1,0:T(8,128)(2,1)S(1)}) fusion(bf16[1792,512]{1,0:T(8,128)(2,1)} %param.9), kind=kLoop, calls=%fused_computation.1 | loop fusion | bytes 3670016 | tf_op jit(solution)/shard_map/slice | solution.py:239
  4.3 3.0 %collective-permute-start = (bf16[896,512]{1,0:T(8,128)(2,1)S(1)}, bf16[896,512]{1,0:T(8,128)(2,1)S(1)}, u32[]{:S(2)}, u32[]{:S(2)}) collective-permute-start(bf16[896,512]{1,0:T(8,128)(2,1)S(1)} %get-tuple-element.36.refs_4_), channel_id=1, source_target_pairs={{0,2},{1,3},{2,0},{3,1},{4,6},{5,7},{6,4},{7,5},{8,10},{9,11},{10,... | collective-permute-start | bytes 2752520 | tf_op jit(solution)/shard_map/ppermute | solution.py:218
  7.3 5.8 %all-to-all-start = ((bf16[8,16,1920]{2,1,0:T(8,128)(2,1)}), bf16[8,16,1920]{2,1,0:T(8,128)(2,1)S(1)}, u32[]{:S(2)}, u32[]{:S(2)}) async-start(bf16[8,16,1920]{2,1,0:T(8,128)(2,1)} %get-tuple-element.26), calls=%async_computation | async-start | bytes 983040 | tf_op jit(solution)/shard_map/all_to_all | solution.py:240
  13.1 0.0 collective-permute-start.1
  13.1 13.5 %all-to-all-done.got_ref = bf16[8,16,1920]{2,1,0:T(8,128)(2,1)S(1)} async-done(((bf16[8,16,1920]{2,1,0:T(8,128)(2,1)}), bf16[8,16,1920]{2,1,0:T(8,128)(2,1)S(1)}, u32[]{:S(2)}, u32[]{:S(2)}) %all-to-all-start) | async-done | bytes 491552 | tf_op jit(solution)/shard_map/all_to_all | solution.py:240
  26.6 1.0 %collective-permute-done.refs_6_ = bf16[896,512]{1,0:T(8,128)(2,1)S(1)} collective-permute-done((bf16[896,512]{1,0:T(8,128)(2,1)S(1)}, bf16[896,512]{1,0:T(8,128)(2,1)S(1)}, u32[]{:S(2)}, u32[]{:S(2)}) %collective-permute-start) | collective-permute-done | bytes 917536 | tf_op jit(solution)/shard_map/ppermute | solution.py:218
  27.6 0.0 collective-permute-start.2
  27.6 0.0 copy-done.5
  27.6 0.0 copy-done.6
  27.6 1.3 %shard_map.95 = bf16[4,16,1920]{2,1,0:T(8,128)(2,1)} custom-call(s32[1]{0:T(128)} %bitcast.me_ref, s32[32]{0:T(128)S(1)} %copy-done.5, s32[40]{0:T(128)S(1)} %copy-done.6, bf16[8,16,1920]{2,1,0:T(8,128)(2,1)S(1)} %all-to-all-done.got_ref), custom_call_target="tpu_custom_call" | custom-call | tf_op jit(solution)/shard_map/pallas_call | solution.py:182
  28.9 3.4 %all-to-all-start.1 = ((bf16[4,16,1920]{2,1,0:T(8,128)(2,1)}), bf16[4,16,1920]{2,1,0:T(8,128)(2,1)S(1)}, u32[]{:S(2)}, u32[]{:S(2)}) async-start(bf16[4,16,1920]{2,1,0:T(8,128)(2,1)} %shard_map.95), calls=%async_computation.1 | async-start | bytes 491520 | tf_op jit(solution)/shard_map/all_to_all | solution.py:253
  32.3 0.0 collective-permute-done.1.refs_5_
  32.3 5.9 %all-to-all-done.1.fac_ref.refs_3_ = bf16[4,16,1920]{2,1,0:T(8,128)(2,1)S(1)} async-done(((bf16[4,16,1920]{2,1,0:T(8,128)(2,1)}), bf16[4,16,1920]{2,1,0:T(8,128)(2,1)S(1)}, u32[]{:S(2)}, u32[]{:S(2)}) %all-to-all-start.1) | async-done | bytes 245792 | tf_op jit(solution)/shard_map/all_to_all | solution.py:253
  38.2 0.0 collective-permute-done.2.refs_7_
  38.2 0.0 copy-start
  38.2 1.5 %copy-done = bf16[128,7168]{1,0:T(8,128)(2,1)S(1)} copy-done((bf16[128,7168]{1,0:T(8,128)(2,1)S(1)}, bf16[128,7168]{1,0:T(8,128)(2,1)}, u32[]{:S(2)}) %copy-start) | copy-done | bytes 1835032
  39.7 0.0 copy-start.4
  39.7 0.9 %copy-done.4 = bf16[128,512]{1,0:T(8,128)(2,1)S(1)} copy-done((bf16[128,512]{1,0:T(8,128)(2,1)S(1)}, bf16[128,512]{1,0:T(8,128)(2,1)}, u32[]{:S(2)}) %copy-start.4) | copy-done | bytes 131096
  40.6 1.4 %shard_map.96 = (bf16[4,16,1920]{2,1,0:T(8,128)(2,1)S(1)}, bf16[128,16]{1,0:T(8,128)(2,1)S(1)}, bf16[512,128]{1,0:T(8,128)(2,1)S(1)}) custom-call(bf16[128,7168]{1,0:T(8,128)(2,1)S(1)} %copy-done, bf16[128,512]{1,0:T(8,128)(2,1)S(1)} %copy-done.4, bf16[4,16,1920]{2,1,0:T(8,128)(2,1)S(1)} %all-to-all-done.1.fac_ref.refs_3_), custom_call_target="tpu_custom_call" | custom-call | tf_op jit(solution)/shard_map/pallas_call | solution.py:182
  42.1 0.0 copy-start.1
  42.1 8.2 %all_to_all.20.got_ref = bf16[4,16,1920]{2,1,0:T(8,128)(2,1)S(1)} all-to-all(bf16[4,16,1920]{2,1,0:T(8,128)(2,1)S(1)} %get-tuple-element.33), channel_id=1, replica_groups=mesh['dp'=8,'fsdp'=4] {'fsdp'}, dimensions={0} | all-to-all | bytes 491520 | tf_op jit(solution)/shard_map/all_to_all | solution.py:268
  50.3 1.5 %shard_map.97 = bf16[8,16,1920]{2,1,0:T(8,128)(2,1)} custom-call(s32[1]{0:T(128)} %bitcast.me_ref, s32[32]{0:T(128)S(1)} %copy-done.5, s32[40]{0:T(128)S(1)} %copy-done.6, bf16[4,16,1920]{2,1,0:T(8,128)(2,1)S(1)} %all_to_all.20.got_ref), custom_call_target="tpu_custom_call" | custom-call | tf_op jit(solution)/shard_map/pallas_call | solution.py:182
  51.8 0.0 copy-done.1
  51.8 0.4 collective-permute-start.4
  52.2 6.0 %all-to-all-start.3 = ((bf16[8,16,1920]{2,1,0:T(8,128)(2,1)}), bf16[8,16,1920]{2,1,0:T(8,128)(2,1)S(1)}, u32[]{:S(2)}, u32[]{:S(2)}) async-start(bf16[8,16,1920]{2,1,0:T(8,128)(2,1)} %shard_map.97), calls=%async_computation.3 | async-start | bytes 983040 | tf_op jit(solution)/shard_map/all_to_all | solution.py:281
  58.1 0.0 copy-start.2
  58.1 0.9 %copy-done.2 = bf16[512,128]{1,0:T(8,128)(2,1)S(1)} copy-done((bf16[512,128]{1,0:T(8,128)(2,1)S(1)}, bf16[512,128]{1,0:T(8,128)(2,1)}, u32[]{:S(2)}) %copy-start.2) | copy-done | bytes 131096
  59.0 0.0 copy-start.7
  59.0 0.0 copy-start.8
  59.0 4.5 %shard_map.98.refs_8_ = bf16[128,7168]{1,0:T(8,128)(2,1)} custom-call(s32[4]{0:T(128)S(1)} %iota_xor_fusion.refs_0_, bf16[512,128]{1,0:T(8,128)(2,1)S(1)} %copy-done.2, bf16[128,16]{1,0:T(8,128)(2,1)S(1)} %get-tuple-element.32.refs_2_, bf16[4,16,1920]{2,1,0:T(8,128)(2,1)S(1)} %all-to-all-done.1.fac_ref.refs_3_, ...), custom_call_target="tpu_custom_call" | custom-call | flops 469762048 | bytes 4587520 | tf_op jit(solution)/shard_map/pallas_call | solution.py:158
  63.5 0.1 collective-permute-start.3
  63.6 8.1 %all-to-all-done.3.got_ref = bf16[8,16,1920]{2,1,0:T(8,128)(2,1)S(1)} async-done(((bf16[8,16,1920]{2,1,0:T(8,128)(2,1)}), bf16[8,16,1920]{2,1,0:T(8,128)(2,1)S(1)}, u32[]{:S(2)}, u32[]{:S(2)}) %all-to-all-start.3) | async-done | bytes 491552 | tf_op jit(solution)/shard_map/all_to_all | solution.py:281
  71.7 1.9 %collective-permute-done.4.refs_6_ = bf16[896,512]{1,0:T(8,128)(2,1)} collective-permute-done((bf16[896,512]{1,0:T(8,128)(2,1)S(1)}, bf16[896,512]{1,0:T(8,128)(2,1)}, u32[]{:S(2)}, u32[]{:S(2)}) %collective-permute-start.4) | collective-permute-done | bytes 917536 | tf_op jit(solution)/shard_map/ppermute | solution.py:218
  73.7 0.0 collective-permute-start.5
  73.7 0.0 copy-done.7
  73.7 0.0 copy-done.8
  73.7 1.6 %shard_map.100 = (f32[5,16,1792]{2,1,0:T(8,128)}, f32[5,16,128]{2,1,0:T(8,128)}) custom-call(s32[8]{0:T(128)S(1)} %copy-done.7, s32[5]{0:T(128)S(1)} %copy-done.8, bf16[8,16,1920]{2,1,0:T(8,128)(2,1)S(1)} %all-to-all-done.3.got_ref), custom_call_target="tpu_custom_call" | custom-call | tf_op jit(solution)/shard_map/pallas_call | solution.py:182
  75.2 0.0 collective-permute-done.3.refs_5_
  75.3 1.1 %collective-permute-done.5.refs_7_ = bf16[896,512]{1,0:T(8,128)(2,1)S(1)} collective-permute-done((bf16[896,512]{1,0:T(8,128)(2,1)}, bf16[896,512]{1,0:T(8,128)(2,1)S(1)}, u32[]{:S(2)}, u32[]{:S(2)}) %collective-permute-start.5) | collective-permute-done | bytes 917536 | tf_op jit(solution)/shard_map/ppermute | solution.py:218
  76.4 0.0 copy-start.3
  76.4 0.9 %copy-done.3 = bf16[512,128]{1,0:T(8,128)(2,1)S(1)} copy-done((bf16[512,128]{1,0:T(8,128)(2,1)S(1)}, bf16[512,128]{1,0:T(8,128)(2,1)}, u32[]{:S(2)}) %copy-start.3) | copy-done | bytes 131096
  77.3 4.3 %shard_map.99 = bf16[128,7168]{1,0:T(8,128)(2,1)} custom-call(s32[4]{0:T(128)S(1)} %iota_xor_fusion.refs_0_, bf16[512,128]{1,0:T(8,128)(2,1)S(1)} %copy-done.3, bf16[128,16]{1,0:T(8,128)(2,1)S(1)} %get-tuple-element.32.refs_2_, bf16[4,16,1920]{2,1,0:T(8,128)(2,1)S(1)} %all-to-all-done.1.fac_ref.refs_3_, ...), custom_call_target="tpu_custom_call", output_to_operand_aliasing={{}: (8, {})} | custom-call | flops 469762048 | bytes 4587520 | tf_op jit(solution)/shard_map/pallas_call | solution.py:158
  (1 shorter events, 0.0 us)
Async XLA Ops:
  2.6 25.0 %copy-start.5 = (s32[32]{0:T(128)S(1)}, s32[32]{0:T(128)}, u32[]{:S(2)}) copy-start(s32[32]{0:T(128)} %apb_ref.5) | copy-start | bytes 388
  2.7 25.0 %copy-start.6 = (s32[40]{0:T(128)S(1)}, s32[40]{0:T(128)}, u32[]{:S(2)}) copy-start(s32[40]{0:T(128)} %row_ref.5) | copy-start | bytes 484
  4.3 23.4 %collective-permute-start = (bf16[896,512]{1,0:T(8,128)(2,1)S(1)}, bf16[896,512]{1,0:T(8,128)(2,1)S(1)}, u32[]{:S(2)}, u32[]{:S(2)}) collective-permute-start(bf16[896,512]{1,0:T(8,128)(2,1)S(1)} %get-tuple-element.36.refs_4_), channel_id=1, source_target_pairs={{0,2},{1,3},{2,0},{3,1},{4,6},{5,7},{6,4},{7,5},{8,10},{9,11},{10,... | collective-permute-start | bytes 2752520 | tf_op jit(solution)/shard_map/ppermute | solution.py:218
  7.3 19.4 %all-to-all-start = ((bf16[8,16,1920]{2,1,0:T(8,128)(2,1)}), bf16[8,16,1920]{2,1,0:T(8,128)(2,1)S(1)}, u32[]{:S(2)}, u32[]{:S(2)}) async-start(bf16[8,16,1920]{2,1,0:T(8,128)(2,1)} %get-tuple-element.26), calls=%async_computation | async-start | bytes 983040 | tf_op jit(solution)/shard_map/all_to_all | solution.py:240
  13.1 19.2 %collective-permute-start.1 = (bf16[896,512]{1,0:T(8,128)(2,1)S(1)}, bf16[896,512]{1,0:T(8,128)(2,1)}, u32[]{:S(2)}, u32[]{:S(2)}) collective-permute-start(bf16[896,512]{1,0:T(8,128)(2,1)S(1)} %get-tuple-element.36.refs_4_), channel_id=1, source_target_pairs={{0,1},{1,0},{2,3},{3,2},{4,5},{5,4},{6,7},{7,6},{8,9},{9,8},{10,11... | collective-permute-start | bytes 2752520 | tf_op jit(solution)/shard_map/ppermute | solution.py:218
  27.6 10.6 %collective-permute-start.2 = (bf16[896,512]{1,0:T(8,128)(2,1)S(1)}, bf16[896,512]{1,0:T(8,128)(2,1)}, u32[]{:S(2)}, u32[]{:S(2)}) collective-permute-start(bf16[896,512]{1,0:T(8,128)(2,1)S(1)} %collective-permute-done.refs_6_), channel_id=1, source_target_pairs={{0,1},{1,0},{2,3},{3,2},{4,5},{5,4},{6,7},{7,6},{8,9},{9,8},{10,11... | collective-permute-start | bytes 2752520 | tf_op jit(solution)/shard_map/ppermute | solution.py:218
  28.9 9.3 %all-to-all-start.1 = ((bf16[4,16,1920]{2,1,0:T(8,128)(2,1)}), bf16[4,16,1920]{2,1,0:T(8,128)(2,1)S(1)}, u32[]{:S(2)}, u32[]{:S(2)}) async-start(bf16[4,16,1920]{2,1,0:T(8,128)(2,1)} %shard_map.95), calls=%async_computation.1 | async-start | bytes 491520 | tf_op jit(solution)/shard_map/all_to_all | solution.py:253
  38.2 1.5 %copy-start = (bf16[128,7168]{1,0:T(8,128)(2,1)S(1)}, bf16[128,7168]{1,0:T(8,128)(2,1)}, u32[]{:S(2)}) copy-start(bf16[128,7168]{1,0:T(8,128)(2,1)} %x_ref.1) | copy-start | bytes 5505028
  39.7 0.9 %copy-start.4 = (bf16[128,512]{1,0:T(8,128)(2,1)S(1)}, bf16[128,512]{1,0:T(8,128)(2,1)}, u32[]{:S(2)}) copy-start(bf16[128,512]{1,0:T(8,128)(2,1)} %dy_ref.1) | copy-start | bytes 393220
  42.1 9.7 %copy-start.1 = (bf16[512,128]{1,0:T(8,128)(2,1)}, bf16[512,128]{1,0:T(8,128)(2,1)S(1)}, u32[]{:S(2)}) copy-start(bf16[512,128]{1,0:T(8,128)(2,1)S(1)} %get-tuple-element.31.refs_1_) | copy-start | bytes 393220
  51.8 21.9 %collective-permute-start.4 = (bf16[896,512]{1,0:T(8,128)(2,1)S(1)}, bf16[896,512]{1,0:T(8,128)(2,1)}, u32[]{:S(2)}, u32[]{:S(2)}) collective-permute-start(bf16[896,512]{1,0:T(8,128)(2,1)S(1)} %get-tuple-element.34.refs_4_), channel_id=1, source_target_pairs={{0,2},{1,3},{2,0},{3,1},{4,6},{5,7},{6,4},{7,5},{8,10},{9,11},{10,... | collective-permute-start | bytes 2752520 | tf_op jit(solution)/shard_map/ppermute | solution.py:218
  52.2 19.6 %all-to-all-start.3 = ((bf16[8,16,1920]{2,1,0:T(8,128)(2,1)}), bf16[8,16,1920]{2,1,0:T(8,128)(2,1)S(1)}, u32[]{:S(2)}, u32[]{:S(2)}) async-start(bf16[8,16,1920]{2,1,0:T(8,128)(2,1)} %shard_map.97), calls=%async_computation.3 | async-start | bytes 983040 | tf_op jit(solution)/shard_map/all_to_all | solution.py:281
  58.1 0.9 %copy-start.2 = (bf16[512,128]{1,0:T(8,128)(2,1)S(1)}, bf16[512,128]{1,0:T(8,128)(2,1)}, u32[]{:S(2)}) copy-start(bf16[512,128]{1,0:T(8,128)(2,1)} %copy-done.1) | copy-start | bytes 393220
  59.0 14.7 %copy-start.7 = (s32[8]{0:T(128)S(1)}, s32[8]{0:T(128)}, u32[]{:S(2)}) copy-start(s32[8]{0:T(128)} %get-tuple-element.42.want_ref) | copy-start | bytes 100
  59.0 14.7 %copy-start.8 = (s32[5]{0:T(128)S(1)}, s32[5]{0:T(128)}, u32[]{:S(2)}) copy-start(s32[5]{0:T(128)} %get-tuple-element.43.count_ref) | copy-start | bytes 64
  63.5 11.7 %collective-permute-start.3 = (bf16[896,512]{1,0:T(8,128)(2,1)S(1)}, bf16[896,512]{1,0:T(8,128)(2,1)S(1)}, u32[]{:S(2)}, u32[]{:S(2)}) collective-permute-start(bf16[896,512]{1,0:T(8,128)(2,1)S(1)} %get-tuple-element.34.refs_4_), channel_id=1, source_target_pairs={{0,1},{1,0},{2,3},{3,2},{4,5},{5,4},{6,7},{7,6},{8,9},{9,8},{10,11... | collective-permute-start | bytes 2752520 | tf_op jit(solution)/shard_map/ppermute | solution.py:218
  73.7 2.7 %collective-permute-start.5 = (bf16[896,512]{1,0:T(8,128)(2,1)}, bf16[896,512]{1,0:T(8,128)(2,1)S(1)}, u32[]{:S(2)}, u32[]{:S(2)}) collective-permute-start(bf16[896,512]{1,0:T(8,128)(2,1)} %collective-permute-done.4.refs_6_), channel_id=1, source_target_pairs={{0,1},{1,0},{2,3},{3,2},{4,5},{5,4},{6,7},{7,6},{8,9},{9,8},{10,11... | collective-permute-start | bytes 2752520 | tf_op jit(solution)/shard_map/ppermute | solution.py:218
  76.4 0.9 %copy-start.3 = (bf16[512,128]{1,0:T(8,128)(2,1)S(1)}, bf16[512,128]{1,0:T(8,128)(2,1)}, u32[]{:S(2)}) copy-start(bf16[512,128]{1,0:T(8,128)(2,1)} %copy-done.1) | copy-start | bytes 393220

commit v3 on v2

v3 whole, which is shorter than its diff:
```python
import functools

import jax
import jax.numpy as jnp
from jax import lax
from jax.experimental import pallas as pl
from jax.experimental.pallas import tpu as pltpu
from jax.sharding import PartitionSpec as P

BLOCK = 128
LANES = 128
adapter_scale = 2.0

SMEM = pl.BlockSpec(memory_space=pltpu.SMEM)
VMEM = pl.BlockSpec(memory_space=pltpu.VMEM)
NT = (((1,), (1,)), ((), ()))


def round_up(n):
    return -(-n // LANES) * LANES


def dot(a, b, dims=(((1,), (0,)), ((), ()))):
    return lax.dot_general(a, b, dims, preferred_element_type=jnp.float32)


def turned(a):
    return a.astype(jnp.float32).T.astype(a.dtype)


def pick_kernel(group_blocks, me_ref, apb_ref, row_ref, down_ref, up_ref, send_ref, want_ref, count_ref):
    slots, _, down_part = down_ref.shape
    up_part = up_ref.shape[2]
    up_at = round_up(down_part)
    groups = send_ref.shape[0]
    first = me_ref[0] * slots
    for s in range(slots):
        count_ref[s] = 0

    def group(g, carry):
        want_ref[g] = 0
        for j in range(group_blocks):
            local = row_ref[apb_ref[g * group_blocks + j]] - first

            @pl.when((local >= 0) & (local < slots))
            def _():
                want_ref[g] = local
                count_ref[local] = count_ref[local] + 1

        slot = want_ref[g]
        send_ref[g, :, :down_part] = down_ref[slot]
        send_ref[g, :, up_at : up_at + up_part] = up_ref[slot]
        return carry

    lax.fori_loop(0, groups, group, 0)


def share_kernel(slots, me_ref, apb_ref, row_ref, got_ref, out_ref):
    blocks = out_ref.shape[0]
    for j in range(blocks):
        owner = lax.div(row_ref[apb_ref[me_ref[0] * blocks + j]], slots)
        out_ref[j] = got_ref[owner]


def block_kernel(
    down_part, up_part, x_ref, dy_ref, fac_ref, grads_ref, back_ref, dy_t_ref, x_buf, sems
):
    shares = fac_ref.shape[0]
    up_at = round_up(down_part)
    back_at = up_at + round_up(up_part)
    parts = shares if down_part % LANES == 0 else 1
    copies = []
    for k in range(parts):
        columns = pl.ds(k * (x_ref.shape[1] // parts), x_ref.shape[1] // parts)
        copies.append(
            pltpu.make_async_copy(x_ref.at[:, columns], x_buf.at[:, columns], sems.at[k])
        )
        copies[k].start()
    low_t = jnp.zeros((fac_ref.shape[1], BLOCK), jnp.float32)
    back_t = jnp.zeros((fac_ref.shape[1], BLOCK), jnp.float32)
    for k in range(shares):
        back_t += dot(
            fac_ref[k, :, up_at : up_at + up_part],
            dy_ref[:, k * up_part : (k + 1) * up_part],
            NT,
        )
    scaled = adapter_scale * back_t
    back = scaled.astype(jnp.bfloat16)
    back_ref[...] = scaled.T.astype(jnp.bfloat16)
    dy_t_ref[...] = turned(dy_ref[...])
    for k in range(shares):
        if k < parts:
            copies[k].wait()
        x = x_buf[:, k * down_part : (k + 1) * down_part]
        low_t += dot(fac_ref[k, :, :down_part], x, NT)
        grads_ref[k, :, :down_part] = dot(back, x).astype(jnp.bfloat16)
        grads_ref[k, :, back_at:] = back
    low = low_t.astype(jnp.bfloat16)
    for k in range(shares):
        grads_ref[k, :, up_at : up_at + up_part] = (
            adapter_scale * dot(low, dy_ref[:, k * up_part : (k + 1) * up_part])
        ).astype(jnp.bfloat16)


def owner_kernel(slots, me_ref, apb_ref, row_ref, got_ref, out_ref, acc_ref):
    blocks = got_ref.shape[0]
    acc_ref[...] = jnp.zeros_like(acc_ref)
    for j in range(blocks):
        owner = lax.div(row_ref[apb_ref[me_ref[0] * blocks + j]], slots)
        acc_ref[owner] += got_ref[j, :, : acc_ref.shape[2]].astype(jnp.float32)
    out_ref[...] = acc_ref[...].astype(jnp.bfloat16)


def total_kernel(want_ref, count_ref, got_ref, down_ref, up_ref):
    slots, _, down_part = down_ref.shape
    up_part = up_ref.shape[2]
    up_at = round_up(down_part)
    down_ref[...] = jnp.zeros_like(down_ref)
    up_ref[...] = jnp.zeros_like(up_ref)

    def group(g, carry):
        slot = want_ref[g]
        down_ref[slot] += got_ref[g, :, :down_part].astype(jnp.float32)
        up_ref[slot] += got_ref[g, :, up_at : up_at + up_part].astype(jnp.float32)
        return carry

    lax.fori_loop(0, got_ref.shape[0], group, 0)
    for s in range(slots):
        divisor = jnp.maximum(count_ref[s], 1).astype(jnp.float32)
        down_ref[s] = down_ref[s] / divisor
        up_ref[s] = up_ref[s] / divisor


def far_kernel(at_ref, w_ref, dy2_ref, dy3_ref, share_ref, got_ref, z2_ref, z3_ref):
    rows = z2_ref.shape[1]
    tokens = dy2_ref.shape[0]
    start = w_ref.shape[0] - rows
    dy_t = jnp.concatenate([turned(dy2_ref[...]), turned(dy3_ref[...])], axis=1)
    frozen_t = dot(w_ref[start:, :], dy_t)
    for i, z_ref in enumerate((z2_ref, z3_ref)):
        peer = lax.bitwise_xor(at_ref[0], 2 + i)
        back = turned(got_ref[peer, :, got_ref.shape[2] - tokens :])
        z_ref[...] = (
            frozen_t[:, i * tokens : (i + 1) * tokens].T
            + dot(back, share_ref[peer, :, start : w_ref.shape[0]])
        ).astype(jnp.bfloat16)


def input_kernel(
    at_ref, dy_t_ref, back_ref, fac_ref, w0_ref, w1_ref, w2_ref, w3_ref, out_ref, buf, sems
):
    part = w0_ref.shape[0]
    copies = []
    for k, w_ref in enumerate((w0_ref, w1_ref, w2_ref, w3_ref)):
        rows = w_ref.shape[0]
        peer = lax.bitwise_xor(at_ref[0], k)
        buf[k, :, :rows] = (
            dot(w_ref[...], dy_t_ref[...]).T + dot(back_ref[...], fac_ref[peer, :, :rows])
        ).astype(jnp.bfloat16)
        first = pl.multiple_of(peer * part, LANES)
        copy = pltpu.make_async_copy(
            buf.at[k, :, pl.ds(0, rows)], out_ref.at[:, pl.ds(first, rows)], sems.at[k]
        )
        copy.start()
        copies.append(copy)
    for copy in copies:
        copy.wait()


def place_kernel(at_ref, z2_ref, z3_ref, in_ref, out_ref, sems):
    rows = z2_ref.shape[1]
    part = out_ref.shape[1] // 4
    copies = []
    for i, z_ref in enumerate((z2_ref, z3_ref)):
        peer = lax.bitwise_xor(at_ref[0], 2 + i)
        first = pl.multiple_of(peer * part + (part - rows), LANES)
        copy = pltpu.make_async_copy(z_ref, out_ref.at[:, pl.ds(first, rows)], sems.at[i])
        copy.start()
        copies.append(copy)
    for copy in copies:
        copy.wait()


def call(
    kernel, out_shape, out_specs, *operands, smem=0, scratch=(), vmem=32, specs=None, aliases=None
):
    return pl.pallas_call(
        kernel,
        out_shape=out_shape,
        in_specs=[SMEM] * smem + (specs or [VMEM] * (len(operands) - smem)),
        input_output_aliases=aliases or {},
        out_specs=out_specs,
        scratch_shapes=scratch,
        compiler_params=pltpu.CompilerParams(vmem_limit_bytes=vmem << 20),
    )(*operands)


def per_device(
    projection_input,
    value_cotangent,
    value_weight,
    adapter_down_table,
    adapter_up_table,
    adapter_per_block,
    adapter_table_row,
):
    dp_count = lax.axis_size("dp")
    fsdp_count = lax.axis_size("fsdp")
    me = lax.axis_index("dp").reshape(1)
    at = lax.axis_index("fsdp")
    tok_rows, width = projection_input.shape
    slots, rank, down_part = adapter_down_table.shape
    up_part = adapter_up_table.shape[2]
    assert tok_rows == BLOCK
    wide = round_up(down_part) + round_up(up_part)
    bf16 = jnp.bfloat16

    def shaped(*shape, dtype=bf16):
        return jax.ShapeDtypeStruct(shape, dtype)

    by_permute = fsdp_count == 4 and down_part % 256 == 0
    near_rows = 3 * down_part // 8 // LANES * LANES

    def cross(array, bit):
        return lax.ppermute(array, "fsdp", [(i, i ^ bit) for i in range(fsdp_count)])

    index = (me, adapter_per_block, adapter_table_row)
    send, want, count = call(
        functools.partial(pick_kernel, fsdp_count),
        (
            shaped(dp_count, rank, wide),
            shaped(dp_count, dtype=jnp.int32),
            shaped(slots, dtype=jnp.int32),
        ),
        (VMEM, SMEM, SMEM),
        *index,
        adapter_down_table,
        adapter_up_table,
        smem=3,
        vmem=60,
    )
    if by_permute:
        value_weight, send = lax.optimization_barrier((value_weight, send))
    owned = lax.all_to_all(send, "dp", split_axis=0, concat_axis=0, tiled=True)
    if by_permute:
        far = cross(value_weight[:near_rows], 2)
        dy2 = cross(value_cotangent, 2)
        owned, far, dy2 = lax.optimization_barrier((owned, far, dy2))
        near = cross(value_weight, 1), far, cross(far, 1)
        dys = dy2, cross(dy2, 1)
    share = call(
        functools.partial(share_kernel, slots),
        shaped(fsdp_count, rank, wide),
        VMEM,
        *index,
        owned,
        smem=3,
    )
    factors = lax.all_to_all(share, "fsdp", split_axis=0, concat_axis=0, tiled=True)
    if by_permute:
        factors, near, dys = lax.optimization_barrier((factors, near, dys))
    grads, back, dy_t = call(
        functools.partial(block_kernel, down_part, up_part),
        (
            shaped(fsdp_count, rank, wide + BLOCK),
            shaped(BLOCK, rank),
            shaped(value_cotangent.shape[1], BLOCK),
        ),
        (VMEM, VMEM, VMEM),
        projection_input,
        value_cotangent,
        factors,
        specs=[pl.BlockSpec(memory_space=pl.ANY), VMEM, VMEM],
        scratch=[
            pltpu.VMEM((BLOCK, width), bf16),
            pltpu.SemaphoreType.DMA((fsdp_count,)),
        ],
        vmem=56,
    )
    got = lax.all_to_all(grads, "fsdp", split_axis=0, concat_axis=0, tiled=True)
    sums = call(
        functools.partial(owner_kernel, slots),
        shaped(dp_count, rank, wide),
        VMEM,
        *index,
        got,
        smem=3,
        scratch=[pltpu.VMEM((dp_count, rank, wide), jnp.float32)],
    )
    arrived = lax.all_to_all(sums, "dp", split_axis=0, concat_axis=0, tiled=True)
    if by_permute:
        at = at.reshape(1)
        far_rows = down_part - near_rows
        z2, z3 = call(
            far_kernel,
            (shaped(BLOCK, far_rows), shaped(BLOCK, far_rows)),
            (VMEM, VMEM),
            at,
            value_weight,
            *dys,
            share,
            got,
            smem=1,
        )
        z2, z3 = cross(z2, 2), cross(z3, 3)
        grad_input = call(
            input_kernel,
            shaped(tok_rows, width),
            pl.BlockSpec(memory_space=pl.ANY),
            at,
            dy_t,
            back,
            factors,
            value_weight,
            *near,
            smem=1,
            scratch=[
                pltpu.VMEM((fsdp_count, tok_rows, down_part), bf16),
                pltpu.SemaphoreType.DMA((fsdp_count,)),
            ],
        )
        grad_input = call(
            place_kernel,
            shaped(tok_rows, width),
            pl.BlockSpec(memory_space=pl.ANY),
            at,
            z2,
            z3,
            grad_input,
            smem=1,
            specs=[VMEM, VMEM, pl.BlockSpec(memory_space=pl.ANY)],
            scratch=[pltpu.SemaphoreType.DMA((2,))],
            aliases={3: 0},
        )
        arrived, grad_input = lax.optimization_barrier((arrived, grad_input))
    grad_down, grad_up = call(
        total_kernel,
        (
            shaped(slots, rank, down_part, dtype=jnp.float32),
            shaped(slots, rank, up_part, dtype=jnp.float32),
        ),
        (VMEM, VMEM),
        want,
        count,
        arrived,
        smem=2,
    )
    if not by_permute:
        weight = lax.all_gather(value_weight, "fsdp", axis=0, tiled=True)
        adapter_term = jnp.einsum(
            "tr,krd->tkd", back, factors[:, :, :down_part], preferred_element_type=jnp.float32
        )
        frozen_term = jnp.einsum(
            "tc,dc->td", value_cotangent, weight, preferred_element_type=jnp.float32
        )
        grad_input = (frozen_term + adapter_term.reshape(tok_rows, width)).astype(bf16)
    return (grad_input, grad_down, grad_up)


def solution(mesh):
    return jax.shard_map(
        per_device,
        mesh=mesh,
        in_specs=(
            P(("dp", "fsdp"), None),
            P(("dp", "fsdp"), None),
            P("fsdp", None),
            P("dp", None, "fsdp"),
            P("dp", None, "fsdp"),
            P(),
            P(),
        ),
        out_specs=(P(("dp", "fsdp"), None), P("dp", None, "fsdp"), P("dp", None, "fsdp")),
        check_vma=False,
    )
```

time: 82.1 us -> 83.8 us (1.021)
  the two profiles are of different devices: /device:TPU:0 before, /device:TPU:1 now
where the time goes in v3:
time: 83.8 us; the launch traced here: 83.1 us
  waiting for transfers between devices  29.5 us (35%)
  starting transfers between devices  21.9 us (26%)
  Pallas kernels  17.3 us (21%)
  blocking collectives  9.25 us (11%)
  local copies, waits for them, and re-layouts  4.35 us (5%)
    ppermute x7, waiting for transfers between devices, cross(): lax.ppermute(array, 'fsdp', [(i, i ^ bit) for i in range(fsdp_count)])  26.5 us
    pallas_call x8, Pallas kernels, call(): pl.pallas_call(kernel, out_shape=out_shape, in_specs=[SMEM] * smem + (spe...  17.3 us
    all_to_all x1, blocking collectives, per_device(): got = lax.all_to_all(grads, 'fsdp', split_axis=0, concat_axis=0, tiled=True)  9.25 us
    all_to_all x1, starting transfers between devices, per_device(): owned = lax.all_to_all(send, 'dp', split_axis=0, concat_axis=0, tiled=True)  6.97 us
    ppermute x7, starting transfers between devices, cross(): lax.ppermute(array, 'fsdp', [(i, i ^ bit) for i in range(fsdp_count)])  5.99 us
    all_to_all x1, starting transfers between devices, per_device(): lax.all_to_all(sums, 'dp', split_axis=0, concat_axis=0, tiled=True)  5.57 us
    all_to_all x1, starting transfers between devices, per_device(): lax.all_to_all(share, 'fsdp', split_axis=0, concat_axis=0, tiled=True)  3.39 us
    unnamed x28, local copies, waits for them, and re-layouts  3.22 us
  transfers between devices with their start and end apart: 10, of which 4 were waited for; matrix products, arithmetic and copies ran while one was open for 1% of the time, Pallas kernels for 10%

profile of v3, /device:TPU:1, one launch (start us, length us, event | category | flops | bytes accessed | tf_op | source)
XLA Modules:
  0.0 83.1 jit_solution(17002388747568843087)
XLA Ops:
  0.6 0.0 copy-start.10
  0.6 0.0 copy-start.9
  0.7 0.0 copy-start.13
  0.7 2.0 %shard_map.94 = (bf16[8,16,1920]{2,1,0:T(8,128)(2,1)}, s32[8]{0:T(128)}, s32[5]{0:T(128)}) custom-call(s32[1]{0:T(128)} %bitcast.me_ref, s32[32]{0:T(128)} %apb_ref.5, s32[40]{0:T(128)} %row_ref.5, bf16[5,16,1792]{2,1,0:T(8,128)(2,1)} %down_ref.1, bf16[5,16,128]{2,1,0:T(8,128)(2,1)} %up_ref.1), custom_call_target="tpu_custom_call" | custom-call | tf_op jit(solution)/shard_map/pallas_call | solution.py:187
  2.7 0.1 collective-permute-start.2
  2.8 7.0 %all-to-all-start = ((bf16[8,16,1920]{2,1,0:T(8,128)(2,1)}), bf16[8,16,1920]{2,1,0:T(8,128)(2,1)S(1)}, u32[]{:S(2)}, u32[]{:S(2)}) async-start(bf16[8,16,1920]{2,1,0:T(8,128)(2,1)} %get-tuple-element.27), calls=%async_computation | async-start | bytes 983040 | tf_op jit(solution)/shard_map/all_to_all | solution.py:244
  9.8 1.1 %slice.3 = bf16[640,512]{1,0:T(8,128)(2,1)S(1)} slice(bf16[1792,512]{1,0:T(8,128)(2,1)} %w0_ref), slice={[0:640], [0:512]} | slice | bytes 1310720 | tf_op jit(solution)/shard_map/slice | solution.py:246
  10.9 1.3 %collective-permute-start = (bf16[640,512]{1,0:T(8,128)(2,1)S(1)}, bf16[640,512]{1,0:T(8,128)(2,1)S(1)}, u32[]{:S(2)}, u32[]{:S(2)}) collective-permute-start(bf16[640,512]{1,0:T(8,128)(2,1)S(1)} %slice.3), channel_id=1, source_target_pairs={{0,2},{1,3},{2,0},{3,1},{4,6},{5,7},{6,4},{7,5},{8,10},{9,11},{10,... | collective-permute-start | bytes 1966088 | tf_op jit(solution)/shard_map/ppermute | solution.py:225
  12.2 0.0 copy-done.13
  12.3 0.2 collective-permute-start.1
  12.5 17.3 %collective-permute-done.1.dy2_ref = bf16[128,512]{1,0:T(8,128)(2,1)S(1)} collective-permute-done((bf16[128,512]{1,0:T(8,128)(2,1)S(1)}, bf16[128,512]{1,0:T(8,128)(2,1)S(1)}, u32[]{:S(2)}, u32[]{:S(2)}) %collective-permute-start.1) | collective-permute-done | bytes 131104 | tf_op jit(solution)/shard_map/ppermute | solution.py:225
  29.8 0.0 copy-start.4
  29.8 0.0 collective-permute-done.w2_ref
  29.8 0.0 all-to-all-done.got_ref
  29.8 1.2 %collective-permute-start.3 = (bf16[640,512]{1,0:T(8,128)(2,1)S(1)}, bf16[640,512]{1,0:T(8,128)(2,1)}, u32[]{:S(2)}, u32[]{:S(2)}) collective-permute-start(bf16[640,512]{1,0:T(8,128)(2,1)S(1)} %collective-permute-done.w2_ref), channel_id=1, source_target_pairs={{0,1},{1,0},{2,3},{3,2},{4,5},{5,4},{6,7},{7,6},{8,9},{9,8},{10,11... | collective-permute-start | bytes 1966088 | tf_op jit(solution)/shard_map/ppermute | solution.py:225
  31.0 0.0 copy-done.10
  31.0 0.0 copy-done.9
  31.0 1.3 %shard_map.95.share_ref = bf16[4,16,1920]{2,1,0:T(8,128)(2,1)} custom-call(s32[1]{0:T(128)} %bitcast.me_ref, s32[32]{0:T(128)S(1)} %copy-done.9, s32[40]{0:T(128)S(1)} %copy-done.10, bf16[8,16,1920]{2,1,0:T(8,128)(2,1)S(1)} %all-to-all-done.got_ref), custom_call_target="tpu_custom_call" | custom-call | tf_op jit(solution)/shard_map/pallas_call | solution.py:187
  32.3 3.4 %all-to-all-start.1 = ((bf16[4,16,1920]{2,1,0:T(8,128)(2,1)}), bf16[4,16,1920]{2,1,0:T(8,128)(2,1)S(1)}, u32[]{:S(2)}, u32[]{:S(2)}) async-start(bf16[4,16,1920]{2,1,0:T(8,128)(2,1)} %shard_map.95.share_ref), calls=%async_computation.1 | async-start | bytes 491520 | tf_op jit(solution)/shard_map/all_to_all | solution.py:259
  35.7 0.0 copy-start
  35.7 0.1 collective-permute-start.4
  35.8 1.3 %collective-permute-done.4.dy3_ref = bf16[128,512]{1,0:T(8,128)(2,1)S(1)} collective-permute-done((bf16[128,512]{1,0:T(8,128)(2,1)S(1)}, bf16[128,512]{1,0:T(8,128)(2,1)S(1)}, u32[]{:S(2)}, u32[]{:S(2)}) %collective-permute-start.4) | collective-permute-done | bytes 131104 | tf_op jit(solution)/shard_map/ppermute | solution.py:225
  37.1 0.0 copy-start.6
  37.1 0.6 copy-done.6
  37.8 2.9 %all-to-all-done.1.fac_ref = bf16[4,16,1920]{2,1,0:T(8,128)(2,1)S(1)} async-done(((bf16[4,16,1920]{2,1,0:T(8,128)(2,1)}), bf16[4,16,1920]{2,1,0:T(8,128)(2,1)S(1)}, u32[]{:S(2)}, u32[]{:S(2)}) %all-to-all-start.1) | async-done | bytes 245792 | tf_op jit(solution)/shard_map/all_to_all | solution.py:259
  40.7 0.0 copy-start.1
  40.7 0.0 collective-permute-done.3.w3_ref
  40.7 0.0 collective-permute-done.2.w1_ref
  40.7 0.7 copy-done.1
  41.4 4.2 %shard_map.96 = (bf16[4,16,2048]{2,1,0:T(8,128)(2,1)}, bf16[128,16]{1,0:T(8,128)(2,1)}, bf16[512,128]{1,0:T(8,128)(2,1)}) custom-call(bf16[128,7168]{1,0:T(8,128)(2,1)} %x_ref.1, bf16[128,512]{1,0:T(8,128)(2,1)} %dy_ref.1, bf16[4,16,1920]{2,1,0:T(8,128)(2,1)} %copy-done.1), custom_call_target="tpu_custom_call" | custom-call | tf_op jit(solution)/shard_map/pallas_call | solution.py:187
  45.7 0.0 copy-done.4
  45.7 9.3 %all_to_all.20.got_ref = bf16[4,16,2048]{2,1,0:T(8,128)(2,1)S(1)} all-to-all(bf16[4,16,2048]{2,1,0:T(8,128)(2,1)} %get-tuple-element.33), channel_id=1, replica_groups=mesh['dp'=8,'fsdp'=4] {'fsdp'}, dimensions={0} | all-to-all | bytes 524288 | tf_op jit(solution)/shard_map/all_to_all | solution.py:280
  54.9 1.5 %shard_map.97 = bf16[8,16,1920]{2,1,0:T(8,128)(2,1)} custom-call(s32[1]{0:T(128)} %bitcast.me_ref, s32[32]{0:T(128)S(1)} %copy-done.9, s32[40]{0:T(128)S(1)} %copy-done.10, bf16[4,16,2048]{2,1,0:T(8,128)(2,1)S(1)} %all_to_all.20.got_ref), custom_call_target="tpu_custom_call" | custom-call | tf_op jit(solution)/shard_map/pallas_call | solution.py:187
  56.4 0.0 copy-start.2
  56.4 0.0 copy-start.8
  56.4 5.6 %all-to-all-start.3 = ((bf16[8,16,1920]{2,1,0:T(8,128)(2,1)}), bf16[8,16,1920]{2,1,0:T(8,128)(2,1)S(1)}, u32[]{:S(2)}, u32[]{:S(2)}) async-start(bf16[8,16,1920]{2,1,0:T(8,128)(2,1)} %shard_map.97), calls=%async_computation.3 | async-start | bytes 983040 | tf_op jit(solution)/shard_map/all_to_all | solution.py:290
  62.0 0.0 copy-start.3
  62.0 0.0 copy-done
  62.0 0.0 copy-start.5
  62.0 0.9 %copy-done.5 = bf16[128,512]{1,0:T(8,128)(2,1)S(1)} copy-done((bf16[128,512]{1,0:T(8,128)(2,1)S(1)}, bf16[128,512]{1,0:T(8,128)(2,1)}, u32[]{:S(2)}) %copy-start.5) | copy-done | bytes 131096
  62.9 0.0 copy-start.7
  62.9 0.9 %copy-done.7 = bf16[128,512]{1,0:T(8,128)(2,1)S(1)} copy-done((bf16[128,512]{1,0:T(8,128)(2,1)S(1)}, bf16[128,512]{1,0:T(8,128)(2,1)}, u32[]{:S(2)}) %copy-start.7) | copy-done | bytes 131096
  63.8 1.8 %shard_map.98 = (bf16[128,1152]{1,0:T(8,128)(2,1)S(1)}, bf16[128,1152]{1,0:T(8,128)(2,1)S(1)}) custom-call(s32[1]{0:T(128)} %bitcast.1.at_ref, bf16[1792,512]{1,0:T(8,128)(2,1)S(1)} %copy-done, bf16[128,512]{1,0:T(8,128)(2,1)S(1)} %copy-done.5, bf16[128,512]{1,0:T(8,128)(2,1)S(1)} %copy-done.7, bf16[4,16,1920]{2,1,0:T(8,128)(2,1)} %shard_map.95.share_ref, ...), custom_call_target="tpu_custom_call" | custom-call | tf_op jit(solution)/shard_map/pallas_call | solution.py:187
  65.6 0.6 collective-permute-start.5
  66.2 2.4 %collective-permute-start.6 = (bf16[128,1152]{1,0:T(8,128)(2,1)S(1)}, bf16[128,1152]{1,0:T(8,128)(2,1)S(1)}, u32[]{:S(2)}, u32[]{:S(2)}) collective-permute-start(bf16[128,1152]{1,0:T(8,128)(2,1)S(1)} %get-tuple-element.37), channel_id=1, source_target_pairs={{0,3},{1,2},{2,1},{3,0},{4,7},{5,6},{6,5},{7,4},{8,11},{9,10},{10,... | collective-permute-start | bytes 884744 | tf_op jit(solution)/shard_map/ppermute | solution.py:225
  68.6 0.0 copy-done.2
  68.6 0.0 copy-done.8
  68.6 0.0 copy-done.3
  68.6 4.2 %shard_map.99.in_ref = bf16[128,7168]{1,0:T(8,128)(2,1)} custom-call(s32[1]{0:T(128)} %bitcast.1.at_ref, bf16[512,128]{1,0:T(8,128)(2,1)S(1)} %copy-done.3, bf16[128,16]{1,0:T(8,128)(2,1)S(1)} %copy-done.8, bf16[4,16,1920]{2,1,0:T(8,128)(2,1)S(1)} %copy-done.2, bf16[1792,512]{1,0:T(8,128)(2,1)S(1)} %copy-done, ...), custom_call_target="tpu_custom_call" | custom-call | tf_op jit(solution)/shard_map/pallas_call | solution.py:187
  72.8 0.0 copy-start.11
  72.8 0.0 copy-start.12
  72.8 0.0 collective-permute-done.5.z2_ref
  72.8 7.9 %collective-permute-done.6.z3_ref = bf16[128,1152]{1,0:T(8,128)(2,1)S(1)} collective-permute-done((bf16[128,1152]{1,0:T(8,128)(2,1)S(1)}, bf16[128,1152]{1,0:T(8,128)(2,1)S(1)}, u32[]{:S(2)}, u32[]{:S(2)}) %collective-permute-start.6) | collective-permute-done | bytes 294944 | tf_op jit(solution)/shard_map/ppermute | solution.py:225
  80.7 0.8 shard_map.100
  81.5 0.0 all-to-all-done.3.got_ref
  81.6 0.0 copy-done.11
  81.6 0.0 copy-done.12
  81.6 1.6 %shard_map.101 = (f32[5,16,1792]{2,1,0:T(8,128)}, f32[5,16,128]{2,1,0:T(8,128)}) custom-call(s32[8]{0:T(128)S(1)} %copy-done.11, s32[5]{0:T(128)S(1)} %copy-done.12, bf16[8,16,1920]{2,1,0:T(8,128)(2,1)S(1)} %all-to-all-done.3.got_ref), custom_call_target="tpu_custom_call" | custom-call | tf_op jit(solution)/shard_map/pallas_call | solution.py:187
Async XLA Ops:
  0.6 30.4 %copy-start.10 = (s32[40]{0:T(128)S(1)}, s32[40]{0:T(128)}, u32[]{:S(2)}) copy-start(s32[40]{0:T(128)} %row_ref.5) | copy-start | bytes 484
  0.6 30.4 %copy-start.9 = (s32[32]{0:T(128)S(1)}, s32[32]{0:T(128)}, u32[]{:S(2)}) copy-start(s32[32]{0:T(128)} %apb_ref.5) | copy-start | bytes 388
  0.7 11.6 %copy-start.13 = (bf16[128,512]{1,0:T(8,128)(2,1)S(1)}, bf16[128,512]{1,0:T(8,128)(2,1)}, u32[]{:S(2)}) copy-start(bf16[128,512]{1,0:T(8,128)(2,1)} %dy_ref.1) | copy-start | bytes 393220
  2.7 38.0 %collective-permute-start.2 = (bf16[1792,512]{1,0:T(8,128)(2,1)}, bf16[1792,512]{1,0:T(8,128)(2,1)}, u32[]{:S(2)}, u32[]{:S(2)}) collective-permute-start(bf16[1792,512]{1,0:T(8,128)(2,1)} %w0_ref), channel_id=1, source_target_pairs={{0,1},{1,0},{2,3},{3,2},{4,5},{5,4},{6,7},{7,6},{8,9},{9,8},{10,11... | collective-permute-start | bytes 5505032 | tf_op jit(solution)/shard_map/ppermute | solution.py:225
  2.8 27.0 %all-to-all-start = ((bf16[8,16,1920]{2,1,0:T(8,128)(2,1)}), bf16[8,16,1920]{2,1,0:T(8,128)(2,1)S(1)}, u32[]{:S(2)}, u32[]{:S(2)}) async-start(bf16[8,16,1920]{2,1,0:T(8,128)(2,1)} %get-tuple-element.27), calls=%async_computation | async-start | bytes 983040 | tf_op jit(solution)/shard_map/all_to_all | solution.py:244
  10.9 18.9 %collective-permute-start = (bf16[640,512]{1,0:T(8,128)(2,1)S(1)}, bf16[640,512]{1,0:T(8,128)(2,1)S(1)}, u32[]{:S(2)}, u32[]{:S(2)}) collective-permute-start(bf16[640,512]{1,0:T(8,128)(2,1)S(1)} %slice.3), channel_id=1, source_target_pairs={{0,2},{1,3},{2,0},{3,1},{4,6},{5,7},{6,4},{7,5},{8,10},{9,11},{10,... | collective-permute-start | bytes 1966088 | tf_op jit(solution)/shard_map/ppermute | solution.py:225
  12.3 17.6 %collective-permute-start.1 = (bf16[128,512]{1,0:T(8,128)(2,1)S(1)}, bf16[128,512]{1,0:T(8,128)(2,1)S(1)}, u32[]{:S(2)}, u32[]{:S(2)}) collective-permute-start(bf16[128,512]{1,0:T(8,128)(2,1)S(1)} %copy-done.13), channel_id=1, source_target_pairs={{0,2},{1,3},{2,0},{3,1},{4,6},{5,7},{6,4},{7,5},{8,10},{9,11},{10,... | collective-permute-start | bytes 393224 | tf_op jit(solution)/shard_map/ppermute | solution.py:225
  29.8 15.8 %copy-start.4 = (bf16[128,512]{1,0:T(8,128)(2,1)}, bf16[128,512]{1,0:T(8,128)(2,1)S(1)}, u32[]{:S(2)}) copy-start(bf16[128,512]{1,0:T(8,128)(2,1)S(1)} %collective-permute-done.1.dy2_ref) | copy-start | bytes 393220
  29.8 10.9 %collective-permute-start.3 = (bf16[640,512]{1,0:T(8,128)(2,1)S(1)}, bf16[640,512]{1,0:T(8,128)(2,1)}, u32[]{:S(2)}, u32[]{:S(2)}) collective-permute-start(bf16[640,512]{1,0:T(8,128)(2,1)S(1)} %collective-permute-done.w2_ref), channel_id=1, source_target_pairs={{0,1},{1,0},{2,3},{3,2},{4,5},{5,4},{6,7},{7,6},{8,9},{9,8},{10,11... | collective-permute-start | bytes 1966088 | tf_op jit(solution)/shard_map/ppermute | solution.py:225
  32.3 8.4 %all-to-all-start.1 = ((bf16[4,16,1920]{2,1,0:T(8,128)(2,1)}), bf16[4,16,1920]{2,1,0:T(8,128)(2,1)S(1)}, u32[]{:S(2)}, u32[]{:S(2)}) async-start(bf16[4,16,1920]{2,1,0:T(8,128)(2,1)} %shard_map.95.share_ref), calls=%async_computation.1 | async-start | bytes 491520 | tf_op jit(solution)/shard_map/all_to_all | solution.py:259
  35.7 26.3 %copy-start = (bf16[1792,512]{1,0:T(8,128)(2,1)S(1)}, bf16[1792,512]{1,0:T(8,128)(2,1)}, u32[]{:S(2)}) copy-start(bf16[1792,512]{1,0:T(8,128)(2,1)} %w0_ref) | copy-start | bytes 5505028
  35.7 1.4 %collective-permute-start.4 = (bf16[128,512]{1,0:T(8,128)(2,1)S(1)}, bf16[128,512]{1,0:T(8,128)(2,1)S(1)}, u32[]{:S(2)}, u32[]{:S(2)}) collective-permute-start(bf16[128,512]{1,0:T(8,128)(2,1)S(1)} %collective-permute-done.1.dy2_ref), channel_id=1, source_target_pairs={{0,1},{1,0},{2,3},{3,2},{4,5},{5,4},{6,7},{7,6},{8,9},{9,8},{10,11... | collective-permute-start | bytes 393224 | tf_op jit(solution)/shard_map/ppermute | solution.py:225
  37.1 0.6 copy-start.6
  40.7 0.7 copy-start.1
  56.4 12.2 %copy-start.2 = (bf16[4,16,1920]{2,1,0:T(8,128)(2,1)S(1)}, bf16[4,16,1920]{2,1,0:T(8,128)(2,1)}, u32[]{:S(2)}) copy-start(bf16[4,16,1920]{2,1,0:T(8,128)(2,1)} %copy-done.1) | copy-start | bytes 737284
  56.4 12.2 %copy-start.8 = (bf16[128,16]{1,0:T(8,128)(2,1)S(1)}, bf16[128,16]{1,0:T(8,128)(2,1)}, u32[]{:S(2)}) copy-start(bf16[128,16]{1,0:T(8,128)(2,1)} %get-tuple-element.39.back_ref) | copy-start | bytes 12292
  56.4 25.1 %all-to-all-start.3 = ((bf16[8,16,1920]{2,1,0:T(8,128)(2,1)}), bf16[8,16,1920]{2,1,0:T(8,128)(2,1)S(1)}, u32[]{:S(2)}, u32[]{:S(2)}) async-start(bf16[8,16,1920]{2,1,0:T(8,128)(2,1)} %shard_map.97), calls=%async_computation.3 | async-start | bytes 983040 | tf_op jit(solution)/shard_map/all_to_all | solution.py:290
  62.0 6.6 %copy-start.3 = (bf16[512,128]{1,0:T(8,128)(2,1)S(1)}, bf16[512,128]{1,0:T(8,128)(2,1)}, u32[]{:S(2)}) copy-start(bf16[512,128]{1,0:T(8,128)(2,1)} %get-tuple-element.38.dy_t_ref) | copy-start | bytes 393220
  62.0 0.9 %copy-start.5 = (bf16[128,512]{1,0:T(8,128)(2,1)S(1)}, bf16[128,512]{1,0:T(8,128)(2,1)}, u32[]{:S(2)}) copy-start(bf16[128,512]{1,0:T(8,128)(2,1)} %copy-done.4) | copy-start | bytes 393220
  62.9 0.9 %copy-start.7 = (bf16[128,512]{1,0:T(8,128)(2,1)S(1)}, bf16[128,512]{1,0:T(8,128)(2,1)}, u32[]{:S(2)}) copy-start(bf16[128,512]{1,0:T(8,128)(2,1)} %copy-done.6) | copy-start | bytes 393220
  65.6 7.2 %collective-permute-start.5 = (bf16[128,1152]{1,0:T(8,128)(2,1)S(1)}, bf16[128,1152]{1,0:T(8,128)(2,1)S(1)}, u32[]{:S(2)}, u32[]{:S(2)}) collective-permute-start(bf16[128,1152]{1,0:T(8,128)(2,1)S(1)} %get-tuple-element.36), channel_id=1, source_target_pairs={{0,2},{1,3},{2,0},{3,1},{4,6},{5,7},{6,4},{7,5},{8,10},{9,11},{10,... | collective-permute-start | bytes 884744 | tf_op jit(solution)/shard_map/ppermute | solution.py:225
  66.2 14.5 %collective-permute-start.6 = (bf16[128,1152]{1,0:T(8,128)(2,1)S(1)}, bf16[128,1152]{1,0:T(8,128)(2,1)S(1)}, u32[]{:S(2)}, u32[]{:S(2)}) collective-permute-start(bf16[128,1152]{1,0:T(8,128)(2,1)S(1)} %get-tuple-element.37), channel_id=1, source_target_pairs={{0,3},{1,2},{2,1},{3,0},{4,7},{5,6},{6,5},{7,4},{8,11},{9,10},{10,... | collective-permute-start | bytes 884744 | tf_op jit(solution)/shard_map/ppermute | solution.py:225
  72.8 8.8 %copy-start.11 = (s32[8]{0:T(128)S(1)}, s32[8]{0:T(128)}, u32[]{:S(2)}) copy-start(s32[8]{0:T(128)} %get-tuple-element.44.want_ref) | copy-start | bytes 100
  72.8 8.8 %copy-start.12 = (s32[5]{0:T(128)S(1)}, s32[5]{0:T(128)}, u32[]{:S(2)}) copy-start(s32[5]{0:T(128)} %get-tuple-element.45.count_ref) | copy-start | bytes 64

commit v4 on v3

--- a/solution.py
+++ b/solution.py
@@ -13,6 +13,7 @@
 
 SMEM = pl.BlockSpec(memory_space=pltpu.SMEM)
 VMEM = pl.BlockSpec(memory_space=pltpu.VMEM)
+ANY = pl.BlockSpec(memory_space=pl.ANY)
 NT = (((1,), (1,)), ((), ()))
 
 
@@ -28,7 +29,29 @@
     return a.astype(jnp.float32).T.astype(a.dtype)
 
 
-def pick_kernel(group_blocks, me_ref, apb_ref, row_ref, down_ref, up_ref, send_ref, want_ref, count_ref):
+def fetch(sources, targets, sems):
+    copies = [
+        pltpu.make_async_copy(source, target, sems.at[i])
+        for i, (source, target) in enumerate(zip(sources, targets))
+    ]
+    for copy in copies:
+        copy.start()
+    return copies
+
+
+def copy_kernel(from_ref, to_ref, sem):
+    copy = pltpu.make_async_copy(from_ref, to_ref, sem)
+    copy.start()
+    copy.wait()
+
+
+def pick_kernel(
+    group_blocks, me_ref, apb_hbm, row_hbm, down_hbm, up_hbm, send_ref, want_ref, count_ref,
+    apb_ref, row_ref, down_ref, up_ref, sems,
+):
+    copies = fetch(
+        (apb_hbm, row_hbm, down_hbm, up_hbm), (apb_ref, row_ref, down_ref, up_ref), sems
+    )
     slots, _, down_part = down_ref.shape
     up_part = up_ref.shape[2]
     up_at = round_up(down_part)
@@ -36,6 +59,8 @@
     first = me_ref[0] * slots
     for s in range(slots):
         count_ref[s] = 0
+    copies[0].wait()
+    copies[1].wait()
 
     def group(g, carry):
         want_ref[g] = 0
@@ -47,12 +72,19 @@
                 want_ref[g] = local
                 count_ref[local] = count_ref[local] + 1
 
+        return carry
+
+    lax.fori_loop(0, groups, group, 0)
+    copies[2].wait()
+    copies[3].wait()
+
+    def put(g, carry):
         slot = want_ref[g]
         send_ref[g, :, :down_part] = down_ref[slot]
         send_ref[g, :, up_at : up_at + up_part] = up_ref[slot]
         return carry
 
-    lax.fori_loop(0, groups, group, 0)
+    lax.fori_loop(0, groups, put, 0)
 
 
 def share_kernel(slots, me_ref, apb_ref, row_ref, got_ref, out_ref):
@@ -63,19 +95,11 @@
 
 
 def block_kernel(
-    down_part, up_part, x_ref, dy_ref, fac_ref, grads_ref, back_ref, dy_t_ref, x_buf, sems
+    down_part, up_part, x_ref, dy_ref, fac_ref, grads_ref, back_ref
 ):
     shares = fac_ref.shape[0]
     up_at = round_up(down_part)
     back_at = up_at + round_up(up_part)
-    parts = shares if down_part % LANES == 0 else 1
-    copies = []
-    for k in range(parts):
-        columns = pl.ds(k * (x_ref.shape[1] // parts), x_ref.shape[1] // parts)
-        copies.append(
-            pltpu.make_async_copy(x_ref.at[:, columns], x_buf.at[:, columns], sems.at[k])
-        )
-        copies[k].start()
     low_t = jnp.zeros((fac_ref.shape[1], BLOCK), jnp.float32)
     back_t = jnp.zeros((fac_ref.shape[1], BLOCK), jnp.float32)
     for k in range(shares):
@@ -87,11 +111,8 @@
     scaled = adapter_scale * back_t
     back = scaled.astype(jnp.bfloat16)
     back_ref[...] = scaled.T.astype(jnp.bfloat16)
-    dy_t_ref[...] = turned(dy_ref[...])
     for k in range(shares):
-        if k < parts:
-            copies[k].wait()
-        x = x_buf[:, k * down_part : (k + 1) * down_part]
+        x = x_ref[:, k * down_part : (k + 1) * down_part]
         low_t += dot(fac_ref[k, :, :down_part], x, NT)
         grads_ref[k, :, :down_part] = dot(back, x).astype(jnp.bfloat16)
         grads_ref[k, :, back_at:] = back
@@ -131,35 +152,67 @@
         up_ref[s] = up_ref[s] / divisor
 
 
-def far_kernel(at_ref, w_ref, dy2_ref, dy3_ref, share_ref, got_ref, z2_ref, z3_ref):
+def far_kernel(
+    near, at_ref, w_hbm, y2_hbm, y3_hbm, share_ref, got_ref, z2_ref, z3_ref, w_ref, dy_ref, sems
+):
     rows = z2_ref.shape[1]
-    tokens = dy2_ref.shape[0]
-    start = w_ref.shape[0] - rows
-    dy_t = jnp.concatenate([turned(dy2_ref[...]), turned(dy3_ref[...])], axis=1)
-    frozen_t = dot(w_ref[start:, :], dy_t)
+    tokens = z2_ref.shape[0]
+    taken = pl.ds(y2_hbm.shape[0] - tokens, tokens)
+    copies = fetch(
+        [y2_hbm.at[taken], y3_hbm.at[taken], w_hbm.at[pl.ds(near, rows)]],
+        [dy_ref.at[pl.ds(0, tokens)], dy_ref.at[pl.ds(tokens, tokens)], w_ref],
+        sems,
+    )
+    copies[0].wait()
+    copies[1].wait()
+    dy_t = turned(dy_ref[...])
+    copies[2].wait()
+    frozen_t = dot(w_ref[...], dy_t)
     for i, z_ref in enumerate((z2_ref, z3_ref)):
         peer = lax.bitwise_xor(at_ref[0], 2 + i)
         back = turned(got_ref[peer, :, got_ref.shape[2] - tokens :])
         z_ref[...] = (
             frozen_t[:, i * tokens : (i + 1) * tokens].T
-            + dot(back, share_ref[peer, :, start : w_ref.shape[0]])
+            + dot(back, share_ref[peer, :, near : near + rows])
         ).astype(jnp.bfloat16)
 
 
 def input_kernel(
-    at_ref, dy_t_ref, back_ref, fac_ref, w0_ref, w1_ref, w2_ref, w3_ref, out_ref, buf, sems
+    at_ref, side_ref, back_ref, fac_ref, dy_hbm, y2_hbm, y3_hbm, x2_hbm, x3_hbm, w0_hbm, w1_hbm,
+    out_ref, dy_ref, few_ref, w0_ref, w1_ref, buf, fetch_sems, sems,
 ):
     part = w0_ref.shape[0]
+    taken = few_ref.shape[1]
+    side = side_ref[0] * taken
+    few = [a.at[pl.ds(0, taken)] for a in (y2_hbm, y3_hbm, x2_hbm, x3_hbm)]
+    fetches = fetch(
+        (*few, w0_hbm, w1_hbm, dy_hbm),
+        (*(few_ref.at[i] for i in range(4)), w0_ref, w1_ref, dy_ref),
+        fetch_sems,
+    )
+    fetches[6].wait()
+    dy_t = turned(dy_ref[...])
     copies = []
-    for k, w_ref in enumerate((w0_ref, w1_ref, w2_ref, w3_ref)):
-        rows = w_ref.shape[0]
+    for i, (k, w_ref, start, rows) in enumerate(
+        (
+            (2, few_ref.at[0], side, taken),
+            (3, few_ref.at[1], side, taken),
+            (2, few_ref.at[2], taken - side, taken),
+            (3, few_ref.at[3], taken - side, taken),
+            (0, w0_ref, 0, part),
+            (1, w1_ref, 0, part),
+        )
+    ):
+        fetches[i].wait()
         peer = lax.bitwise_xor(at_ref[0], k)
-        buf[k, :, :rows] = (
-            dot(w_ref[...], dy_t_ref[...]).T + dot(back_ref[...], fac_ref[peer, :, :rows])
+        start = pl.multiple_of(start, LANES)
+        buf[i, :, :rows] = (
+            dot(w_ref[...], dy_t).T
+            + dot(back_ref[...], fac_ref[peer, :, pl.ds(start, rows)])
         ).astype(jnp.bfloat16)
-        first = pl.multiple_of(peer * part, LANES)
+        first = pl.multiple_of(peer * part + start, LANES)
         copy = pltpu.make_async_copy(
-            buf.at[k, :, pl.ds(0, rows)], out_ref.at[:, pl.ds(first, rows)], sems.at[k]
+            buf.at[i, :, pl.ds(0, rows)], out_ref.at[:, pl.ds(first, rows)], sems.at[i]
         )
         copy.start()
         copies.append(copy)
@@ -181,8 +234,12 @@
         copy.wait()
 
 
+def in_hbm(*arrays):
+    return [pltpu.with_memory_space_constraint(a, pltpu.HBM) for a in arrays]
+
+
 def call(
-    kernel, out_shape, out_specs, *operands, smem=0, scratch=(), vmem=32, specs=None, aliases=None
+    kernel, out_shape, out_specs, *operands, smem=0, scratch=(), vmem=8, specs=None, aliases=None
 ):
     return pl.pallas_call(
         kernel,
@@ -219,10 +276,12 @@
         return jax.ShapeDtypeStruct(shape, dtype)
 
     by_permute = fsdp_count == 4 and down_part % 256 == 0
-    near_rows = 3 * down_part // 8 // LANES * LANES
-
-    def cross(array, bit):
-        return lax.ppermute(array, "fsdp", [(i, i ^ bit) for i in range(fsdp_count)])
+    by_permute = by_permute and dp_count % 2 == 0
+    side_rows = down_part // 4 // LANES * LANES
+    near_rows = 2 * side_rows
+
+    def cross(array, bit, axis="fsdp"):
+        return lax.ppermute(array, axis, [(i, i ^ bit) for i in range(lax.axis_size(axis))])
 
     index = (me, adapter_per_block, adapter_table_row)
     send, want, count = call(
@@ -233,21 +292,38 @@
             shaped(slots, dtype=jnp.int32),
         ),
         (VMEM, SMEM, SMEM),
-        *index,
-        adapter_down_table,
-        adapter_up_table,
-        smem=3,
-        vmem=60,
+        me,
+        *in_hbm(*index[1:], adapter_down_table, adapter_up_table),
+        smem=1,
+        specs=[ANY] * 4,
+        scratch=[
+            pltpu.SMEM(adapter_per_block.shape, jnp.int32),
+            pltpu.SMEM(adapter_table_row.shape, jnp.int32),
+            pltpu.VMEM(adapter_down_table.shape, bf16),
+            pltpu.VMEM(adapter_up_table.shape, bf16),
+            pltpu.SemaphoreType.DMA((4,)),
+        ],
     )
     if by_permute:
         value_weight, send = lax.optimization_barrier((value_weight, send))
     owned = lax.all_to_all(send, "dp", split_axis=0, concat_axis=0, tiled=True)
     if by_permute:
-        far = cross(value_weight[:near_rows], 2)
-        dy2 = cross(value_cotangent, 2)
-        owned, far, dy2 = lax.optimization_barrier((owned, far, dy2))
-        near = cross(value_weight, 1), far, cross(far, 1)
-        dys = dy2, cross(dy2, 1)
+        side = me & 1
+        some = lax.dynamic_slice_in_dim(value_weight, side[0] * side_rows, side_rows, 0)
+        y2 = cross(jnp.concatenate([some, value_cotangent], axis=0), 2)
+        at_hand, _ = lax.optimization_barrier((projection_input, send))
+        at_hand = call(
+            copy_kernel,
+            shaped(tok_rows, width),
+            ANY,
+            *in_hbm(at_hand),
+            specs=[ANY],
+            scratch=[pltpu.SemaphoreType.DMA],
+        )
+        owned, y2, at_hand = lax.optimization_barrier((owned, y2, at_hand))
+        near = cross(value_weight, 1), cross(y2, 1)
+    else:
+        at_hand = projection_input
     share = call(
         functools.partial(share_kernel, slots),
         shaped(fsdp_count, rank, wide),
@@ -256,28 +332,26 @@
         owned,
         smem=3,
     )
+    if by_permute:
+        x2, share = lax.optimization_barrier((y2, share))
+        x2 = cross(x2, 1, "dp")
     factors = lax.all_to_all(share, "fsdp", split_axis=0, concat_axis=0, tiled=True)
-    if by_permute:
-        factors, near, dys = lax.optimization_barrier((factors, near, dys))
-    grads, back, dy_t = call(
+    grads, back = call(
         functools.partial(block_kernel, down_part, up_part),
         (
             shaped(fsdp_count, rank, wide + BLOCK),
             shaped(BLOCK, rank),
-            shaped(value_cotangent.shape[1], BLOCK),
         ),
-        (VMEM, VMEM, VMEM),
-        projection_input,
+        (VMEM, VMEM),
+        at_hand,
         value_cotangent,
         factors,
-        specs=[pl.BlockSpec(memory_space=pl.ANY), VMEM, VMEM],
-        scratch=[
-            pltpu.VMEM((BLOCK, width), bf16),
-            pltpu.SemaphoreType.DMA((fsdp_count,)),
-        ],
-        vmem=56,
+        vmem=20,
     )
     got = lax.all_to_all(grads, "fsdp", split_axis=0, concat_axis=0, tiled=True)
+    if by_permute:
+        got, x2, near = lax.optimization_barrier((got, x2, near))
+        x3 = cross(x2, 1)
     sums = call(
         functools.partial(owner_kernel, slots),
         shaped(dp_count, rank, wide),
@@ -292,15 +366,21 @@
         at = at.reshape(1)
         far_rows = down_part - near_rows
         z2, z3 = call(
-            far_kernel,
+            functools.partial(far_kernel, near_rows),
             (shaped(BLOCK, far_rows), shaped(BLOCK, far_rows)),
             (VMEM, VMEM),
             at,
-            value_weight,
-            *dys,
+            *in_hbm(value_weight, y2, near[1]),
             share,
             got,
             smem=1,
+            specs=[ANY] * 3 + [VMEM] * 2,
+            vmem=20,
+            scratch=[
+                pltpu.VMEM((far_rows, value_weight.shape[1]), bf16),
+                pltpu.VMEM((2 * BLOCK, value_weight.shape[1]), bf16),
+                pltpu.SemaphoreType.DMA((3,)),
+            ],
         )
         z2, z3 = cross(z2, 2), cross(z3, 3)
         grad_input = call(
@@ -308,15 +388,21 @@
             shaped(tok_rows, width),
             pl.BlockSpec(memory_space=pl.ANY),
             at,
-            dy_t,
+            side,
             back,
             factors,
-            value_weight,
-            *near,
-            smem=1,
+            *in_hbm(value_cotangent, y2, near[1], x2, x3, value_weight, near[0]),
+            smem=2,
+            specs=[VMEM] * 2 + [ANY] * 7,
+            vmem=24,
             scratch=[
-                pltpu.VMEM((fsdp_count, tok_rows, down_part), bf16),
-                pltpu.SemaphoreType.DMA((fsdp_count,)),
+                pltpu.VMEM(value_cotangent.shape, bf16),
+                pltpu.VMEM((4, side_rows, value_weight.shape[1]), bf16),
+                pltpu.VMEM(value_weight.shape, bf16),
+                pltpu.VMEM(value_weight.shape, bf16),
+                pltpu.VMEM((6, tok_rows, down_part), bf16),
+                pltpu.SemaphoreType.DMA((7,)),
+                pltpu.SemaphoreType.DMA((6,)),
             ],
         )
         grad_input = call(

time: 83.8 us -> 71.6 us (0.85)
  the two profiles are of different devices: /device:TPU:1 before, /device:TPU:0 now
where the time goes in v4:
time: 71.6 us; the launch traced here: 71.2 us
  Pallas kernels  18.8 us (26%)
  starting transfers between devices  17.2 us (24%)
  blocking collectives  17 us (24%)
  waiting for transfers between devices  14.8 us (21%)
  local copies, waits for them, and re-layouts  2.61 us (4%)
  between operations  0.79 us (1%)
    pallas_call x9, Pallas kernels, call(): pl.pallas_call(kernel, out_shape=out_shape, in_specs=[SMEM] * smem + (spe...  18.8 us
    ppermute x7, waiting for transfers between devices, cross(): lax.ppermute(array, axis, [(i, i ^ bit) for i in range(lax.axis_size(axis...  14.8 us
    all_to_all x1, blocking collectives, per_device(): lax.all_to_all(share, 'fsdp', split_axis=0, concat_axis=0, tiled=True)  8.55 us
    all_to_all x1, blocking collectives, per_device(): got = lax.all_to_all(grads, 'fsdp', split_axis=0, concat_axis=0, tiled=True)  8.42 us
    all_to_all x1, starting transfers between devices, per_device(): owned = lax.all_to_all(send, 'dp', split_axis=0, concat_axis=0, tiled=True)  6.83 us
    ppermute x7, starting transfers between devices, cross(): lax.ppermute(array, axis, [(i, i ^ bit) for i in range(lax.axis_size(axis...  5.82 us
    all_to_all x1, starting transfers between devices, per_device(): lax.all_to_all(sums, 'dp', split_axis=0, concat_axis=0, tiled=True)  4.54 us
    unnamed x12, local copies, waits for them, and re-layouts  1.59 us
  transfers between devices with their start and end apart: 9, of which 2 were waited for; matrix products, arithmetic and copies ran while one was open for 1% of the time, Pallas kernels for 19%

profile of v4, /device:TPU:0, one launch (start us, length us, event | category | flops | bytes accessed | tf_op | source)
XLA Modules:
  0.0 71.2 jit_solution(2943532607383186766)
XLA Ops:
  0.6 0.0 copy-start
  0.6 1.9 %shard_map.94 = (bf16[8,16,1920]{2,1,0:T(8,128)(2,1)}, s32[8]{0:T(128)S(1)}, s32[5]{0:T(128)S(1)}) custom-call(s32[1]{0:T(128)} %bitcast.me_ref, s32[32]{0:T(128)} %apb_ref.3, s32[40]{0:T(128)} %row_ref.3, bf16[5,16,1792]{2,1,0:T(8,128)(2,1)} %down_hbm.1, bf16[5,16,128]{2,1,0:T(8,128)(2,1)} %up_hbm.1), custom_call_target="tpu_custom_call" | custom-call | tf_op jit(solution)/shard_map/pallas_call | solution.py:244
  2.6 0.5 collective-permute-start.2
  3.1 6.8 %all-to-all-start = ((bf16[8,16,1920]{2,1,0:T(8,128)(2,1)}), bf16[8,16,1920]{2,1,0:T(8,128)(2,1)S(1)}, u32[]{:S(2)}, u32[]{:S(2)}) async-start(bf16[8,16,1920]{2,1,0:T(8,128)(2,1)} %get-tuple-element.27), calls=%async_computation | async-start | bytes 983040 | tf_op jit(solution)/shard_map/all_to_all | solution.py:309
  9.9 1.0 %constant_dynamic-slice_fusion = bf16[384,512]{1,0:T(8,128)(2,1)S(1)} fusion(bf16[1792,512]{1,0:T(8,128)(2,1)} %w0_hbm, s32[]{:T(128)S(6)} %select_n.3), kind=kLoop, calls=%fused_computation.1 | loop fusion | bytes 786436 | tf_op jit(solution)/shard_map/dynamic_slice | solution.py:312
  11.0 0.0 copy-done
  11.0 0.0 copy-start.1
  11.0 0.0 copy-start.2
  11.0 1.6 %collective-permute-start = (bf16[512,512]{1,0:T(8,128)(2,1)S(1)}, bf16[512,512]{1,0:T(8,128)(2,1)S(1)}, u32[]{:S(2)}, u32[]{:S(2)}) collective-permute-start(bf16[512,512]{1,0:T(8,128)(2,1)S(1)} %pad_maximum_fusion), channel_id=1, source_target_pairs={{0,2},{1,3},{2,0},{3,1},{4,6},{5,7},{6,4},{7,5},{8,10},{9,11},{10,... | collective-permute-start | bytes 1572872 | tf_op jit(solution)/shard_map/ppermute | solution.py:284
  12.6 1.5 %shard_map.95.x_ref = bf16[128,7168]{1,0:T(8,128)(2,1)S(1)} custom-call(bf16[128,7168]{1,0:T(8,128)(2,1)} %from_ref), custom_call_target="tpu_custom_call" | custom-call | tf_op jit(solution)/shard_map/pallas_call | solution.py:244
  14.1 11.0 %collective-permute-done.y2_hbm = bf16[512,512]{1,0:T(8,128)(2,1)S(1)} collective-permute-done((bf16[512,512]{1,0:T(8,128)(2,1)S(1)}, bf16[512,512]{1,0:T(8,128)(2,1)S(1)}, u32[]{:S(2)}, u32[]{:S(2)}) %collective-permute-start) | collective-permute-done | bytes 524320 | tf_op jit(solution)/shard_map/ppermute | solution.py:284
  25.1 0.0 copy-start.3
  25.1 0.0 all-to-all-done.got_ref
  25.1 0.0 copy-done.1
  25.2 0.0 copy-done.2
  25.2 0.6 shard_map.96.share_ref
  25.7 1.8 %collective-permute-start.1 = (bf16[512,512]{1,0:T(8,128)(2,1)S(1)}, bf16[512,512]{1,0:T(8,128)(2,1)}, u32[]{:S(2)}, u32[]{:S(2)}) collective-permute-start(bf16[512,512]{1,0:T(8,128)(2,1)S(1)} %collective-permute-done.y2_hbm), channel_id=1, source_target_pairs={{0,4},{4,0},{8,12},{12,8},{16,20},{20,16},{24,28},{28,24},{1,5},{5... | collective-permute-start | bytes 1572872 | tf_op jit(solution)/shard_map/ppermute | solution.py:284
  27.6 0.0 collective-permute-start.3
  27.6 8.6 %all_to_all.20.fac_ref = bf16[4,16,1920]{2,1,0:T(8,128)(2,1)S(1)} all-to-all(bf16[4,16,1920]{2,1,0:T(8,128)(2,1)S(1)} %shard_map.96.share_ref), channel_id=1, replica_groups=mesh['dp'=8,'fsdp'=4] {'fsdp'}, dimensions={0} | all-to-all | bytes 491520 | tf_op jit(solution)/shard_map/all_to_all | solution.py:338
  36.1 1.3 %shard_map.97 = (bf16[4,16,2048]{2,1,0:T(8,128)(2,1)S(1)}, bf16[128,16]{1,0:T(8,128)(2,1)S(1)}) custom-call(bf16[128,7168]{1,0:T(8,128)(2,1)S(1)} %shard_map.95.x_ref, bf16[128,512]{1,0:T(8,128)(2,1)S(1)} %copy-done, bf16[4,16,1920]{2,1,0:T(8,128)(2,1)S(1)} %all_to_all.20.fac_ref), custom_call_target="tpu_custom_call" | custom-call | tf_op jit(solution)/shard_map/pallas_call | solution.py:244
  37.4 8.4 %all_to_all.21.got_ref = bf16[4,16,2048]{2,1,0:T(8,128)(2,1)S(1)} all-to-all(bf16[4,16,2048]{2,1,0:T(8,128)(2,1)S(1)} %get-tuple-element.34), channel_id=1, replica_groups=mesh['dp'=8,'fsdp'=4] {'fsdp'}, dimensions={0} | all-to-all | bytes 524288 | tf_op jit(solution)/shard_map/all_to_all | solution.py:351
  45.9 0.0 copy-done.3
  45.9 0.0 collective-permute-done.1.x2_hbm
  45.9 0.0 collective-permute-done.3.y3_hbm
  45.9 0.0 copy-start.4
  45.9 0.8 %copy-done.4 = bf16[512,512]{1,0:T(8,128)(2,1)} copy-done((bf16[512,512]{1,0:T(8,128)(2,1)}, bf16[512,512]{1,0:T(8,128)(2,1)S(1)}, u32[]{:S(2)}) %copy-start.4) | copy-done | bytes 524312
  46.7 0.0 collective-permute-done.2.w1_hbm
  46.7 1.5 %shard_map.98 = bf16[8,16,1920]{2,1,0:T(8,128)(2,1)} custom-call(s32[1]{0:T(128)} %bitcast.me_ref, s32[32]{0:T(128)S(1)} %copy-done.1, s32[40]{0:T(128)S(1)} %copy-done.2, bf16[4,16,2048]{2,1,0:T(8,128)(2,1)S(1)} %all_to_all.21.got_ref), custom_call_target="tpu_custom_call" | custom-call | tf_op jit(solution)/shard_map/pallas_call | solution.py:244
  48.1 4.5 %all-to-all-start.3 = ((bf16[8,16,1920]{2,1,0:T(8,128)(2,1)}), bf16[8,16,1920]{2,1,0:T(8,128)(2,1)S(1)}, u32[]{:S(2)}, u32[]{:S(2)}) async-start(bf16[8,16,1920]{2,1,0:T(8,128)(2,1)} %shard_map.98), calls=%async_computation.3 | async-start | bytes 983040 | tf_op jit(solution)/shard_map/all_to_all | solution.py:364
  52.7 0.0 collective-permute-start.6
  52.7 2.1 %shard_map.99 = (bf16[128,1024]{1,0:T(8,128)(2,1)S(1)}, bf16[128,1024]{1,0:T(8,128)(2,1)S(1)}) custom-call(s32[1]{0:T(128)} %bitcast.2.at_ref, bf16[1792,512]{1,0:T(8,128)(2,1)} %w0_hbm, bf16[512,512]{1,0:T(8,128)(2,1)} %copy-done.3, bf16[512,512]{1,0:T(8,128)(2,1)} %copy-done.4, bf16[4,16,1920]{2,1,0:T(8,128)(2,1)S(1)} %shard_map.96.share_ref, ...), custom_call_target="tpu_custom_call" | custom-call | tf_op jit(solution)/shard_map/pallas_call | solution.py:244
  54.8 0.4 collective-permute-start.4
  55.2 1.5 %collective-permute-start.5 = (bf16[128,1024]{1,0:T(8,128)(2,1)S(1)}, bf16[128,1024]{1,0:T(8,128)(2,1)S(1)}, u32[]{:S(2)}, u32[]{:S(2)}) collective-permute-start(bf16[128,1024]{1,0:T(8,128)(2,1)S(1)} %get-tuple-element.39), channel_id=1, source_target_pairs={{0,3},{1,2},{2,1},{3,0},{4,7},{5,6},{6,5},{7,4},{8,11},{9,10},{10,... | collective-permute-start | bytes 786440 | tf_op jit(solution)/shard_map/ppermute | solution.py:284
  56.7 0.0 collective-permute-done.6.x3_hbm
  56.7 0.0 copy-start.5
  56.7 0.8 %copy-done.5 = bf16[512,512]{1,0:T(8,128)(2,1)} copy-done((bf16[512,512]{1,0:T(8,128)(2,1)}, bf16[512,512]{1,0:T(8,128)(2,1)S(1)}, u32[]{:S(2)}) %copy-start.5) | copy-done | bytes 524312
  57.5 7.5 %shard_map.100.in_ref = bf16[128,7168]{1,0:T(8,128)(2,1)} custom-call(s32[1]{0:T(128)} %bitcast.2.at_ref, s32[1]{0:T(128)S(6)} %and.5.side_ref, bf16[128,16]{1,0:T(8,128)(2,1)S(1)} %get-tuple-element.40.back_ref, bf16[4,16,1920]{2,1,0:T(8,128)(2,1)S(1)} %all_to_all.20.fac_ref, bf16[128,512]{1,0:T(8,128)(2,1)} %dy_hbm.1, bf16[512,512]{1,0:T(8,128)(2,1)} %copy-done.3, ...), custom_call_target="tpu_custom_call" | custom-call | tf_op jit(solution)/shard_map/pallas_call | solution.py:244
  65.0 0.0 collective-permute-done.4.z2_ref
  65.0 3.8 %collective-permute-done.5.z3_ref = bf16[128,1024]{1,0:T(8,128)(2,1)S(1)} collective-permute-done((bf16[128,1024]{1,0:T(8,128)(2,1)S(1)}, bf16[128,1024]{1,0:T(8,128)(2,1)S(1)}, u32[]{:S(2)}, u32[]{:S(2)}) %collective-permute-start.5) | collective-permute-done | bytes 262176 | tf_op jit(solution)/shard_map/ppermute | solution.py:284
  68.8 0.8 %shard_map.101 = bf16[128,7168]{1,0:T(8,128)(2,1)} custom-call(s32[1]{0:T(128)} %bitcast.2.at_ref, bf16[128,1024]{1,0:T(8,128)(2,1)S(1)} %collective-permute-done.4.z2_ref, bf16[128,1024]{1,0:T(8,128)(2,1)S(1)} %collective-permute-done.5.z3_ref, bf16[128,7168]{1,0:T(8,128)(2,1)} %shard_map.100.in_ref), custom_call_target="tpu_custom_call", output_to_operand_aliasing={{}: (3, {})} | custom-call | tf_op jit(solution)/shard_map/pallas_call | solution.py:244
  69.6 0.0 all-to-all-done.3.got_ref
  69.6 1.6 %shard_map.102 = (f32[5,16,1792]{2,1,0:T(8,128)}, f32[5,16,128]{2,1,0:T(8,128)}) custom-call(s32[8]{0:T(128)S(1)} %get-tuple-element.44.want_ref, s32[5]{0:T(128)S(1)} %get-tuple-element.45.count_ref, bf16[8,16,1920]{2,1,0:T(8,128)(2,1)S(1)} %all-to-all-done.3.got_ref), custom_call_target="tpu_custom_call" | custom-call | tf_op jit(solution)/shard_map/pallas_call | solution.py:244
  (1 shorter events, 0.0 us)
Async XLA Ops:
  0.6 10.3 %copy-start = (bf16[128,512]{1,0:T(8,128)(2,1)S(1)}, bf16[128,512]{1,0:T(8,128)(2,1)}, u32[]{:S(2)}) copy-start(bf16[128,512]{1,0:T(8,128)(2,1)} %dy_hbm.1) | copy-start | bytes 393220
  2.6 44.1 %collective-permute-start.2 = (bf16[1792,512]{1,0:T(8,128)(2,1)}, bf16[1792,512]{1,0:T(8,128)(2,1)}, u32[]{:S(2)}, u32[]{:S(2)}) collective-permute-start(bf16[1792,512]{1,0:T(8,128)(2,1)} %w0_hbm), channel_id=1, source_target_pairs={{0,1},{1,0},{2,3},{3,2},{4,5},{5,4},{6,7},{7,6},{8,9},{9,8},{10,11... | collective-permute-start | bytes 5505032 | tf_op jit(solution)/shard_map/ppermute | solution.py:284
  3.1 22.0 %all-to-all-start = ((bf16[8,16,1920]{2,1,0:T(8,128)(2,1)}), bf16[8,16,1920]{2,1,0:T(8,128)(2,1)S(1)}, u32[]{:S(2)}, u32[]{:S(2)}) async-start(bf16[8,16,1920]{2,1,0:T(8,128)(2,1)} %get-tuple-element.27), calls=%async_computation | async-start | bytes 983040 | tf_op jit(solution)/shard_map/all_to_all | solution.py:309
  11.0 14.1 %copy-start.1 = (s32[32]{0:T(128)S(1)}, s32[32]{0:T(128)}, u32[]{:S(2)}) copy-start(s32[32]{0:T(128)} %apb_ref.3) | copy-start | bytes 388
  11.0 14.1 %copy-start.2 = (s32[40]{0:T(128)S(1)}, s32[40]{0:T(128)}, u32[]{:S(2)}) copy-start(s32[40]{0:T(128)} %row_ref.3) | copy-start | bytes 484
  11.0 14.1 %collective-permute-start = (bf16[512,512]{1,0:T(8,128)(2,1)S(1)}, bf16[512,512]{1,0:T(8,128)(2,1)S(1)}, u32[]{:S(2)}, u32[]{:S(2)}) collective-permute-start(bf16[512,512]{1,0:T(8,128)(2,1)S(1)} %pad_maximum_fusion), channel_id=1, source_target_pairs={{0,2},{1,3},{2,0},{3,1},{4,6},{5,7},{6,4},{7,5},{8,10},{9,11},{10,... | collective-permute-start | bytes 1572872 | tf_op jit(solution)/shard_map/ppermute | solution.py:284
  25.1 20.7 %copy-start.3 = (bf16[512,512]{1,0:T(8,128)(2,1)}, bf16[512,512]{1,0:T(8,128)(2,1)S(1)}, u32[]{:S(2)}) copy-start(bf16[512,512]{1,0:T(8,128)(2,1)S(1)} %collective-permute-done.y2_hbm) | copy-start | bytes 1572868
  25.7 20.1 %collective-permute-start.1 = (bf16[512,512]{1,0:T(8,128)(2,1)S(1)}, bf16[512,512]{1,0:T(8,128)(2,1)}, u32[]{:S(2)}, u32[]{:S(2)}) collective-permute-start(bf16[512,512]{1,0:T(8,128)(2,1)S(1)} %collective-permute-done.y2_hbm), channel_id=1, source_target_pairs={{0,4},{4,0},{8,12},{12,8},{16,20},{20,16},{24,28},{28,24},{1,5},{5... | collective-permute-start | bytes 1572872 | tf_op jit(solution)/shard_map/ppermute | solution.py:284
  27.6 18.3 %collective-permute-start.3 = (bf16[512,512]{1,0:T(8,128)(2,1)S(1)}, bf16[512,512]{1,0:T(8,128)(2,1)S(1)}, u32[]{:S(2)}, u32[]{:S(2)}) collective-permute-start(bf16[512,512]{1,0:T(8,128)(2,1)S(1)} %collective-permute-done.y2_hbm), channel_id=1, source_target_pairs={{0,1},{1,0},{2,3},{3,2},{4,5},{5,4},{6,7},{7,6},{8,9},{9,8},{10,11... | collective-permute-start | bytes 1572872 | tf_op jit(solution)/shard_map/ppermute | solution.py:284
  45.9 0.8 %copy-start.4 = (bf16[512,512]{1,0:T(8,128)(2,1)}, bf16[512,512]{1,0:T(8,128)(2,1)S(1)}, u32[]{:S(2)}) copy-start(bf16[512,512]{1,0:T(8,128)(2,1)S(1)} %collective-permute-done.3.y3_hbm) | copy-start | bytes 1572868
  48.1 21.4 %all-to-all-start.3 = ((bf16[8,16,1920]{2,1,0:T(8,128)(2,1)}), bf16[8,16,1920]{2,1,0:T(8,128)(2,1)S(1)}, u32[]{:S(2)}, u32[]{:S(2)}) async-start(bf16[8,16,1920]{2,1,0:T(8,128)(2,1)} %shard_map.98), calls=%async_computation.3 | async-start | bytes 983040 | tf_op jit(solution)/shard_map/all_to_all | solution.py:364
  52.7 4.0 %collective-permute-start.6 = (bf16[512,512]{1,0:T(8,128)(2,1)}, bf16[512,512]{1,0:T(8,128)(2,1)S(1)}, u32[]{:S(2)}, u32[]{:S(2)}) collective-permute-start(bf16[512,512]{1,0:T(8,128)(2,1)} %collective-permute-done.1.x2_hbm), channel_id=1, source_target_pairs={{0,1},{1,0},{2,3},{3,2},{4,5},{5,4},{6,7},{7,6},{8,9},{9,8},{10,11... | collective-permute-start | bytes 1572872 | tf_op jit(solution)/shard_map/ppermute | solution.py:284
  54.8 10.2 %collective-permute-start.4 = (bf16[128,1024]{1,0:T(8,128)(2,1)S(1)}, bf16[128,1024]{1,0:T(8,128)(2,1)S(1)}, u32[]{:S(2)}, u32[]{:S(2)}) collective-permute-start(bf16[128,1024]{1,0:T(8,128)(2,1)S(1)} %get-tuple-element.38), channel_id=1, source_target_pairs={{0,2},{1,3},{2,0},{3,1},{4,6},{5,7},{6,4},{7,5},{8,10},{9,11},{10,... | collective-permute-start | bytes 786440 | tf_op jit(solution)/shard_map/ppermute | solution.py:284
  55.2 13.6 %collective-permute-start.5 = (bf16[128,1024]{1,0:T(8,128)(2,1)S(1)}, bf16[128,1024]{1,0:T(8,128)(2,1)S(1)}, u32[]{:S(2)}, u32[]{:S(2)}) collective-permute-start(bf16[128,1024]{1,0:T(8,128)(2,1)S(1)} %get-tuple-element.39), channel_id=1, source_target_pairs={{0,3},{1,2},{2,1},{3,0},{4,7},{5,6},{6,5},{7,4},{8,11},{9,10},{10,... | collective-permute-start | bytes 786440 | tf_op jit(solution)/shard_map/ppermute | solution.py:284
  56.7 0.8 %copy-start.5 = (bf16[512,512]{1,0:T(8,128)(2,1)}, bf16[512,512]{1,0:T(8,128)(2,1)S(1)}, u32[]{:S(2)}) copy-start(bf16[512,512]{1,0:T(8,128)(2,1)S(1)} %collective-permute-done.6.x3_hbm) | copy-start | bytes 1572868

commit v5 on v4

--- a/solution.py
+++ b/solution.py
@@ -46,11 +46,21 @@
 
 
 def pick_kernel(
-    group_blocks, me_ref, apb_hbm, row_hbm, down_hbm, up_hbm, send_ref, want_ref, count_ref,
-    apb_ref, row_ref, down_ref, up_ref, sems,
+    group_blocks, me_ref, apb_hbm, row_hbm, down_hbm, up_hbm, w_hbm, send_ref, want_ref,
+    count_ref, some_ref, apb_ref, row_ref, down_ref, up_ref, sems,
 ):
+    rows = some_ref.shape[0]
+    start = pl.multiple_of(lax.rem(me_ref[0], 2) * rows, 16)
     copies = fetch(
-        (apb_hbm, row_hbm, down_hbm, up_hbm), (apb_ref, row_ref, down_ref, up_ref), sems
+        (apb_hbm, row_hbm, down_hbm, up_hbm, w_hbm.at[pl.ds(start, rows)]),
+        (
+            apb_ref,
+            row_ref,
+            down_ref,
+            up_ref,
+            some_ref,
+        ),
+        sems,
     )
     slots, _, down_part = down_ref.shape
     up_part = up_ref.shape[2]
@@ -85,6 +95,7 @@
         return carry
 
     lax.fori_loop(0, groups, put, 0)
+    copies[4].wait()
 
 
 def share_kernel(slots, me_ref, apb_ref, row_ref, got_ref, out_ref):
@@ -123,13 +134,23 @@
         ).astype(jnp.bfloat16)
 
 
-def owner_kernel(slots, me_ref, apb_ref, row_ref, got_ref, out_ref, acc_ref):
+def owner_kernel(slots, me_ref, apb_ref, row_ref, got_ref, out_ref, total_ref):
     blocks = got_ref.shape[0]
-    acc_ref[...] = jnp.zeros_like(acc_ref)
+    wide = out_ref.shape[2]
+    owners = [
+        lax.div(row_ref[apb_ref[me_ref[0] * blocks + j]], slots) for j in range(blocks)
+    ]
+    out_ref[...] = jnp.zeros_like(out_ref)
     for j in range(blocks):
-        owner = lax.div(row_ref[apb_ref[me_ref[0] * blocks + j]], slots)
-        acc_ref[owner] += got_ref[j, :, : acc_ref.shape[2]].astype(jnp.float32)
-    out_ref[...] = acc_ref[...].astype(jnp.bfloat16)
+        total_ref[...] = got_ref[j, :, :wide].astype(jnp.float32)
+        for i in range(blocks):
+            if i != j:
+
+                @pl.when(owners[i] == owners[j])
+                def _():
+                    total_ref[...] += got_ref[i, :, :wide].astype(jnp.float32)
+
+        out_ref[owners[j]] = total_ref[...].astype(jnp.bfloat16)
 
 
 def total_kernel(want_ref, count_ref, got_ref, down_ref, up_ref):
@@ -152,29 +173,15 @@
         up_ref[s] = up_ref[s] / divisor
 
 
-def far_kernel(
-    near, at_ref, w_hbm, y2_hbm, y3_hbm, share_ref, got_ref, z2_ref, z3_ref, w_ref, dy_ref, sems
-):
-    rows = z2_ref.shape[1]
-    tokens = z2_ref.shape[0]
-    taken = pl.ds(y2_hbm.shape[0] - tokens, tokens)
-    copies = fetch(
-        [y2_hbm.at[taken], y3_hbm.at[taken], w_hbm.at[pl.ds(near, rows)]],
-        [dy_ref.at[pl.ds(0, tokens)], dy_ref.at[pl.ds(tokens, tokens)], w_ref],
-        sems,
-    )
+def far_kernel(near, bits, at_ref, w_hbm, dy_ref, share_ref, got_ref, z_ref, w_ref, sems):
+    tokens, rows = z_ref.shape
+    copies = fetch([w_hbm.at[pl.ds(near, rows)]], [w_ref], sems)
+    peer = lax.bitwise_xor(at_ref[0], bits)
+    dy_t = turned(dy_ref[...])
+    back = turned(got_ref[peer, :, got_ref.shape[2] - tokens :])
+    adapted = dot(back, share_ref[peer, :, near : near + rows])
     copies[0].wait()
-    copies[1].wait()
-    dy_t = turned(dy_ref[...])
-    copies[2].wait()
-    frozen_t = dot(w_ref[...], dy_t)
-    for i, z_ref in enumerate((z2_ref, z3_ref)):
-        peer = lax.bitwise_xor(at_ref[0], 2 + i)
-        back = turned(got_ref[peer, :, got_ref.shape[2] - tokens :])
-        z_ref[...] = (
-            frozen_t[:, i * tokens : (i + 1) * tokens].T
-            + dot(back, share_ref[peer, :, near : near + rows])
-        ).astype(jnp.bfloat16)
+    z_ref[...] = (dot(w_ref[...], dy_t).T + adapted).astype(jnp.bfloat16)
 
 
 def input_kernel(
@@ -277,51 +284,49 @@
 
     by_permute = fsdp_count == 4 and down_part % 256 == 0
     by_permute = by_permute and dp_count % 2 == 0
-    side_rows = down_part // 4 // LANES * LANES
+    side_rows = round_up(down_part // 4) if by_permute else 16
     near_rows = 2 * side_rows
 
     def cross(array, bit, axis="fsdp"):
         return lax.ppermute(array, axis, [(i, i ^ bit) for i in range(lax.axis_size(axis))])
 
     index = (me, adapter_per_block, adapter_table_row)
-    send, want, count = call(
+    send, want, count, some = call(
         functools.partial(pick_kernel, fsdp_count),
         (
             shaped(dp_count, rank, wide),
             shaped(dp_count, dtype=jnp.int32),
             shaped(slots, dtype=jnp.int32),
+            shaped(side_rows, value_weight.shape[1]),
         ),
-        (VMEM, SMEM, SMEM),
+        (VMEM, SMEM, SMEM, VMEM),
         me,
-        *in_hbm(*index[1:], adapter_down_table, adapter_up_table),
+        *in_hbm(*index[1:], adapter_down_table, adapter_up_table, value_weight),
         smem=1,
-        specs=[ANY] * 4,
+        specs=[ANY] * 5,
         scratch=[
             pltpu.SMEM(adapter_per_block.shape, jnp.int32),
             pltpu.SMEM(adapter_table_row.shape, jnp.int32),
             pltpu.VMEM(adapter_down_table.shape, bf16),
             pltpu.VMEM(adapter_up_table.shape, bf16),
-            pltpu.SemaphoreType.DMA((4,)),
+            pltpu.SemaphoreType.DMA((5,)),
         ],
     )
-    if by_permute:
-        value_weight, send = lax.optimization_barrier((value_weight, send))
     owned = lax.all_to_all(send, "dp", split_axis=0, concat_axis=0, tiled=True)
     if by_permute:
         side = me & 1
-        some = lax.dynamic_slice_in_dim(value_weight, side[0] * side_rows, side_rows, 0)
-        y2 = cross(jnp.concatenate([some, value_cotangent], axis=0), 2)
+        y2 = cross(some, 2)
+        dy2 = cross(value_cotangent, 2)
         at_hand, _ = lax.optimization_barrier((projection_input, send))
         at_hand = call(
             copy_kernel,
             shaped(tok_rows, width),
-            ANY,
+            VMEM,
             *in_hbm(at_hand),
             specs=[ANY],
             scratch=[pltpu.SemaphoreType.DMA],
         )
         owned, y2, at_hand = lax.optimization_barrier((owned, y2, at_hand))
-        near = cross(value_weight, 1), cross(y2, 1)
     else:
         at_hand = projection_input
     share = call(
@@ -333,7 +338,8 @@
         smem=3,
     )
     if by_permute:
-        x2, share = lax.optimization_barrier((y2, share))
+        x2, share, dy2, beside = lax.optimization_barrier((y2, share, dy2, value_weight))
+        near = cross(beside, 1), cross(x2, 1)
         x2 = cross(x2, 1, "dp")
     factors = lax.all_to_all(share, "fsdp", split_axis=0, concat_axis=0, tiled=True)
     grads, back = call(
@@ -351,7 +357,8 @@
     got = lax.all_to_all(grads, "fsdp", split_axis=0, concat_axis=0, tiled=True)
     if by_permute:
         got, x2, near = lax.optimization_barrier((got, x2, near))
-        x3 = cross(x2, 1)
+        got, dy2 = lax.optimization_barrier((got, dy2))
+        x3, dy3 = cross(x2, 1), cross(dy2, 1)
     sums = call(
         functools.partial(owner_kernel, slots),
         shaped(dp_count, rank, wide),
@@ -359,30 +366,35 @@
         *index,
         got,
         smem=3,
-        scratch=[pltpu.VMEM((dp_count, rank, wide), jnp.float32)],
+        scratch=[pltpu.VMEM((rank, wide), jnp.float32)],
     )
     arrived = lax.all_to_all(sums, "dp", split_axis=0, concat_axis=0, tiled=True)
     if by_permute:
         at = at.reshape(1)
         far_rows = down_part - near_rows
-        z2, z3 = call(
-            functools.partial(far_kernel, near_rows),
-            (shaped(BLOCK, far_rows), shaped(BLOCK, far_rows)),
-            (VMEM, VMEM),
-            at,
-            *in_hbm(value_weight, y2, near[1]),
-            share,
-            got,
-            smem=1,
-            specs=[ANY] * 3 + [VMEM] * 2,
-            vmem=20,
-            scratch=[
-                pltpu.VMEM((far_rows, value_weight.shape[1]), bf16),
-                pltpu.VMEM((2 * BLOCK, value_weight.shape[1]), bf16),
-                pltpu.SemaphoreType.DMA((3,)),
-            ],
-        )
-        z2, z3 = cross(z2, 2), cross(z3, 3)
+        z2, z3 = (
+            cross(
+                call(
+                    functools.partial(far_kernel, near_rows, bits),
+                    shaped(BLOCK, far_rows),
+                    VMEM,
+                    at,
+                    *in_hbm(value_weight),
+                    dy,
+                    share,
+                    got,
+                    smem=1,
+                    specs=[ANY] + [VMEM] * 3,
+                    vmem=12,
+                    scratch=[
+                        pltpu.VMEM((far_rows, value_weight.shape[1]), bf16),
+                        pltpu.SemaphoreType.DMA((1,)),
+                    ],
+                ),
+                bits,
+            )
+            for bits, dy in ((2, dy2), (3, dy3))
+        )
         grad_input = call(
             input_kernel,
             shaped(tok_rows, width),
@@ -391,7 +403,11 @@
             side,
             back,
             factors,
-            *in_hbm(value_cotangent, y2, near[1], x2, x3, value_weight, near[0]),
+            *in_hbm(value_cotangent, y2),
+            near[1],
+            *in_hbm(x2),
+            x3,
+            *in_hbm(value_weight, near[0]),
             smem=2,
             specs=[VMEM] * 2 + [ANY] * 7,
             vmem=24,

time: 71.6 us -> 68.5 us (0.957)
  waiting for transfers between devices: 14.8 us -> 12.1 us
  local copies, waits for them, and re-layouts: 2.61 us -> 0.02 us
  Pallas kernels: 18.8 us -> 20.2 us
    ppermute x7 -> x9, waiting for transfers between devices: 14.8 us -> 12.1 us  [cross(): lax.ppermute(array, axis, [(i, i ^ bit) for i in range(lax.axis_size(axis...]
    unnamed x12 -> x6, local copies, waits for them, and re-layouts: 1.59 us -> 0.02 us
    pallas_call x9 -> x10, Pallas kernels: 18.8 us -> 20.2 us  [call(): pl.pallas_call(kernel, out_shape=out_shape, in_specs=[SMEM] * smem + (spe...]
    dynamic_slice x1 -> x0, local copies, waits for them, and re-layouts: 1.02 us -> none  [per_device(): lax.dynamic_slice_in_dim(value_weight, side[0] * side_rows, side_rows, 0)]
    ppermute x7 -> x9, starting transfers between devices: 5.82 us -> 6.04 us  [cross(): lax.ppermute(array, axis, [(i, i ^ bit) for i in range(lax.axis_size(axis...]
  transfers between devices with their start and end apart: 9 -> 11, of which waited for: 2 -> 2; matrix products, arithmetic and copies ran while one was open for 1% -> 0% of each run, Pallas kernels for 19% -> 22%
where the time goes in v5:
time: 68.5 us; the launch traced here: 67.8 us
  Pallas kernels  20.2 us (29%)
  starting transfers between devices  17.9 us (26%)
  blocking collectives  16.9 us (25%)
  waiting for transfers between devices  12.1 us (18%)
  between operations  0.76 us (1%)
    pallas_call x10, Pallas kernels, call(): pl.pallas_call(kernel, out_shape=out_shape, in_specs=[SMEM] * smem + (spe...  20.2 us
    ppermute x9, waiting for transfers between devices, cross(): lax.ppermute(array, axis, [(i, i ^ bit) for i in range(lax.axis_size(axis...  12.1 us
    all_to_all x1, blocking collectives, per_device(): lax.all_to_all(share, 'fsdp', split_axis=0, concat_axis=0, tiled=True)  8.44 us
    all_to_all x1, blocking collectives, per_device(): got = lax.all_to_all(grads, 'fsdp', split_axis=0, concat_axis=0, tiled=True)  8.42 us
    all_to_all x1, starting transfers between devices, per_device(): owned = lax.all_to_all(send, 'dp', split_axis=0, concat_axis=0, tiled=True)  7.26 us
    ppermute x9, starting transfers between devices, cross(): lax.ppermute(array, axis, [(i, i ^ bit) for i in range(lax.axis_size(axis...  6.04 us
    all_to_all x1, starting transfers between devices, per_device(): lax.all_to_all(sums, 'dp', split_axis=0, concat_axis=0, tiled=True)  4.56 us
  transfers between devices with their start and end apart: 11, of which 2 were waited for; matrix products, arithmetic and copies ran while one was open for 0% of the time, Pallas kernels for 22%

profile of v5, /device:TPU:0, one launch (start us, length us, event | category | flops | bytes accessed | tf_op | source)
XLA Modules:
  0.0 67.8 jit_solution(836176843931903133)
XLA Ops:
  0.6 0.0 copy-start
  0.6 2.0 %shard_map.94 = (bf16[8,16,1920]{2,1,0:T(8,128)(2,1)}, s32[8]{0:T(128)S(1)}, s32[5]{0:T(128)S(1)}, bf16[512,512]{1,0:T(8,128)(2,1)S(1)}) custom-call(s32[1]{0:T(128)} %bitcast.me_ref, s32[32]{0:T(128)} %apb_ref.3, s32[40]{0:T(128)} %row_ref.3, bf16[5,16,1792]{2,1,0:T(8,128)(2,1)} %down_hbm.1, bf16[5,16,128]{2,1,0:T(8,128)(2,1)} %up_hbm.1, ...), custom_call_target="tpu_custom_call" | custom-call | tf_op jit(solution)/shard_map/pallas_call | solution.py:251
  2.7 7.3 %all-to-all-start = ((bf16[8,16,1920]{2,1,0:T(8,128)(2,1)}), bf16[8,16,1920]{2,1,0:T(8,128)(2,1)S(1)}, u32[]{:S(2)}, u32[]{:S(2)}) async-start(bf16[8,16,1920]{2,1,0:T(8,128)(2,1)} %get-tuple-element.27), calls=%async_computation | async-start | bytes 983040 | tf_op jit(solution)/shard_map/all_to_all | solution.py:315
  9.9 0.0 copy-start.1
  9.9 0.0 copy-start.2
  10.0 1.6 %collective-permute-start = (bf16[512,512]{1,0:T(8,128)(2,1)S(1)}, bf16[512,512]{1,0:T(8,128)(2,1)}, u32[]{:S(2)}, u32[]{:S(2)}) collective-permute-start(bf16[512,512]{1,0:T(8,128)(2,1)S(1)} %get-tuple-element.28), channel_id=1, source_target_pairs={{0,2},{1,3},{2,0},{3,1},{4,6},{5,7},{6,4},{7,5},{8,10},{9,11},{10,... | collective-permute-start | bytes 1572872 | tf_op jit(solution)/shard_map/ppermute | solution.py:291
  11.5 0.0 copy-done
  11.5 0.5 collective-permute-start.1
  12.0 1.5 %shard_map.95.x_ref = bf16[128,7168]{1,0:T(8,128)(2,1)S(1)} custom-call(bf16[128,7168]{1,0:T(8,128)(2,1)} %from_ref), custom_call_target="tpu_custom_call" | custom-call | tf_op jit(solution)/shard_map/pallas_call | solution.py:251
  13.6 11.3 %collective-permute-done.y2_hbm = bf16[512,512]{1,0:T(8,128)(2,1)} collective-permute-done((bf16[512,512]{1,0:T(8,128)(2,1)S(1)}, bf16[512,512]{1,0:T(8,128)(2,1)}, u32[]{:S(2)}, u32[]{:S(2)}) %collective-permute-start) | collective-permute-done | bytes 524320 | tf_op jit(solution)/shard_map/ppermute | solution.py:291
  24.9 0.0 all-to-all-done.got_ref
  24.9 0.0 copy-done.1
  24.9 0.0 copy-done.2
  24.9 0.6 shard_map.96.share_ref
  25.5 0.7 %collective-permute-done.1.dy_ref = bf16[128,512]{1,0:T(8,128)(2,1)S(1)} collective-permute-done((bf16[128,512]{1,0:T(8,128)(2,1)S(1)}, bf16[128,512]{1,0:T(8,128)(2,1)S(1)}, u32[]{:S(2)}, u32[]{:S(2)}) %collective-permute-start.1) | collective-permute-done | bytes 131104 | tf_op jit(solution)/shard_map/ppermute | solution.py:291
  26.2 0.0 collective-permute-start.3
  26.2 1.7 %collective-permute-start.2 = (bf16[512,512]{1,0:T(8,128)(2,1)}, bf16[512,512]{1,0:T(8,128)(2,1)}, u32[]{:S(2)}, u32[]{:S(2)}) collective-permute-start(bf16[512,512]{1,0:T(8,128)(2,1)} %collective-permute-done.y2_hbm), channel_id=1, source_target_pairs={{0,4},{4,0},{8,12},{12,8},{16,20},{20,16},{24,28},{28,24},{1,5},{5... | collective-permute-start | bytes 1572872 | tf_op jit(solution)/shard_map/ppermute | solution.py:291
  27.9 0.2 collective-permute-start.4
  28.1 8.4 %all_to_all.20.fac_ref = bf16[4,16,1920]{2,1,0:T(8,128)(2,1)S(1)} all-to-all(bf16[4,16,1920]{2,1,0:T(8,128)(2,1)S(1)} %shard_map.96.share_ref), channel_id=1, replica_groups=mesh['dp'=8,'fsdp'=4] {'fsdp'}, dimensions={0} | all-to-all | bytes 491520 | tf_op jit(solution)/shard_map/all_to_all | solution.py:344
  36.5 1.3 %shard_map.97 = (bf16[4,16,2048]{2,1,0:T(8,128)(2,1)S(1)}, bf16[128,16]{1,0:T(8,128)(2,1)S(1)}) custom-call(bf16[128,7168]{1,0:T(8,128)(2,1)S(1)} %shard_map.95.x_ref, bf16[128,512]{1,0:T(8,128)(2,1)S(1)} %copy-done, bf16[4,16,1920]{2,1,0:T(8,128)(2,1)S(1)} %all_to_all.20.fac_ref), custom_call_target="tpu_custom_call" | custom-call | tf_op jit(solution)/shard_map/pallas_call | solution.py:251
  37.9 8.4 %all_to_all.21.got_ref = bf16[4,16,2048]{2,1,0:T(8,128)(2,1)S(1)} all-to-all(bf16[4,16,2048]{2,1,0:T(8,128)(2,1)S(1)} %get-tuple-element.34), channel_id=1, replica_groups=mesh['dp'=8,'fsdp'=4] {'fsdp'}, dimensions={0} | all-to-all | bytes 524288 | tf_op jit(solution)/shard_map/all_to_all | solution.py:357
  46.3 0.0 collective-permute-done.2.x2_hbm
  46.3 0.0 collective-permute-done.4.y3_hbm
  46.3 0.0 collective-permute-done.3.w1_hbm
  46.3 1.5 %shard_map.98 = bf16[8,16,1920]{2,1,0:T(8,128)(2,1)} custom-call(s32[1]{0:T(128)} %bitcast.me_ref, s32[32]{0:T(128)S(1)} %copy-done.1, s32[40]{0:T(128)S(1)} %copy-done.2, bf16[4,16,2048]{2,1,0:T(8,128)(2,1)S(1)} %all_to_all.21.got_ref), custom_call_target="tpu_custom_call" | custom-call | tf_op jit(solution)/shard_map/pallas_call | solution.py:251
  47.8 4.6 %all-to-all-start.3 = ((bf16[8,16,1920]{2,1,0:T(8,128)(2,1)}), bf16[8,16,1920]{2,1,0:T(8,128)(2,1)S(1)}, u32[]{:S(2)}, u32[]{:S(2)}) async-start(bf16[8,16,1920]{2,1,0:T(8,128)(2,1)} %shard_map.98), calls=%async_computation.3 | async-start | bytes 983040 | tf_op jit(solution)/shard_map/all_to_all | solution.py:371
  52.3 0.0 collective-permute-start.8
  52.4 0.5 collective-permute-start.6
  52.9 1.7 %shard_map.99 = bf16[128,768]{1,0:T(8,128)(2,1)S(1)} custom-call(s32[1]{0:T(128)} %bitcast.1.at_ref, bf16[1792,512]{1,0:T(8,128)(2,1)} %w0_hbm.1, bf16[128,512]{1,0:T(8,128)(2,1)S(1)} %collective-permute-done.1.dy_ref, bf16[4,16,1920]{2,1,0:T(8,128)(2,1)S(1)} %shard_map.96.share_ref, bf16[4,16,2048]{2,1,0:T(8,128)(2,1)S(1)} %all_to_all.21.got_ref), custom_call_target="tpu_custom_call" | custom-call | tf_op jit(solution)/shard_map/pallas_call | solution.py:251
  54.5 0.4 collective-permute-start.5
  55.0 0.0 collective-permute-done.6.dy_ref
  55.0 1.7 %shard_map.100 = bf16[128,768]{1,0:T(8,128)(2,1)S(1)} custom-call(s32[1]{0:T(128)} %bitcast.1.at_ref, bf16[1792,512]{1,0:T(8,128)(2,1)} %w0_hbm.1, bf16[128,512]{1,0:T(8,128)(2,1)S(1)} %collective-permute-done.6.dy_ref, bf16[4,16,1920]{2,1,0:T(8,128)(2,1)S(1)} %shard_map.96.share_ref, bf16[4,16,2048]{2,1,0:T(8,128)(2,1)S(1)} %all_to_all.21.got_ref), custom_call_target="tpu_custom_call" | custom-call | tf_op jit(solution)/shard_map/pallas_call | solution.py:251
  56.6 1.1 %collective-permute-start.7 = (bf16[128,768]{1,0:T(8,128)(2,1)S(1)}, bf16[128,768]{1,0:T(8,128)(2,1)S(1)}, u32[]{:S(2)}, u32[]{:S(2)}) collective-permute-start(bf16[128,768]{1,0:T(8,128)(2,1)S(1)} %shard_map.100), channel_id=1, source_target_pairs={{0,3},{1,2},{2,1},{3,0},{4,7},{5,6},{6,5},{7,4},{8,11},{9,10},{10,... | collective-permute-start | bytes 589832 | tf_op jit(solution)/shard_map/ppermute | solution.py:291
  57.8 0.0 collective-permute-done.8.x3_hbm
  57.8 7.6 %shard_map.101.in_ref = bf16[128,7168]{1,0:T(8,128)(2,1)} custom-call(s32[1]{0:T(128)} %bitcast.1.at_ref, s32[1]{0:T(128)S(6)} %and.5.side_ref, bf16[128,16]{1,0:T(8,128)(2,1)S(1)} %get-tuple-element.41.back_ref, bf16[4,16,1920]{2,1,0:T(8,128)(2,1)S(1)} %all_to_all.20.fac_ref, bf16[128,512]{1,0:T(8,128)(2,1)} %dy_hbm.1, ...), custom_call_target="tpu_custom_call" | custom-call | tf_op jit(solution)/shard_map/pallas_call | solution.py:251
  65.4 0.0 collective-permute-done.5.z2_ref
  65.4 0.0 collective-permute-done.7.z3_ref
  65.4 0.8 %shard_map.102 = bf16[128,7168]{1,0:T(8,128)(2,1)} custom-call(s32[1]{0:T(128)} %bitcast.1.at_ref, bf16[128,768]{1,0:T(8,128)(2,1)S(1)} %collective-permute-done.5.z2_ref, bf16[128,768]{1,0:T(8,128)(2,1)S(1)} %collective-permute-done.7.z3_ref, bf16[128,7168]{1,0:T(8,128)(2,1)} %shard_map.101.in_ref), custom_call_target="tpu_custom_call", output_to_operand_aliasing={{}: (3, {})} | custom-call | tf_op jit(solution)/shard_map/pallas_call | solution.py:251
  66.2 0.0 all-to-all-done.3.got_ref
  66.2 1.6 %shard_map.103 = (f32[5,16,1792]{2,1,0:T(8,128)}, f32[5,16,128]{2,1,0:T(8,128)}) custom-call(s32[8]{0:T(128)S(1)} %get-tuple-element.46.want_ref, s32[5]{0:T(128)S(1)} %get-tuple-element.47.count_ref, bf16[8,16,1920]{2,1,0:T(8,128)(2,1)S(1)} %all-to-all-done.3.got_ref), custom_call_target="tpu_custom_call" | custom-call | tf_op jit(solution)/shard_map/pallas_call | solution.py:251
Async XLA Ops:
  0.6 10.9 %copy-start = (bf16[128,512]{1,0:T(8,128)(2,1)S(1)}, bf16[128,512]{1,0:T(8,128)(2,1)}, u32[]{:S(2)}) copy-start(bf16[128,512]{1,0:T(8,128)(2,1)} %dy_hbm.1) | copy-start | bytes 393220
  2.7 22.2 %all-to-all-start = ((bf16[8,16,1920]{2,1,0:T(8,128)(2,1)}), bf16[8,16,1920]{2,1,0:T(8,128)(2,1)S(1)}, u32[]{:S(2)}, u32[]{:S(2)}) async-start(bf16[8,16,1920]{2,1,0:T(8,128)(2,1)} %get-tuple-element.27), calls=%async_computation | async-start | bytes 983040 | tf_op jit(solution)/shard_map/all_to_all | solution.py:315
  9.9 15.0 %copy-start.1 = (s32[32]{0:T(128)S(1)}, s32[32]{0:T(128)}, u32[]{:S(2)}) copy-start(s32[32]{0:T(128)} %apb_ref.3) | copy-start | bytes 388
  9.9 15.0 %copy-start.2 = (s32[40]{0:T(128)S(1)}, s32[40]{0:T(128)}, u32[]{:S(2)}) copy-start(s32[40]{0:T(128)} %row_ref.3) | copy-start | bytes 484
  10.0 15.0 %collective-permute-start = (bf16[512,512]{1,0:T(8,128)(2,1)S(1)}, bf16[512,512]{1,0:T(8,128)(2,1)}, u32[]{:S(2)}, u32[]{:S(2)}) collective-permute-start(bf16[512,512]{1,0:T(8,128)(2,1)S(1)} %get-tuple-element.28), channel_id=1, source_target_pairs={{0,2},{1,3},{2,0},{3,1},{4,6},{5,7},{6,4},{7,5},{8,10},{9,11},{10,... | collective-permute-start | bytes 1572872 | tf_op jit(solution)/shard_map/ppermute | solution.py:291
  11.5 14.7 %collective-permute-start.1 = (bf16[128,512]{1,0:T(8,128)(2,1)S(1)}, bf16[128,512]{1,0:T(8,128)(2,1)S(1)}, u32[]{:S(2)}, u32[]{:S(2)}) collective-permute-start(bf16[128,512]{1,0:T(8,128)(2,1)S(1)} %copy-done), channel_id=1, source_target_pairs={{0,2},{1,3},{2,0},{3,1},{4,6},{5,7},{6,4},{7,5},{8,10},{9,11},{10,... | collective-permute-start | bytes 393224 | tf_op jit(solution)/shard_map/ppermute | solution.py:291
  26.2 20.1 %collective-permute-start.3 = (bf16[1792,512]{1,0:T(8,128)(2,1)}, bf16[1792,512]{1,0:T(8,128)(2,1)}, u32[]{:S(2)}, u32[]{:S(2)}) collective-permute-start(bf16[1792,512]{1,0:T(8,128)(2,1)} %w0_hbm.1), channel_id=1, source_target_pairs={{0,1},{1,0},{2,3},{3,2},{4,5},{5,4},{6,7},{7,6},{8,9},{9,8},{10,11... | collective-permute-start | bytes 5505032 | tf_op jit(solution)/shard_map/ppermute | solution.py:291
  26.2 20.1 %collective-permute-start.2 = (bf16[512,512]{1,0:T(8,128)(2,1)}, bf16[512,512]{1,0:T(8,128)(2,1)}, u32[]{:S(2)}, u32[]{:S(2)}) collective-permute-start(bf16[512,512]{1,0:T(8,128)(2,1)} %collective-permute-done.y2_hbm), channel_id=1, source_target_pairs={{0,4},{4,0},{8,12},{12,8},{16,20},{20,16},{24,28},{28,24},{1,5},{5... | collective-permute-start | bytes 1572872 | tf_op jit(solution)/shard_map/ppermute | solution.py:291
  27.9 18.4 %collective-permute-start.4 = (bf16[512,512]{1,0:T(8,128)(2,1)}, bf16[512,512]{1,0:T(8,128)(2,1)S(1)}, u32[]{:S(2)}, u32[]{:S(2)}) collective-permute-start(bf16[512,512]{1,0:T(8,128)(2,1)} %collective-permute-done.y2_hbm), channel_id=1, source_target_pairs={{0,1},{1,0},{2,3},{3,2},{4,5},{5,4},{6,7},{7,6},{8,9},{9,8},{10,11... | collective-permute-start | bytes 1572872 | tf_op jit(solution)/shard_map/ppermute | solution.py:291
  47.8 18.4 %all-to-all-start.3 = ((bf16[8,16,1920]{2,1,0:T(8,128)(2,1)}), bf16[8,16,1920]{2,1,0:T(8,128)(2,1)S(1)}, u32[]{:S(2)}, u32[]{:S(2)}) async-start(bf16[8,16,1920]{2,1,0:T(8,128)(2,1)} %shard_map.98), calls=%async_computation.3 | async-start | bytes 983040 | tf_op jit(solution)/shard_map/all_to_all | solution.py:371
  52.3 5.4 %collective-permute-start.8 = (bf16[512,512]{1,0:T(8,128)(2,1)}, bf16[512,512]{1,0:T(8,128)(2,1)S(1)}, u32[]{:S(2)}, u32[]{:S(2)}) collective-permute-start(bf16[512,512]{1,0:T(8,128)(2,1)} %collective-permute-done.2.x2_hbm), channel_id=1, source_target_pairs={{0,1},{1,0},{2,3},{3,2},{4,5},{5,4},{6,7},{7,6},{8,9},{9,8},{10,11... | collective-permute-start | bytes 1572872 | tf_op jit(solution)/shard_map/ppermute | solution.py:291
  52.4 2.6 %collective-permute-start.6 = (bf16[128,512]{1,0:T(8,128)(2,1)S(1)}, bf16[128,512]{1,0:T(8,128)(2,1)S(1)}, u32[]{:S(2)}, u32[]{:S(2)}) collective-permute-start(bf16[128,512]{1,0:T(8,128)(2,1)S(1)} %collective-permute-done.1.dy_ref), channel_id=1, source_target_pairs={{0,1},{1,0},{2,3},{3,2},{4,5},{5,4},{6,7},{7,6},{8,9},{9,8},{10,11... | collective-permute-start | bytes 393224 | tf_op jit(solution)/shard_map/ppermute | solution.py:291
  54.5 10.9 %collective-permute-start.5 = (bf16[128,768]{1,0:T(8,128)(2,1)S(1)}, bf16[128,768]{1,0:T(8,128)(2,1)S(1)}, u32[]{:S(2)}, u32[]{:S(2)}) collective-permute-start(bf16[128,768]{1,0:T(8,128)(2,1)S(1)} %shard_map.99), channel_id=1, source_target_pairs={{0,2},{1,3},{2,0},{3,1},{4,6},{5,7},{6,4},{7,5},{8,10},{9,11},{10,... | collective-permute-start | bytes 589832 | tf_op jit(solution)/shard_map/ppermute | solution.py:291
  56.6 8.8 %collective-permute-start.7 = (bf16[128,768]{1,0:T(8,128)(2,1)S(1)}, bf16[128,768]{1,0:T(8,128)(2,1)S(1)}, u32[]{:S(2)}, u32[]{:S(2)}) collective-permute-start(bf16[128,768]{1,0:T(8,128)(2,1)S(1)} %shard_map.100), channel_id=1, source_target_pairs={{0,3},{1,2},{2,1},{3,0},{4,7},{5,6},{6,5},{7,4},{8,11},{9,10},{10,... | collective-permute-start | bytes 589832 | tf_op jit(solution)/shard_map/ppermute | solution.py:291

commit v6 on v5

--- a/solution.py
+++ b/solution.py
@@ -98,57 +98,67 @@
     copies[4].wait()
 
 
-def share_kernel(slots, me_ref, apb_ref, row_ref, got_ref, out_ref):
-    blocks = out_ref.shape[0]
-    for j in range(blocks):
-        owner = lax.div(row_ref[apb_ref[me_ref[0] * blocks + j]], slots)
-        out_ref[j] = got_ref[owner]
-
-
-def block_kernel(
-    down_part, up_part, x_ref, dy_ref, fac_ref, grads_ref, back_ref
-):
-    shares = fac_ref.shape[0]
+def peer_of(by_xor, at_ref, k):
+    return lax.bitwise_xor(at_ref[0], k) if by_xor else k
+
+
+def columns(ref, peer, width):
+    if isinstance(peer, int):
+        return ref[:, peer * width : (peer + 1) * width]
+    return ref[:, pl.ds(pl.multiple_of(peer * width, LANES), width)]
+
+
+def share_kernel(by_xor, slots, at_ref, me_ref, apb_ref, row_ref, got_ref, *out_refs):
+    blocks = len(out_refs)
+    for k, out_ref in enumerate(out_refs):
+        block = me_ref[0] * blocks + peer_of(by_xor, at_ref, k)
+        out_ref[...] = got_ref[lax.div(row_ref[apb_ref[block]], slots)]
+
+
+def block_kernel(by_xor, down_part, up_part, shares, at_ref, x_ref, dy_ref, *refs):
+    fac_refs, grads_refs, back_ref = refs[:shares], refs[shares:-1], refs[-1]
     up_at = round_up(down_part)
-    back_at = up_at + round_up(up_part)
-    low_t = jnp.zeros((fac_ref.shape[1], BLOCK), jnp.float32)
-    back_t = jnp.zeros((fac_ref.shape[1], BLOCK), jnp.float32)
+    wide = up_at + round_up(up_part)
+    peers = [peer_of(by_xor, at_ref, k) for k in range(shares)]
+    rank = fac_refs[0].shape[0]
+    low_t = jnp.zeros((rank, BLOCK), jnp.float32)
+    back_t = jnp.zeros((rank, BLOCK), jnp.float32)
     for k in range(shares):
         back_t += dot(
-            fac_ref[k, :, up_at : up_at + up_part],
-            dy_ref[:, k * up_part : (k + 1) * up_part],
-            NT,
+            fac_refs[k][:, up_at : up_at + up_part], columns(dy_ref, peers[k], up_part), NT
         )
     scaled = adapter_scale * back_t
     back = scaled.astype(jnp.bfloat16)
     back_ref[...] = scaled.T.astype(jnp.bfloat16)
     for k in range(shares):
-        x = x_ref[:, k * down_part : (k + 1) * down_part]
-        low_t += dot(fac_ref[k, :, :down_part], x, NT)
-        grads_ref[k, :, :down_part] = dot(back, x).astype(jnp.bfloat16)
-        grads_ref[k, :, back_at:] = back
+        x = columns(x_ref, peers[k], down_part)
+        low_t += dot(fac_refs[k][:, :down_part], x, NT)
+        grads_refs[k][:, :down_part] = dot(back, x).astype(jnp.bfloat16)
+        grads_refs[k][:, wide:] = back
     low = low_t.astype(jnp.bfloat16)
     for k in range(shares):
-        grads_ref[k, :, up_at : up_at + up_part] = (
-            adapter_scale * dot(low, dy_ref[:, k * up_part : (k + 1) * up_part])
+        grads_refs[k][:, up_at : up_at + up_part] = (
+            adapter_scale * dot(low, columns(dy_ref, peers[k], up_part))
         ).astype(jnp.bfloat16)
 
 
-def owner_kernel(slots, me_ref, apb_ref, row_ref, got_ref, out_ref, total_ref):
-    blocks = got_ref.shape[0]
+def owner_kernel(by_xor, slots, at_ref, me_ref, apb_ref, row_ref, *refs):
+    got_refs, out_ref, total_ref = refs[:-2], refs[-2], refs[-1]
+    blocks = len(got_refs)
     wide = out_ref.shape[2]
     owners = [
-        lax.div(row_ref[apb_ref[me_ref[0] * blocks + j]], slots) for j in range(blocks)
+        lax.div(row_ref[apb_ref[me_ref[0] * blocks + peer_of(by_xor, at_ref, k)]], slots)
+        for k in range(blocks)
     ]
     out_ref[...] = jnp.zeros_like(out_ref)
     for j in range(blocks):
-        total_ref[...] = got_ref[j, :, :wide].astype(jnp.float32)
+        total_ref[...] = got_refs[j][:, :wide].astype(jnp.float32)
         for i in range(blocks):
             if i != j:
 
                 @pl.when(owners[i] == owners[j])
                 def _():
-                    total_ref[...] += got_ref[i, :, :wide].astype(jnp.float32)
+                    total_ref[...] += got_refs[i][:, :wide].astype(jnp.float32)
 
         out_ref[owners[j]] = total_ref[...].astype(jnp.bfloat16)
 
@@ -173,22 +183,22 @@
         up_ref[s] = up_ref[s] / divisor
 
 
-def far_kernel(near, bits, at_ref, w_hbm, dy_ref, share_ref, got_ref, z_ref, w_ref, sems):
+def far_kernel(near, w_hbm, dy_ref, share_ref, got_ref, z_ref, w_ref, sems):
     tokens, rows = z_ref.shape
     copies = fetch([w_hbm.at[pl.ds(near, rows)]], [w_ref], sems)
-    peer = lax.bitwise_xor(at_ref[0], bits)
     dy_t = turned(dy_ref[...])
-    back = turned(got_ref[peer, :, got_ref.shape[2] - tokens :])
-    adapted = dot(back, share_ref[peer, :, near : near + rows])
+    back = turned(got_ref[:, got_ref.shape[1] - tokens :])
+    adapted = dot(back, share_ref[:, near : near + rows])
     copies[0].wait()
     z_ref[...] = (dot(w_ref[...], dy_t).T + adapted).astype(jnp.bfloat16)
 
 
 def input_kernel(
-    at_ref, side_ref, back_ref, fac_ref, dy_hbm, y2_hbm, y3_hbm, x2_hbm, x3_hbm, w0_hbm, w1_hbm,
+    at_ref, side_ref, back_ref, fac0_ref, fac1_ref, fac2_ref, fac3_ref, dy_hbm, y2_hbm, y3_hbm, x2_hbm, x3_hbm, w0_hbm, w1_hbm,
     out_ref, dy_ref, few_ref, w0_ref, w1_ref, buf, fetch_sems, sems,
 ):
     part = w0_ref.shape[0]
+    fac_refs = (fac0_ref, fac1_ref, fac2_ref, fac3_ref)
     taken = few_ref.shape[1]
     side = side_ref[0] * taken
     few = [a.at[pl.ds(0, taken)] for a in (y2_hbm, y3_hbm, x2_hbm, x3_hbm)]
@@ -215,7 +225,7 @@
         start = pl.multiple_of(start, LANES)
         buf[i, :, :rows] = (
             dot(w_ref[...], dy_t).T
-            + dot(back_ref[...], fac_ref[peer, :, pl.ds(start, rows)])
+            + dot(back_ref[...], fac_refs[k][:, pl.ds(start, rows)])
         ).astype(jnp.bfloat16)
         first = pl.multiple_of(peer * part + start, LANES)
         copy = pltpu.make_async_copy(
@@ -290,6 +300,13 @@
     def cross(array, bit, axis="fsdp"):
         return lax.ppermute(array, axis, [(i, i ^ bit) for i in range(lax.axis_size(axis))])
 
+    def exchange(arrays):
+        if by_permute:
+            return [cross(a, k) if k else a for k, a in enumerate(arrays)]
+        stacked = lax.all_to_all(jnp.stack(arrays), "fsdp", split_axis=0, concat_axis=0, tiled=True)
+        return [stacked[k] for k in range(fsdp_count)]
+
+    at = at.reshape(1)
     index = (me, adapter_per_block, adapter_table_row)
     send, want, count, some = call(
         functools.partial(pick_kernel, fsdp_count),
@@ -330,60 +347,58 @@
     else:
         at_hand = projection_input
     share = call(
-        functools.partial(share_kernel, slots),
-        shaped(fsdp_count, rank, wide),
-        VMEM,
+        functools.partial(share_kernel, by_permute, slots),
+        [shaped(rank, wide)] * fsdp_count,
+        [VMEM] * fsdp_count,
+        at,
         *index,
         owned,
-        smem=3,
+        smem=4,
     )
     if by_permute:
         x2, share, dy2, beside = lax.optimization_barrier((y2, share, dy2, value_weight))
         near = cross(beside, 1), cross(x2, 1)
         x2 = cross(x2, 1, "dp")
-    factors = lax.all_to_all(share, "fsdp", split_axis=0, concat_axis=0, tiled=True)
-    grads, back = call(
-        functools.partial(block_kernel, down_part, up_part),
-        (
-            shaped(fsdp_count, rank, wide + BLOCK),
-            shaped(BLOCK, rank),
-        ),
-        (VMEM, VMEM),
+    factors = exchange(share)
+    *grads, back = call(
+        functools.partial(block_kernel, by_permute, down_part, up_part, fsdp_count),
+        [shaped(rank, wide + BLOCK)] * fsdp_count + [shaped(BLOCK, rank)],
+        [VMEM] * (fsdp_count + 1),
+        at,
         at_hand,
         value_cotangent,
-        factors,
+        *factors,
+        smem=1,
         vmem=20,
     )
-    got = lax.all_to_all(grads, "fsdp", split_axis=0, concat_axis=0, tiled=True)
+    got = exchange(grads)
     if by_permute:
         got, x2, near = lax.optimization_barrier((got, x2, near))
         got, dy2 = lax.optimization_barrier((got, dy2))
         x3, dy3 = cross(x2, 1), cross(dy2, 1)
     sums = call(
-        functools.partial(owner_kernel, slots),
+        functools.partial(owner_kernel, by_permute, slots),
         shaped(dp_count, rank, wide),
         VMEM,
+        at,
         *index,
-        got,
-        smem=3,
+        *got,
+        smem=4,
         scratch=[pltpu.VMEM((rank, wide), jnp.float32)],
     )
     arrived = lax.all_to_all(sums, "dp", split_axis=0, concat_axis=0, tiled=True)
     if by_permute:
-        at = at.reshape(1)
         far_rows = down_part - near_rows
         z2, z3 = (
             cross(
                 call(
-                    functools.partial(far_kernel, near_rows, bits),
+                    functools.partial(far_kernel, near_rows),
                     shaped(BLOCK, far_rows),
                     VMEM,
-                    at,
                     *in_hbm(value_weight),
                     dy,
-                    share,
-                    got,
-                    smem=1,
+                    share[bits],
+                    got[bits],
                     specs=[ANY] + [VMEM] * 3,
                     vmem=12,
                     scratch=[
@@ -402,14 +417,14 @@
             at,
             side,
             back,
-            factors,
+            *factors,
             *in_hbm(value_cotangent, y2),
             near[1],
             *in_hbm(x2),
             x3,
             *in_hbm(value_weight, near[0]),
             smem=2,
-            specs=[VMEM] * 2 + [ANY] * 7,
+            specs=[VMEM] * 5 + [ANY] * 7,
             vmem=24,
             scratch=[
                 pltpu.VMEM(value_cotangent.shape, bf16),
@@ -449,13 +464,17 @@
     )
     if not by_permute:
         weight = lax.all_gather(value_weight, "fsdp", axis=0, tiled=True)
-        adapter_term = jnp.einsum(
-            "tr,krd->tkd", back, factors[:, :, :down_part], preferred_element_type=jnp.float32
+        adapter_term = jnp.concatenate(
+            [
+                jnp.dot(back, share[:, :down_part], preferred_element_type=jnp.float32)
+                for share in factors
+            ],
+            axis=1,
         )
         frozen_term = jnp.einsum(
             "tc,dc->td", value_cotangent, weight, preferred_element_type=jnp.float32
         )
-        grad_input = (frozen_term + adapter_term.reshape(tok_rows, width)).astype(bf16)
+        grad_input = (frozen_term + adapter_term).astype(bf16)
     return (grad_input, grad_down, grad_up)
 
 

time: 68.5 us -> 65 us (0.949)
  blocking collectives: 16.9 us -> 0 us
  waiting for transfers between devices: 12.1 us -> 19.4 us
  starting transfers between devices: 17.9 us -> 24.1 us
    all_to_all x2 -> x0, blocking collectives: 16.9 us -> none  [the longest x1 8.44 us: per_device(): lax.all_to_all(share, 'fsdp', split_axis=0, concat_axis=0, tiled=True)]
    ppermute x9 -> x15, waiting for transfers between devices: 12.1 us -> 19.2 us  [cross(): lax.ppermute(array, axis, [(i, i ^ bit) for i in range(lax.axis_size(axis...]
    ppermute x9 -> x15, starting transfers between devices: 6.04 us -> 12.1 us  [cross(): lax.ppermute(array, axis, [(i, i ^ bit) for i in range(lax.axis_size(axis...]
  transfers between devices with their start and end apart: 11 -> 17, of which waited for: 2 -> 8; matrix products, arithmetic and copies ran while one was open for 0% -> 0% of each run, Pallas kernels for 22% -> 24%
where the time goes in v6:
time: 65 us; the launch traced here: 64.5 us
  starting transfers between devices  24.1 us (37%)
  Pallas kernels  20.2 us (31%)
  waiting for transfers between devices  19.4 us (30%)
  between operations  0.76 us (1%)
    pallas_call x10, Pallas kernels, call(): pl.pallas_call(kernel, out_shape=out_shape, in_specs=[SMEM] * smem + (spe...  20.2 us
    ppermute x15, waiting for transfers between devices, cross(): lax.ppermute(array, axis, [(i, i ^ bit) for i in range(lax.axis_size(axis...  19.2 us
    ppermute x15, starting transfers between devices, cross(): lax.ppermute(array, axis, [(i, i ^ bit) for i in range(lax.axis_size(axis...  12.1 us
    all_to_all x1, starting transfers between devices, per_device(): owned = lax.all_to_all(send, 'dp', split_axis=0, concat_axis=0, tiled=True)  7.26 us
    all_to_all x1, starting transfers between devices, per_device(): lax.all_to_all(sums, 'dp', split_axis=0, concat_axis=0, tiled=True)  4.74 us
  transfers between devices with their start and end apart: 17, of which 8 were waited for; matrix products, arithmetic and copies ran while one was open for 0% of the time, Pallas kernels for 24%

profile of v6, /device:TPU:0, one launch (start us, length us, event | category | flops | bytes accessed | tf_op | source)
XLA Modules:
  0.0 64.5 jit_solution(12467661162279086364)
XLA Ops:
  0.6 0.0 copy-start
  0.6 2.0 %shard_map.94 = (bf16[8,16,1920]{2,1,0:T(8,128)(2,1)}, s32[8]{0:T(128)S(1)}, s32[5]{0:T(128)S(1)}, bf16[512,512]{1,0:T(8,128)(2,1)S(1)}) custom-call(s32[1]{0:T(128)} %bitcast.1.me_ref, s32[32]{0:T(128)} %apb_ref.3, s32[40]{0:T(128)} %row_ref.3, bf16[5,16,1792]{2,1,0:T(8,128)(2,1)} %down_hbm.1, bf16[5,16,128]{2,1,0:T(8,128)(2,1)} %up_hbm.1, ...), custom_call_target="tpu_custom_call" | custom-call | tf_op jit(solution)/shard_map/pallas_call | solution.py:261
  2.7 7.3 %all-to-all-start = ((bf16[8,16,1920]{2,1,0:T(8,128)(2,1)}), bf16[8,16,1920]{2,1,0:T(8,128)(2,1)S(1)}, u32[]{:S(2)}, u32[]{:S(2)}) async-start(bf16[8,16,1920]{2,1,0:T(8,128)(2,1)} %get-tuple-element.43), calls=%async_computation | async-start | bytes 983040 | tf_op jit(solution)/shard_map/all_to_all | solution.py:332
  9.9 0.0 copy-start.1
  9.9 0.0 copy-start.2
  10.0 1.6 %collective-permute-start = (bf16[512,512]{1,0:T(8,128)(2,1)S(1)}, bf16[512,512]{1,0:T(8,128)(2,1)}, u32[]{:S(2)}, u32[]{:S(2)}) collective-permute-start(bf16[512,512]{1,0:T(8,128)(2,1)S(1)} %get-tuple-element.44), channel_id=1, source_target_pairs={{0,2},{1,3},{2,0},{3,1},{4,6},{5,7},{6,4},{7,5},{8,10},{9,11},{10,... | collective-permute-start | bytes 1572872 | tf_op jit(solution)/shard_map/ppermute | solution.py:301
  11.5 0.0 copy-done
  11.5 0.5 collective-permute-start.1
  12.0 1.5 %shard_map.95.x_ref = bf16[128,7168]{1,0:T(8,128)(2,1)S(1)} custom-call(bf16[128,7168]{1,0:T(8,128)(2,1)} %from_ref), custom_call_target="tpu_custom_call" | custom-call | tf_op jit(solution)/shard_map/pallas_call | solution.py:261
  13.6 11.3 %collective-permute-done.y2_hbm = bf16[512,512]{1,0:T(8,128)(2,1)} collective-permute-done((bf16[512,512]{1,0:T(8,128)(2,1)S(1)}, bf16[512,512]{1,0:T(8,128)(2,1)}, u32[]{:S(2)}, u32[]{:S(2)}) %collective-permute-start) | collective-permute-done | bytes 524320 | tf_op jit(solution)/shard_map/ppermute | solution.py:301
  24.9 0.0 all-to-all-done.got_ref
  24.9 0.0 copy-done.1
  24.9 0.0 copy-done.2
  24.9 0.6 shard_map.96
  25.5 0.7 %collective-permute-done.1.dy_ref = bf16[128,512]{1,0:T(8,128)(2,1)S(1)} collective-permute-done((bf16[128,512]{1,0:T(8,128)(2,1)S(1)}, bf16[128,512]{1,0:T(8,128)(2,1)S(1)}, u32[]{:S(2)}, u32[]{:S(2)}) %collective-permute-start.1) | collective-permute-done | bytes 131104 | tf_op jit(solution)/shard_map/ppermute | solution.py:301
  26.2 0.0 collective-permute-start.9
  26.2 0.5 collective-permute-start.10
  26.7 1.7 %collective-permute-start.8 = (bf16[512,512]{1,0:T(8,128)(2,1)}, bf16[512,512]{1,0:T(8,128)(2,1)}, u32[]{:S(2)}, u32[]{:S(2)}) collective-permute-start(bf16[512,512]{1,0:T(8,128)(2,1)} %collective-permute-done.y2_hbm), channel_id=1, source_target_pairs={{0,4},{4,0},{8,12},{12,8},{16,20},{20,16},{24,28},{28,24},{1,5},{5... | collective-permute-start | bytes 1572872 | tf_op jit(solution)/shard_map/ppermute | solution.py:301
  28.4 0.0 collective-permute-start.2
  28.4 1.5 %collective-permute-start.3 = (bf16[16,1920]{1,0:T(8,128)(2,1)S(1)}, bf16[16,1920]{1,0:T(8,128)(2,1)S(1)}, u32[]{:S(2)}, u32[]{:S(2)}) collective-permute-start(bf16[16,1920]{1,0:T(8,128)(2,1)S(1)} %get-tuple-element.55.share_ref), channel_id=1, source_target_pairs={{0,2},{1,3},{2,0},{3,1},{4,6},{5,7},{6,4},{7,5},{8,10},{9,11},{10,... | collective-permute-start | bytes 184328 | tf_op jit(solution)/shard_map/ppermute | solution.py:301
  29.9 0.9 %collective-permute-done.2.refs_1_.fac1_ref = bf16[16,1920]{1,0:T(8,128)(2,1)S(1)} collective-permute-done((bf16[16,1920]{1,0:T(8,128)(2,1)S(1)}, bf16[16,1920]{1,0:T(8,128)(2,1)S(1)}, u32[]{:S(2)}, u32[]{:S(2)}) %collective-permute-start.2) | collective-permute-done | bytes 61472 | tf_op jit(solution)/shard_map/ppermute | solution.py:301
  30.8 1.3 %collective-permute-start.4 = (bf16[16,1920]{1,0:T(8,128)(2,1)S(1)}, bf16[16,1920]{1,0:T(8,128)(2,1)S(1)}, u32[]{:S(2)}, u32[]{:S(2)}) collective-permute-start(bf16[16,1920]{1,0:T(8,128)(2,1)S(1)} %get-tuple-element.56.share_ref), channel_id=1, source_target_pairs={{0,3},{1,2},{2,1},{3,0},{4,7},{5,6},{6,5},{7,4},{8,11},{9,10},{10,... | collective-permute-start | bytes 184328 | tf_op jit(solution)/shard_map/ppermute | solution.py:301
  32.1 0.7 %collective-permute-done.3.refs_2_.fac2_ref = bf16[16,1920]{1,0:T(8,128)(2,1)S(1)} collective-permute-done((bf16[16,1920]{1,0:T(8,128)(2,1)S(1)}, bf16[16,1920]{1,0:T(8,128)(2,1)S(1)}, u32[]{:S(2)}, u32[]{:S(2)}) %collective-permute-start.3) | collective-permute-done | bytes 61472 | tf_op jit(solution)/shard_map/ppermute | solution.py:301
  32.8 2.0 %collective-permute-done.4.refs_3_.fac3_ref = bf16[16,1920]{1,0:T(8,128)(2,1)S(1)} collective-permute-done((bf16[16,1920]{1,0:T(8,128)(2,1)S(1)}, bf16[16,1920]{1,0:T(8,128)(2,1)S(1)}, u32[]{:S(2)}, u32[]{:S(2)}) %collective-permute-start.4) | collective-permute-done | bytes 61472 | tf_op jit(solution)/shard_map/ppermute | solution.py:301
  34.8 1.3 %shard_map.97 = (bf16[16,2048]{1,0:T(8,128)(2,1)S(1)}, bf16[16,2048]{1,0:T(8,128)(2,1)S(1)}, bf16[16,2048]{1,0:T(8,128)(2,1)S(1)}, bf16[16,2048]{1,0:T(8,128)(2,1)S(1)}, bf16[128,16]{1,0:T(8,128)(2,1)S(1)}) custom-call(s32[1]{0:T(128)} %bitcast.at_ref, bf16[128,7168]{1,0:T(8,128)(2,1)S(1)} %shard_map.95.x_ref, bf16[128,512]{1,0:T(8,128)(2,1)S(1)} %copy-done, ...), custom_call_target="tpu_custom_call" | custom-call | tf_op jit(solution)/shard_map/pallas_call | solution.py:261
  36.2 0.6 collective-permute-start.5
  36.7 1.5 %collective-permute-start.6 = (bf16[16,2048]{1,0:T(8,128)(2,1)S(1)}, bf16[16,2048]{1,0:T(8,128)(2,1)S(1)}, u32[]{:S(2)}, u32[]{:S(2)}) collective-permute-start(bf16[16,2048]{1,0:T(8,128)(2,1)S(1)} %get-tuple-element.59), channel_id=1, source_target_pairs={{0,2},{1,3},{2,0},{3,1},{4,6},{5,7},{6,4},{7,5},{8,10},{9,11},{10,... | collective-permute-start | bytes 196616 | tf_op jit(solution)/shard_map/ppermute | solution.py:301
  38.3 0.0 collective-permute-done.5.refs_1_
  38.3 0.9 %collective-permute-start.7 = (bf16[16,2048]{1,0:T(8,128)(2,1)S(1)}, bf16[16,2048]{1,0:T(8,128)(2,1)S(1)}, u32[]{:S(2)}, u32[]{:S(2)}) collective-permute-start(bf16[16,2048]{1,0:T(8,128)(2,1)S(1)} %get-tuple-element.60), channel_id=1, source_target_pairs={{0,3},{1,2},{2,1},{3,0},{4,7},{5,6},{6,5},{7,4},{8,11},{9,10},{10,... | collective-permute-start | bytes 196616 | tf_op jit(solution)/shard_map/ppermute | solution.py:301
  39.1 1.9 %collective-permute-done.6.refs_2_.got_ref = bf16[16,2048]{1,0:T(8,128)(2,1)S(1)} collective-permute-done((bf16[16,2048]{1,0:T(8,128)(2,1)S(1)}, bf16[16,2048]{1,0:T(8,128)(2,1)S(1)}, u32[]{:S(2)}, u32[]{:S(2)}) %collective-permute-start.6) | collective-permute-done | bytes 65568 | tf_op jit(solution)/shard_map/ppermute | solution.py:301
  41.0 1.6 %collective-permute-done.7.refs_3_.got_ref = bf16[16,2048]{1,0:T(8,128)(2,1)S(1)} collective-permute-done((bf16[16,2048]{1,0:T(8,128)(2,1)S(1)}, bf16[16,2048]{1,0:T(8,128)(2,1)S(1)}, u32[]{:S(2)}, u32[]{:S(2)}) %collective-permute-start.7) | collective-permute-done | bytes 65568 | tf_op jit(solution)/shard_map/ppermute | solution.py:301
  42.6 0.0 collective-permute-done.10.y3_hbm
  42.6 0.0 collective-permute-done.8.x2_hbm
  42.6 0.0 collective-permute-done.9.w1_hbm
  42.6 1.5 %shard_map.98 = bf16[8,16,1920]{2,1,0:T(8,128)(2,1)} custom-call(s32[1]{0:T(128)} %bitcast.at_ref, s32[1]{0:T(128)} %bitcast.1.me_ref, s32[32]{0:T(128)S(1)} %copy-done.1, s32[40]{0:T(128)S(1)} %copy-done.2, bf16[16,2048]{1,0:T(8,128)(2,1)S(1)} %get-tuple-element.68.refs_0_, bf16[16,2048]{1,0:T(8,128)(2,1)S(1)} %collective-permute-done.5.refs_1_, ...), custom_call_target="tpu_custom_call" | custom-call | tf_op jit(solution)/shard_map/pallas_call | solution.py:261
  44.1 4.7 %all-to-all-start.1 = ((bf16[8,16,1920]{2,1,0:T(8,128)(2,1)}), bf16[8,16,1920]{2,1,0:T(8,128)(2,1)S(1)}, u32[]{:S(2)}, u32[]{:S(2)}) async-start(bf16[8,16,1920]{2,1,0:T(8,128)(2,1)} %shard_map.98), calls=%async_computation.1 | async-start | bytes 983040 | tf_op jit(solution)/shard_map/all_to_all | solution.py:389
  48.9 0.0 collective-permute-start.14
  48.9 0.5 collective-permute-start.12
  49.4 1.7 %shard_map.99 = bf16[128,768]{1,0:T(8,128)(2,1)S(1)} custom-call(bf16[1792,512]{1,0:T(8,128)(2,1)} %w0_hbm.1, bf16[128,512]{1,0:T(8,128)(2,1)S(1)} %collective-permute-done.1.dy_ref, bf16[16,1920]{1,0:T(8,128)(2,1)S(1)} %get-tuple-element.55.share_ref, bf16[16,2048]{1,0:T(8,128)(2,1)S(1)} %collective-permute-done.6.refs_2_.got_ref), custom_call_target="tpu_custom_call" | custom-call | tf_op jit(solution)/shard_map/pallas_call | solution.py:261
  51.1 1.0 %collective-permute-start.11 = (bf16[128,768]{1,0:T(8,128)(2,1)S(1)}, bf16[128,768]{1,0:T(8,128)(2,1)S(1)}, u32[]{:S(2)}, u32[]{:S(2)}) collective-permute-start(bf16[128,768]{1,0:T(8,128)(2,1)S(1)} %shard_map.99), channel_id=1, source_target_pairs={{0,2},{1,3},{2,0},{3,1},{4,6},{5,7},{6,4},{7,5},{8,10},{9,11},{10,... | collective-permute-start | bytes 589832 | tf_op jit(solution)/shard_map/ppermute | solution.py:301
  52.0 0.0 collective-permute-done.12.dy_ref
  52.0 1.7 %shard_map.100 = bf16[128,768]{1,0:T(8,128)(2,1)S(1)} custom-call(bf16[1792,512]{1,0:T(8,128)(2,1)} %w0_hbm.1, bf16[128,512]{1,0:T(8,128)(2,1)S(1)} %collective-permute-done.12.dy_ref, bf16[16,1920]{1,0:T(8,128)(2,1)S(1)} %get-tuple-element.56.share_ref, bf16[16,2048]{1,0:T(8,128)(2,1)S(1)} %collective-permute-done.7.refs_3_.got_ref), custom_call_target="tpu_custom_call" | custom-call | tf_op jit(solution)/shard_map/pallas_call | solution.py:261
  53.7 0.6 collective-permute-start.13
  54.3 0.0 collective-permute-done.14.x3_hbm
  54.3 7.6 %shard_map.101.in_ref = bf16[128,7168]{1,0:T(8,128)(2,1)} custom-call(s32[1]{0:T(128)} %bitcast.at_ref, s32[1]{0:T(128)S(6)} %and.5.side_ref, bf16[128,16]{1,0:T(8,128)(2,1)S(1)} %get-tuple-element.73.back_ref, bf16[16,1920]{1,0:T(8,128)(2,1)S(1)} %get-tuple-element.53.refs_0_.fac0_ref, bf16[16,1920]{1,0:T(8,128)(2,1)S(1)} %collective-permute-done.2.refs_1_.fac1_ref, ...), custom_call_target="tpu_custom_call" | custom-call | tf_op jit(solution)/shard_map/pallas_call | solution.py:261
  61.9 0.0 collective-permute-done.11.z2_ref
  61.9 0.0 collective-permute-done.13.z3_ref
  62.0 0.8 %shard_map.102 = bf16[128,7168]{1,0:T(8,128)(2,1)} custom-call(s32[1]{0:T(128)} %bitcast.at_ref, bf16[128,768]{1,0:T(8,128)(2,1)S(1)} %collective-permute-done.11.z2_ref, bf16[128,768]{1,0:T(8,128)(2,1)S(1)} %collective-permute-done.13.z3_ref, bf16[128,7168]{1,0:T(8,128)(2,1)} %shard_map.101.in_ref), custom_call_target="tpu_custom_call", output_to_operand_aliasing={{}: (3, {})} | custom-call | tf_op jit(solution)/shard_map/pallas_call | solution.py:261
  62.7 0.2 all-to-all-done.1.got_ref
  62.9 1.6 %shard_map.103 = (f32[5,16,1792]{2,1,0:T(8,128)}, f32[5,16,128]{2,1,0:T(8,128)}) custom-call(s32[8]{0:T(128)S(1)} %get-tuple-element.78.want_ref, s32[5]{0:T(128)S(1)} %get-tuple-element.79.count_ref, bf16[8,16,1920]{2,1,0:T(8,128)(2,1)S(1)} %all-to-all-done.1.got_ref), custom_call_target="tpu_custom_call" | custom-call | tf_op jit(solution)/shard_map/pallas_call | solution.py:261
Async XLA Ops:
  0.6 10.9 %copy-start = (bf16[128,512]{1,0:T(8,128)(2,1)S(1)}, bf16[128,512]{1,0:T(8,128)(2,1)}, u32[]{:S(2)}) copy-start(bf16[128,512]{1,0:T(8,128)(2,1)} %dy_hbm.1) | copy-start | bytes 393220
  2.7 22.2 %all-to-all-start = ((bf16[8,16,1920]{2,1,0:T(8,128)(2,1)}), bf16[8,16,1920]{2,1,0:T(8,128)(2,1)S(1)}, u32[]{:S(2)}, u32[]{:S(2)}) async-start(bf16[8,16,1920]{2,1,0:T(8,128)(2,1)} %get-tuple-element.43), calls=%async_computation | async-start | bytes 983040 | tf_op jit(solution)/shard_map/all_to_all | solution.py:332
  9.9 15.0 %copy-start.1 = (s32[32]{0:T(128)S(1)}, s32[32]{0:T(128)}, u32[]{:S(2)}) copy-start(s32[32]{0:T(128)} %apb_ref.3) | copy-start | bytes 388
  9.9 15.0 %copy-start.2 = (s32[40]{0:T(128)S(1)}, s32[40]{0:T(128)}, u32[]{:S(2)}) copy-start(s32[40]{0:T(128)} %row_ref.3) | copy-start | bytes 484
  10.0 15.0 %collective-permute-start = (bf16[512,512]{1,0:T(8,128)(2,1)S(1)}, bf16[512,512]{1,0:T(8,128)(2,1)}, u32[]{:S(2)}, u32[]{:S(2)}) collective-permute-start(bf16[512,512]{1,0:T(8,128)(2,1)S(1)} %get-tuple-element.44), channel_id=1, source_target_pairs={{0,2},{1,3},{2,0},{3,1},{4,6},{5,7},{6,4},{7,5},{8,10},{9,11},{10,... | collective-permute-start | bytes 1572872 | tf_op jit(solution)/shard_map/ppermute | solution.py:301
  11.5 14.7 %collective-permute-start.1 = (bf16[128,512]{1,0:T(8,128)(2,1)S(1)}, bf16[128,512]{1,0:T(8,128)(2,1)S(1)}, u32[]{:S(2)}, u32[]{:S(2)}) collective-permute-start(bf16[128,512]{1,0:T(8,128)(2,1)S(1)} %copy-done), channel_id=1, source_target_pairs={{0,2},{1,3},{2,0},{3,1},{4,6},{5,7},{6,4},{7,5},{8,10},{9,11},{10,... | collective-permute-start | bytes 393224 | tf_op jit(solution)/shard_map/ppermute | solution.py:301
  26.2 16.4 %collective-permute-start.9 = (bf16[1792,512]{1,0:T(8,128)(2,1)}, bf16[1792,512]{1,0:T(8,128)(2,1)}, u32[]{:S(2)}, u32[]{:S(2)}) collective-permute-start(bf16[1792,512]{1,0:T(8,128)(2,1)} %w0_hbm.1), channel_id=1, source_target_pairs={{0,1},{1,0},{2,3},{3,2},{4,5},{5,4},{6,7},{7,6},{8,9},{9,8},{10,11... | collective-permute-start | bytes 5505032 | tf_op jit(solution)/shard_map/ppermute | solution.py:301
  26.2 16.4 %collective-permute-start.10 = (bf16[512,512]{1,0:T(8,128)(2,1)}, bf16[512,512]{1,0:T(8,128)(2,1)S(1)}, u32[]{:S(2)}, u32[]{:S(2)}) collective-permute-start(bf16[512,512]{1,0:T(8,128)(2,1)} %collective-permute-done.y2_hbm), channel_id=1, source_target_pairs={{0,1},{1,0},{2,3},{3,2},{4,5},{5,4},{6,7},{7,6},{8,9},{9,8},{10,11... | collective-permute-start | bytes 1572872 | tf_op jit(solution)/shard_map/ppermute | solution.py:301
  26.7 15.9 %collective-permute-start.8 = (bf16[512,512]{1,0:T(8,128)(2,1)}, bf16[512,512]{1,0:T(8,128)(2,1)}, u32[]{:S(2)}, u32[]{:S(2)}) collective-permute-start(bf16[512,512]{1,0:T(8,128)(2,1)} %collective-permute-done.y2_hbm), channel_id=1, source_target_pairs={{0,4},{4,0},{8,12},{12,8},{16,20},{20,16},{24,28},{28,24},{1,5},{5... | collective-permute-start | bytes 1572872 | tf_op jit(solution)/shard_map/ppermute | solution.py:301
  28.4 2.4 %collective-permute-start.2 = (bf16[16,1920]{1,0:T(8,128)(2,1)S(1)}, bf16[16,1920]{1,0:T(8,128)(2,1)S(1)}, u32[]{:S(2)}, u32[]{:S(2)}) collective-permute-start(bf16[16,1920]{1,0:T(8,128)(2,1)S(1)} %get-tuple-element.54), channel_id=1, source_target_pairs={{0,1},{1,0},{2,3},{3,2},{4,5},{5,4},{6,7},{7,6},{8,9},{9,8},{10,11... | collective-permute-start | bytes 184328 | tf_op jit(solution)/shard_map/ppermute | solution.py:301
  28.4 4.4 %collective-permute-start.3 = (bf16[16,1920]{1,0:T(8,128)(2,1)S(1)}, bf16[16,1920]{1,0:T(8,128)(2,1)S(1)}, u32[]{:S(2)}, u32[]{:S(2)}) collective-permute-start(bf16[16,1920]{1,0:T(8,128)(2,1)S(1)} %get-tuple-element.55.share_ref), channel_id=1, source_target_pairs={{0,2},{1,3},{2,0},{3,1},{4,6},{5,7},{6,4},{7,5},{8,10},{9,11},{10,... | collective-permute-start | bytes 184328 | tf_op jit(solution)/shard_map/ppermute | solution.py:301
  30.8 4.0 %collective-permute-start.4 = (bf16[16,1920]{1,0:T(8,128)(2,1)S(1)}, bf16[16,1920]{1,0:T(8,128)(2,1)S(1)}, u32[]{:S(2)}, u32[]{:S(2)}) collective-permute-start(bf16[16,1920]{1,0:T(8,128)(2,1)S(1)} %get-tuple-element.56.share_ref), channel_id=1, source_target_pairs={{0,3},{1,2},{2,1},{3,0},{4,7},{5,6},{6,5},{7,4},{8,11},{9,10},{10,... | collective-permute-start | bytes 184328 | tf_op jit(solution)/shard_map/ppermute | solution.py:301
  36.2 2.1 %collective-permute-start.5 = (bf16[16,2048]{1,0:T(8,128)(2,1)S(1)}, bf16[16,2048]{1,0:T(8,128)(2,1)S(1)}, u32[]{:S(2)}, u32[]{:S(2)}) collective-permute-start(bf16[16,2048]{1,0:T(8,128)(2,1)S(1)} %get-tuple-element.58), channel_id=1, source_target_pairs={{0,1},{1,0},{2,3},{3,2},{4,5},{5,4},{6,7},{7,6},{8,9},{9,8},{10,11... | collective-permute-start | bytes 196616 | tf_op jit(solution)/shard_map/ppermute | solution.py:301
  36.7 4.3 %collective-permute-start.6 = (bf16[16,2048]{1,0:T(8,128)(2,1)S(1)}, bf16[16,2048]{1,0:T(8,128)(2,1)S(1)}, u32[]{:S(2)}, u32[]{:S(2)}) collective-permute-start(bf16[16,2048]{1,0:T(8,128)(2,1)S(1)} %get-tuple-element.59), channel_id=1, source_target_pairs={{0,2},{1,3},{2,0},{3,1},{4,6},{5,7},{6,4},{7,5},{8,10},{9,11},{10,... | collective-permute-start | bytes 196616 | tf_op jit(solution)/shard_map/ppermute | solution.py:301
  38.3 4.4 %collective-permute-start.7 = (bf16[16,2048]{1,0:T(8,128)(2,1)S(1)}, bf16[16,2048]{1,0:T(8,128)(2,1)S(1)}, u32[]{:S(2)}, u32[]{:S(2)}) collective-permute-start(bf16[16,2048]{1,0:T(8,128)(2,1)S(1)} %get-tuple-element.60), channel_id=1, source_target_pairs={{0,3},{1,2},{2,1},{3,0},{4,7},{5,6},{6,5},{7,4},{8,11},{9,10},{10,... | collective-permute-start | bytes 196616 | tf_op jit(solution)/shard_map/ppermute | solution.py:301
  44.1 18.8 %all-to-all-start.1 = ((bf16[8,16,1920]{2,1,0:T(8,128)(2,1)}), bf16[8,16,1920]{2,1,0:T(8,128)(2,1)S(1)}, u32[]{:S(2)}, u32[]{:S(2)}) async-start(bf16[8,16,1920]{2,1,0:T(8,128)(2,1)} %shard_map.98), calls=%async_computation.1 | async-start | bytes 983040 | tf_op jit(solution)/shard_map/all_to_all | solution.py:389
  48.9 5.4 %collective-permute-start.14 = (bf16[512,512]{1,0:T(8,128)(2,1)}, bf16[512,512]{1,0:T(8,128)(2,1)S(1)}, u32[]{:S(2)}, u32[]{:S(2)}) collective-permute-start(bf16[512,512]{1,0:T(8,128)(2,1)} %collective-permute-done.8.x2_hbm), channel_id=1, source_target_pairs={{0,1},{1,0},{2,3},{3,2},{4,5},{5,4},{6,7},{7,6},{8,9},{9,8},{10,11... | collective-permute-start | bytes 1572872 | tf_op jit(solution)/shard_map/ppermute | solution.py:301
  48.9 3.2 %collective-permute-start.12 = (bf16[128,512]{1,0:T(8,128)(2,1)S(1)}, bf16[128,512]{1,0:T(8,128)(2,1)S(1)}, u32[]{:S(2)}, u32[]{:S(2)}) collective-permute-start(bf16[128,512]{1,0:T(8,128)(2,1)S(1)} %collective-permute-done.1.dy_ref), channel_id=1, source_target_pairs={{0,1},{1,0},{2,3},{3,2},{4,5},{5,4},{6,7},{7,6},{8,9},{9,8},{10,11... | collective-permute-start | bytes 393224 | tf_op jit(solution)/shard_map/ppermute | solution.py:301
  51.1 10.9 %collective-permute-start.11 = (bf16[128,768]{1,0:T(8,128)(2,1)S(1)}, bf16[128,768]{1,0:T(8,128)(2,1)S(1)}, u32[]{:S(2)}, u32[]{:S(2)}) collective-permute-start(bf16[128,768]{1,0:T(8,128)(2,1)S(1)} %shard_map.99), channel_id=1, source_target_pairs={{0,2},{1,3},{2,0},{3,1},{4,6},{5,7},{6,4},{7,5},{8,10},{9,11},{10,... | collective-permute-start | bytes 589832 | tf_op jit(solution)/shard_map/ppermute | solution.py:301
  53.7 8.2 %collective-permute-start.13 = (bf16[128,768]{1,0:T(8,128)(2,1)S(1)}, bf16[128,768]{1,0:T(8,128)(2,1)S(1)}, u32[]{:S(2)}, u32[]{:S(2)}) collective-permute-start(bf16[128,768]{1,0:T(8,128)(2,1)S(1)} %shard_map.100), channel_id=1, source_target_pairs={{0,3},{1,2},{2,1},{3,0},{4,7},{5,6},{6,5},{7,4},{8,11},{9,10},{10,... | collective-permute-start | bytes 589832 | tf_op jit(solution)/shard_map/ppermute | solution.py:301

commit v7 on v6

--- a/solution.py
+++ b/solution.py
@@ -356,8 +356,7 @@
         smem=4,
     )
     if by_permute:
-        x2, share, dy2, beside = lax.optimization_barrier((y2, share, dy2, value_weight))
-        near = cross(beside, 1), cross(x2, 1)
+        x2, share, dy2 = lax.optimization_barrier((y2, share, dy2))
         x2 = cross(x2, 1, "dp")
     factors = exchange(share)
     *grads, back = call(
@@ -373,9 +372,8 @@
     )
     got = exchange(grads)
     if by_permute:
-        got, x2, near = lax.optimization_barrier((got, x2, near))
         got, dy2 = lax.optimization_barrier((got, dy2))
-        x3, dy3 = cross(x2, 1), cross(dy2, 1)
+        dy3 = cross(dy2, 1)
     sums = call(
         functools.partial(owner_kernel, by_permute, slots),
         shaped(dp_count, rank, wide),
@@ -386,6 +384,10 @@
         smem=4,
         scratch=[pltpu.VMEM((rank, wide), jnp.float32)],
     )
+    if by_permute:
+        sums, beside, y2, x2 = lax.optimization_barrier((sums, value_weight, y2, x2))
+        near = cross(beside, 1), cross(y2, 1)
+        x3 = cross(x2, 1)
     arrived = lax.all_to_all(sums, "dp", split_axis=0, concat_axis=0, tiled=True)
     if by_permute:
         far_rows = down_part - near_rows

time: 65 us -> 63.5 us (0.977)
  starting transfers between devices: 24.1 us -> 21.9 us
  waiting for transfers between devices: 19.4 us -> 20.1 us
    ppermute x15, starting transfers between devices: 12.1 us -> 10.1 us  [cross(): lax.ppermute(array, axis, [(i, i ^ bit) for i in range(lax.axis_size(axis...]
    ppermute x15, waiting for transfers between devices: 19.2 us -> 20 us  [cross(): lax.ppermute(array, axis, [(i, i ^ bit) for i in range(lax.axis_size(axis...]
  transfers between devices with their start and end apart: 17 -> 17, of which waited for: 8 -> 7; matrix products, arithmetic and copies ran while one was open for 0% -> 0% of each run, Pallas kernels for 24% -> 26%
where the time goes in v7:
time: 63.5 us; the launch traced here: 63.1 us
  starting transfers between devices  21.9 us (34%)
  Pallas kernels  20.2 us (32%)
  waiting for transfers between devices  20.1 us (32%)
  between operations  0.76 us (1%)
    pallas_call x10, Pallas kernels, call(): pl.pallas_call(kernel, out_shape=out_shape, in_specs=[SMEM] * smem + (spe...  20.2 us
    ppermute x15, waiting for transfers between devices, cross(): lax.ppermute(array, axis, [(i, i ^ bit) for i in range(lax.axis_size(axis...  20 us
    ppermute x15, starting transfers between devices, cross(): lax.ppermute(array, axis, [(i, i ^ bit) for i in range(lax.axis_size(axis...  10.1 us
    all_to_all x1, starting transfers between devices, per_device(): owned = lax.all_to_all(send, 'dp', split_axis=0, concat_axis=0, tiled=True)  7.26 us
    all_to_all x1, starting transfers between devices, per_device(): lax.all_to_all(sums, 'dp', split_axis=0, concat_axis=0, tiled=True)  4.54 us
  transfers between devices with their start and end apart: 17, of which 7 were waited for; matrix products, arithmetic and copies ran while one was open for 0% of the time, Pallas kernels for 26%

profile of v7, /device:TPU:0, one launch (start us, length us, event | category | flops | bytes accessed | tf_op | source)
XLA Modules:
  0.0 63.1 jit_solution(1764713175974143325)
XLA Ops:
  0.6 0.0 copy-start
  0.6 2.0 %shard_map.94 = (bf16[8,16,1920]{2,1,0:T(8,128)(2,1)}, s32[8]{0:T(128)S(1)}, s32[5]{0:T(128)S(1)}, bf16[512,512]{1,0:T(8,128)(2,1)S(1)}) custom-call(s32[1]{0:T(128)} %bitcast.1.me_ref, s32[32]{0:T(128)} %apb_ref.3, s32[40]{0:T(128)} %row_ref.3, bf16[5,16,1792]{2,1,0:T(8,128)(2,1)} %down_hbm.1, bf16[5,16,128]{2,1,0:T(8,128)(2,1)} %up_hbm.1, ...), custom_call_target="tpu_custom_call" | custom-call | tf_op jit(solution)/shard_map/pallas_call | solution.py:261
  2.7 7.3 %all-to-all-start = ((bf16[8,16,1920]{2,1,0:T(8,128)(2,1)}), bf16[8,16,1920]{2,1,0:T(8,128)(2,1)S(1)}, u32[]{:S(2)}, u32[]{:S(2)}) async-start(bf16[8,16,1920]{2,1,0:T(8,128)(2,1)} %get-tuple-element.39), calls=%async_computation | async-start | bytes 983040 | tf_op jit(solution)/shard_map/all_to_all | solution.py:332
  9.9 0.0 copy-start.1
  9.9 0.0 copy-start.2
  10.0 1.6 %collective-permute-start = (bf16[512,512]{1,0:T(8,128)(2,1)S(1)}, bf16[512,512]{1,0:T(8,128)(2,1)}, u32[]{:S(2)}, u32[]{:S(2)}) collective-permute-start(bf16[512,512]{1,0:T(8,128)(2,1)S(1)} %get-tuple-element.40), channel_id=1, source_target_pairs={{0,2},{1,3},{2,0},{3,1},{4,6},{5,7},{6,4},{7,5},{8,10},{9,11},{10,... | collective-permute-start | bytes 1572872 | tf_op jit(solution)/shard_map/ppermute | solution.py:301
  11.5 0.0 copy-done
  11.5 0.5 collective-permute-start.1
  12.0 1.5 %shard_map.95.x_ref = bf16[128,7168]{1,0:T(8,128)(2,1)S(1)} custom-call(bf16[128,7168]{1,0:T(8,128)(2,1)} %from_ref), custom_call_target="tpu_custom_call" | custom-call | tf_op jit(solution)/shard_map/pallas_call | solution.py:261
  13.6 11.3 %collective-permute-done.y2_hbm = bf16[512,512]{1,0:T(8,128)(2,1)} collective-permute-done((bf16[512,512]{1,0:T(8,128)(2,1)S(1)}, bf16[512,512]{1,0:T(8,128)(2,1)}, u32[]{:S(2)}, u32[]{:S(2)}) %collective-permute-start) | collective-permute-done | bytes 524320 | tf_op jit(solution)/shard_map/ppermute | solution.py:301
  24.9 0.0 all-to-all-done.got_ref
  24.9 0.0 copy-done.1
  24.9 0.0 copy-done.2
  24.9 0.6 shard_map.96
  25.5 0.7 %collective-permute-done.1.dy_ref = bf16[128,512]{1,0:T(8,128)(2,1)S(1)} collective-permute-done((bf16[128,512]{1,0:T(8,128)(2,1)S(1)}, bf16[128,512]{1,0:T(8,128)(2,1)S(1)}, u32[]{:S(2)}, u32[]{:S(2)}) %collective-permute-start.1) | collective-permute-done | bytes 131104 | tf_op jit(solution)/shard_map/ppermute | solution.py:301
  26.2 1.7 %collective-permute-start.8 = (bf16[512,512]{1,0:T(8,128)(2,1)}, bf16[512,512]{1,0:T(8,128)(2,1)S(1)}, u32[]{:S(2)}, u32[]{:S(2)}) collective-permute-start(bf16[512,512]{1,0:T(8,128)(2,1)} %collective-permute-done.y2_hbm), channel_id=1, source_target_pairs={{0,4},{4,0},{8,12},{12,8},{16,20},{20,16},{24,28},{28,24},{1,5},{5... | collective-permute-start | bytes 1572872 | tf_op jit(solution)/shard_map/ppermute | solution.py:301
  27.9 0.0 collective-permute-start.2
  27.9 1.5 %collective-permute-start.3 = (bf16[16,1920]{1,0:T(8,128)(2,1)S(1)}, bf16[16,1920]{1,0:T(8,128)(2,1)S(1)}, u32[]{:S(2)}, u32[]{:S(2)}) collective-permute-start(bf16[16,1920]{1,0:T(8,128)(2,1)S(1)} %get-tuple-element.51.share_ref), channel_id=1, source_target_pairs={{0,2},{1,3},{2,0},{3,1},{4,6},{5,7},{6,4},{7,5},{8,10},{9,11},{10,... | collective-permute-start | bytes 184328 | tf_op jit(solution)/shard_map/ppermute | solution.py:301
  29.4 0.3 collective-permute-start.4
  29.7 0.0 collective-permute-done.2.refs_1_.fac1_ref
  29.7 2.6 %collective-permute-done.3.refs_2_.fac2_ref = bf16[16,1920]{1,0:T(8,128)(2,1)S(1)} collective-permute-done((bf16[16,1920]{1,0:T(8,128)(2,1)S(1)}, bf16[16,1920]{1,0:T(8,128)(2,1)S(1)}, u32[]{:S(2)}, u32[]{:S(2)}) %collective-permute-start.3) | collective-permute-done | bytes 61472 | tf_op jit(solution)/shard_map/ppermute | solution.py:301
  32.3 1.1 %collective-permute-done.4.refs_3_.fac3_ref = bf16[16,1920]{1,0:T(8,128)(2,1)S(1)} collective-permute-done((bf16[16,1920]{1,0:T(8,128)(2,1)S(1)}, bf16[16,1920]{1,0:T(8,128)(2,1)S(1)}, u32[]{:S(2)}, u32[]{:S(2)}) %collective-permute-start.4) | collective-permute-done | bytes 61472 | tf_op jit(solution)/shard_map/ppermute | solution.py:301
  33.4 1.3 %shard_map.97 = (bf16[16,2048]{1,0:T(8,128)(2,1)S(1)}, bf16[16,2048]{1,0:T(8,128)(2,1)S(1)}, bf16[16,2048]{1,0:T(8,128)(2,1)S(1)}, bf16[16,2048]{1,0:T(8,128)(2,1)S(1)}, bf16[128,16]{1,0:T(8,128)(2,1)S(1)}) custom-call(s32[1]{0:T(128)} %bitcast.at_ref, bf16[128,7168]{1,0:T(8,128)(2,1)S(1)} %shard_map.95.x_ref, bf16[128,512]{1,0:T(8,128)(2,1)S(1)} %copy-done, ...), custom_call_target="tpu_custom_call" | custom-call | tf_op jit(solution)/shard_map/pallas_call | solution.py:261
  34.7 0.5 collective-permute-start.5
  35.2 1.5 %collective-permute-start.6 = (bf16[16,2048]{1,0:T(8,128)(2,1)S(1)}, bf16[16,2048]{1,0:T(8,128)(2,1)S(1)}, u32[]{:S(2)}, u32[]{:S(2)}) collective-permute-start(bf16[16,2048]{1,0:T(8,128)(2,1)S(1)} %get-tuple-element.55), channel_id=1, source_target_pairs={{0,2},{1,3},{2,0},{3,1},{4,6},{5,7},{6,4},{7,5},{8,10},{9,11},{10,... | collective-permute-start | bytes 196616 | tf_op jit(solution)/shard_map/ppermute | solution.py:301
  36.7 0.0 collective-permute-start.7
  36.7 0.0 collective-permute-done.5.refs_1_
  36.7 2.8 %collective-permute-done.6.refs_2_.got_ref = bf16[16,2048]{1,0:T(8,128)(2,1)S(1)} collective-permute-done((bf16[16,2048]{1,0:T(8,128)(2,1)S(1)}, bf16[16,2048]{1,0:T(8,128)(2,1)S(1)}, u32[]{:S(2)}, u32[]{:S(2)}) %collective-permute-start.6) | collective-permute-done | bytes 65568 | tf_op jit(solution)/shard_map/ppermute | solution.py:301
  39.5 1.5 %collective-permute-done.7.refs_3_.got_ref = bf16[16,2048]{1,0:T(8,128)(2,1)S(1)} collective-permute-done((bf16[16,2048]{1,0:T(8,128)(2,1)S(1)}, bf16[16,2048]{1,0:T(8,128)(2,1)S(1)}, u32[]{:S(2)}, u32[]{:S(2)}) %collective-permute-start.7) | collective-permute-done | bytes 65568 | tf_op jit(solution)/shard_map/ppermute | solution.py:301
  41.0 1.5 %shard_map.98 = bf16[8,16,1920]{2,1,0:T(8,128)(2,1)} custom-call(s32[1]{0:T(128)} %bitcast.at_ref, s32[1]{0:T(128)} %bitcast.1.me_ref, s32[32]{0:T(128)S(1)} %copy-done.1, s32[40]{0:T(128)S(1)} %copy-done.2, bf16[16,2048]{1,0:T(8,128)(2,1)S(1)} %get-tuple-element.58.refs_0_, bf16[16,2048]{1,0:T(8,128)(2,1)S(1)} %collective-permute-done.5.refs_1_, ...), custom_call_target="tpu_custom_call" | custom-call | tf_op jit(solution)/shard_map/pallas_call | solution.py:261
  42.5 0.0 collective-permute-done.8.x2_hbm
  42.5 0.0 copy-start.3
  42.5 0.1 collective-permute-start.14
  42.6 4.5 %all-to-all-start.1 = ((bf16[8,16,1920]{2,1,0:T(8,128)(2,1)}), bf16[8,16,1920]{2,1,0:T(8,128)(2,1)S(1)}, u32[]{:S(2)}, u32[]{:S(2)}) async-start(bf16[8,16,1920]{2,1,0:T(8,128)(2,1)} %shard_map.98), calls=%async_computation.1 | async-start | bytes 983040 | tf_op jit(solution)/shard_map/all_to_all | solution.py:391
  47.1 0.2 collective-permute-start.12
  47.3 0.3 collective-permute-start.13
  47.6 0.2 collective-permute-start.10
  47.8 1.7 %shard_map.99 = bf16[128,768]{1,0:T(8,128)(2,1)S(1)} custom-call(bf16[1792,512]{1,0:T(8,128)(2,1)} %w0_hbm.1, bf16[128,512]{1,0:T(8,128)(2,1)S(1)} %collective-permute-done.1.dy_ref, bf16[16,1920]{1,0:T(8,128)(2,1)S(1)} %get-tuple-element.51.share_ref, bf16[16,2048]{1,0:T(8,128)(2,1)S(1)} %collective-permute-done.6.refs_2_.got_ref), custom_call_target="tpu_custom_call" | custom-call | tf_op jit(solution)/shard_map/pallas_call | solution.py:261
  49.5 1.0 %collective-permute-start.9 = (bf16[128,768]{1,0:T(8,128)(2,1)S(1)}, bf16[128,768]{1,0:T(8,128)(2,1)S(1)}, u32[]{:S(2)}, u32[]{:S(2)}) collective-permute-start(bf16[128,768]{1,0:T(8,128)(2,1)S(1)} %shard_map.99), channel_id=1, source_target_pairs={{0,2},{1,3},{2,0},{3,1},{4,6},{5,7},{6,4},{7,5},{8,10},{9,11},{10,... | collective-permute-start | bytes 589832 | tf_op jit(solution)/shard_map/ppermute | solution.py:301
  50.5 0.0 collective-permute-done.10.dy_ref
  50.5 1.7 %shard_map.100 = bf16[128,768]{1,0:T(8,128)(2,1)S(1)} custom-call(bf16[1792,512]{1,0:T(8,128)(2,1)} %w0_hbm.1, bf16[128,512]{1,0:T(8,128)(2,1)S(1)} %collective-permute-done.10.dy_ref, bf16[16,1920]{1,0:T(8,128)(2,1)S(1)} %get-tuple-element.52.share_ref, bf16[16,2048]{1,0:T(8,128)(2,1)S(1)} %collective-permute-done.7.refs_3_.got_ref), custom_call_target="tpu_custom_call" | custom-call | tf_op jit(solution)/shard_map/pallas_call | solution.py:261
  52.2 0.0 copy-done.3
  52.2 0.8 %collective-permute-start.11 = (bf16[128,768]{1,0:T(8,128)(2,1)S(1)}, bf16[128,768]{1,0:T(8,128)(2,1)S(1)}, u32[]{:S(2)}, u32[]{:S(2)}) collective-permute-start(bf16[128,768]{1,0:T(8,128)(2,1)S(1)} %shard_map.100), channel_id=1, source_target_pairs={{0,3},{1,2},{2,1},{3,0},{4,7},{5,6},{6,5},{7,4},{8,11},{9,10},{10,... | collective-permute-start | bytes 589832 | tf_op jit(solution)/shard_map/ppermute | solution.py:301
  53.0 0.0 collective-permute-done.12.y3_hbm
  53.0 0.0 collective-permute-done.13.x3_hbm
  53.0 0.0 collective-permute-done.14.w1_hbm
  53.0 7.6 %shard_map.101.in_ref = bf16[128,7168]{1,0:T(8,128)(2,1)} custom-call(s32[1]{0:T(128)} %bitcast.at_ref, s32[1]{0:T(128)S(6)} %and.5.side_ref, bf16[128,16]{1,0:T(8,128)(2,1)S(1)} %get-tuple-element.65.back_ref, bf16[16,1920]{1,0:T(8,128)(2,1)S(1)} %get-tuple-element.49.refs_0_.fac0_ref, bf16[16,1920]{1,0:T(8,128)(2,1)S(1)} %collective-permute-done.2.refs_1_.fac1_ref, ...), custom_call_target="tpu_custom_call" | custom-call | tf_op jit(solution)/shard_map/pallas_call | solution.py:261
  60.6 0.0 collective-permute-done.9.z2_ref
  60.6 0.0 collective-permute-done.11.z3_ref
  60.6 0.8 %shard_map.102 = bf16[128,7168]{1,0:T(8,128)(2,1)} custom-call(s32[1]{0:T(128)} %bitcast.at_ref, bf16[128,768]{1,0:T(8,128)(2,1)S(1)} %collective-permute-done.9.z2_ref, bf16[128,768]{1,0:T(8,128)(2,1)S(1)} %collective-permute-done.11.z3_ref, bf16[128,7168]{1,0:T(8,128)(2,1)} %shard_map.101.in_ref), custom_call_target="tpu_custom_call", output_to_operand_aliasing={{}: (3, {})} | custom-call | tf_op jit(solution)/shard_map/pallas_call | solution.py:261
  61.4 0.1 all-to-all-done.1.got_ref
  61.5 1.6 %shard_map.103 = (f32[5,16,1792]{2,1,0:T(8,128)}, f32[5,16,128]{2,1,0:T(8,128)}) custom-call(s32[8]{0:T(128)S(1)} %get-tuple-element.70.want_ref, s32[5]{0:T(128)S(1)} %get-tuple-element.71.count_ref, bf16[8,16,1920]{2,1,0:T(8,128)(2,1)S(1)} %all-to-all-done.1.got_ref), custom_call_target="tpu_custom_call" | custom-call | tf_op jit(solution)/shard_map/pallas_call | solution.py:261
Async XLA Ops:
  0.6 10.9 %copy-start = (bf16[128,512]{1,0:T(8,128)(2,1)S(1)}, bf16[128,512]{1,0:T(8,128)(2,1)}, u32[]{:S(2)}) copy-start(bf16[128,512]{1,0:T(8,128)(2,1)} %dy_hbm.1) | copy-start | bytes 393220
  2.7 22.2 %all-to-all-start = ((bf16[8,16,1920]{2,1,0:T(8,128)(2,1)}), bf16[8,16,1920]{2,1,0:T(8,128)(2,1)S(1)}, u32[]{:S(2)}, u32[]{:S(2)}) async-start(bf16[8,16,1920]{2,1,0:T(8,128)(2,1)} %get-tuple-element.39), calls=%async_computation | async-start | bytes 983040 | tf_op jit(solution)/shard_map/all_to_all | solution.py:332
  9.9 15.0 %copy-start.1 = (s32[32]{0:T(128)S(1)}, s32[32]{0:T(128)}, u32[]{:S(2)}) copy-start(s32[32]{0:T(128)} %apb_ref.3) | copy-start | bytes 388
  9.9 15.0 %copy-start.2 = (s32[40]{0:T(128)S(1)}, s32[40]{0:T(128)}, u32[]{:S(2)}) copy-start(s32[40]{0:T(128)} %row_ref.3) | copy-start | bytes 484
  10.0 15.0 %collective-permute-start = (bf16[512,512]{1,0:T(8,128)(2,1)S(1)}, bf16[512,512]{1,0:T(8,128)(2,1)}, u32[]{:S(2)}, u32[]{:S(2)}) collective-permute-start(bf16[512,512]{1,0:T(8,128)(2,1)S(1)} %get-tuple-element.40), channel_id=1, source_target_pairs={{0,2},{1,3},{2,0},{3,1},{4,6},{5,7},{6,4},{7,5},{8,10},{9,11},{10,... | collective-permute-start | bytes 1572872 | tf_op jit(solution)/shard_map/ppermute | solution.py:301
  11.5 14.7 %collective-permute-start.1 = (bf16[128,512]{1,0:T(8,128)(2,1)S(1)}, bf16[128,512]{1,0:T(8,128)(2,1)S(1)}, u32[]{:S(2)}, u32[]{:S(2)}) collective-permute-start(bf16[128,512]{1,0:T(8,128)(2,1)S(1)} %copy-done), channel_id=1, source_target_pairs={{0,2},{1,3},{2,0},{3,1},{4,6},{5,7},{6,4},{7,5},{8,10},{9,11},{10,... | collective-permute-start | bytes 393224 | tf_op jit(solution)/shard_map/ppermute | solution.py:301
  26.2 16.3 %collective-permute-start.8 = (bf16[512,512]{1,0:T(8,128)(2,1)}, bf16[512,512]{1,0:T(8,128)(2,1)S(1)}, u32[]{:S(2)}, u32[]{:S(2)}) collective-permute-start(bf16[512,512]{1,0:T(8,128)(2,1)} %collective-permute-done.y2_hbm), channel_id=1, source_target_pairs={{0,4},{4,0},{8,12},{12,8},{16,20},{20,16},{24,28},{28,24},{1,5},{5... | collective-permute-start | bytes 1572872 | tf_op jit(solution)/shard_map/ppermute | solution.py:301
  27.9 1.9 %collective-permute-start.2 = (bf16[16,1920]{1,0:T(8,128)(2,1)S(1)}, bf16[16,1920]{1,0:T(8,128)(2,1)S(1)}, u32[]{:S(2)}, u32[]{:S(2)}) collective-permute-start(bf16[16,1920]{1,0:T(8,128)(2,1)S(1)} %get-tuple-element.50), channel_id=1, source_target_pairs={{0,1},{1,0},{2,3},{3,2},{4,5},{5,4},{6,7},{7,6},{8,9},{9,8},{10,11... | collective-permute-start | bytes 184328 | tf_op jit(solution)/shard_map/ppermute | solution.py:301
  27.9 4.4 %collective-permute-start.3 = (bf16[16,1920]{1,0:T(8,128)(2,1)S(1)}, bf16[16,1920]{1,0:T(8,128)(2,1)S(1)}, u32[]{:S(2)}, u32[]{:S(2)}) collective-permute-start(bf16[16,1920]{1,0:T(8,128)(2,1)S(1)} %get-tuple-element.51.share_ref), channel_id=1, source_target_pairs={{0,2},{1,3},{2,0},{3,1},{4,6},{5,7},{6,4},{7,5},{8,10},{9,11},{10,... | collective-permute-start | bytes 184328 | tf_op jit(solution)/shard_map/ppermute | solution.py:301
  29.4 4.0 %collective-permute-start.4 = (bf16[16,1920]{1,0:T(8,128)(2,1)S(1)}, bf16[16,1920]{1,0:T(8,128)(2,1)S(1)}, u32[]{:S(2)}, u32[]{:S(2)}) collective-permute-start(bf16[16,1920]{1,0:T(8,128)(2,1)S(1)} %get-tuple-element.52.share_ref), channel_id=1, source_target_pairs={{0,3},{1,2},{2,1},{3,0},{4,7},{5,6},{6,5},{7,4},{8,11},{9,10},{10,... | collective-permute-start | bytes 184328 | tf_op jit(solution)/shard_map/ppermute | solution.py:301
  34.7 1.9 %collective-permute-start.5 = (bf16[16,2048]{1,0:T(8,128)(2,1)S(1)}, bf16[16,2048]{1,0:T(8,128)(2,1)S(1)}, u32[]{:S(2)}, u32[]{:S(2)}) collective-permute-start(bf16[16,2048]{1,0:T(8,128)(2,1)S(1)} %get-tuple-element.54), channel_id=1, source_target_pairs={{0,1},{1,0},{2,3},{3,2},{4,5},{5,4},{6,7},{7,6},{8,9},{9,8},{10,11... | collective-permute-start | bytes 196616 | tf_op jit(solution)/shard_map/ppermute | solution.py:301
  35.2 4.3 %collective-permute-start.6 = (bf16[16,2048]{1,0:T(8,128)(2,1)S(1)}, bf16[16,2048]{1,0:T(8,128)(2,1)S(1)}, u32[]{:S(2)}, u32[]{:S(2)}) collective-permute-start(bf16[16,2048]{1,0:T(8,128)(2,1)S(1)} %get-tuple-element.55), channel_id=1, source_target_pairs={{0,2},{1,3},{2,0},{3,1},{4,6},{5,7},{6,4},{7,5},{8,10},{9,11},{10,... | collective-permute-start | bytes 196616 | tf_op jit(solution)/shard_map/ppermute | solution.py:301
  36.7 4.3 %collective-permute-start.7 = (bf16[16,2048]{1,0:T(8,128)(2,1)S(1)}, bf16[16,2048]{1,0:T(8,128)(2,1)S(1)}, u32[]{:S(2)}, u32[]{:S(2)}) collective-permute-start(bf16[16,2048]{1,0:T(8,128)(2,1)S(1)} %get-tuple-element.56), channel_id=1, source_target_pairs={{0,3},{1,2},{2,1},{3,0},{4,7},{5,6},{6,5},{7,4},{8,11},{9,10},{10,... | collective-permute-start | bytes 196616 | tf_op jit(solution)/shard_map/ppermute | solution.py:301
  42.5 9.7 %copy-start.3 = (bf16[512,512]{1,0:T(8,128)(2,1)}, bf16[512,512]{1,0:T(8,128)(2,1)S(1)}, u32[]{:S(2)}) copy-start(bf16[512,512]{1,0:T(8,128)(2,1)S(1)} %collective-permute-done.8.x2_hbm) | copy-start | bytes 1572868
  42.5 10.5 %collective-permute-start.14 = (bf16[1792,512]{1,0:T(8,128)(2,1)}, bf16[1792,512]{1,0:T(8,128)(2,1)}, u32[]{:S(2)}, u32[]{:S(2)}) collective-permute-start(bf16[1792,512]{1,0:T(8,128)(2,1)} %w0_hbm.1), channel_id=1, source_target_pairs={{0,1},{1,0},{2,3},{3,2},{4,5},{5,4},{6,7},{7,6},{8,9},{9,8},{10,11... | collective-permute-start | bytes 5505032 | tf_op jit(solution)/shard_map/ppermute | solution.py:301
  42.6 18.9 %all-to-all-start.1 = ((bf16[8,16,1920]{2,1,0:T(8,128)(2,1)}), bf16[8,16,1920]{2,1,0:T(8,128)(2,1)S(1)}, u32[]{:S(2)}, u32[]{:S(2)}) async-start(bf16[8,16,1920]{2,1,0:T(8,128)(2,1)} %shard_map.98), calls=%async_computation.1 | async-start | bytes 983040 | tf_op jit(solution)/shard_map/all_to_all | solution.py:391
  47.1 5.9 %collective-permute-start.12 = (bf16[512,512]{1,0:T(8,128)(2,1)}, bf16[512,512]{1,0:T(8,128)(2,1)S(1)}, u32[]{:S(2)}, u32[]{:S(2)}) collective-permute-start(bf16[512,512]{1,0:T(8,128)(2,1)} %collective-permute-done.y2_hbm), channel_id=1, source_target_pairs={{0,1},{1,0},{2,3},{3,2},{4,5},{5,4},{6,7},{7,6},{8,9},{9,8},{10,11... | collective-permute-start | bytes 1572872 | tf_op jit(solution)/shard_map/ppermute | solution.py:301
  47.3 5.7 %collective-permute-start.13 = (bf16[512,512]{1,0:T(8,128)(2,1)S(1)}, bf16[512,512]{1,0:T(8,128)(2,1)S(1)}, u32[]{:S(2)}, u32[]{:S(2)}) collective-permute-start(bf16[512,512]{1,0:T(8,128)(2,1)S(1)} %collective-permute-done.8.x2_hbm), channel_id=1, source_target_pairs={{0,1},{1,0},{2,3},{3,2},{4,5},{5,4},{6,7},{7,6},{8,9},{9,8},{10,11... | collective-permute-start | bytes 1572872 | tf_op jit(solution)/shard_map/ppermute | solution.py:301
  47.6 2.9 %collective-permute-start.10 = (bf16[128,512]{1,0:T(8,128)(2,1)S(1)}, bf16[128,512]{1,0:T(8,128)(2,1)S(1)}, u32[]{:S(2)}, u32[]{:S(2)}) collective-permute-start(bf16[128,512]{1,0:T(8,128)(2,1)S(1)} %collective-permute-done.1.dy_ref), channel_id=1, source_target_pairs={{0,1},{1,0},{2,3},{3,2},{4,5},{5,4},{6,7},{7,6},{8,9},{9,8},{10,11... | collective-permute-start | bytes 393224 | tf_op jit(solution)/shard_map/ppermute | solution.py:301
  49.5 11.2 %collective-permute-start.9 = (bf16[128,768]{1,0:T(8,128)(2,1)S(1)}, bf16[128,768]{1,0:T(8,128)(2,1)S(1)}, u32[]{:S(2)}, u32[]{:S(2)}) collective-permute-start(bf16[128,768]{1,0:T(8,128)(2,1)S(1)} %shard_map.99), channel_id=1, source_target_pairs={{0,2},{1,3},{2,0},{3,1},{4,6},{5,7},{6,4},{7,5},{8,10},{9,11},{10,... | collective-permute-start | bytes 589832 | tf_op jit(solution)/shard_map/ppermute | solution.py:301
  52.2 8.4 %collective-permute-start.11 = (bf16[128,768]{1,0:T(8,128)(2,1)S(1)}, bf16[128,768]{1,0:T(8,128)(2,1)S(1)}, u32[]{:S(2)}, u32[]{:S(2)}) collective-permute-start(bf16[128,768]{1,0:T(8,128)(2,1)S(1)} %shard_map.100), channel_id=1, source_target_pairs={{0,3},{1,2},{2,1},{3,0},{4,7},{5,6},{6,5},{7,4},{8,11},{9,10},{10,... | collective-permute-start | bytes 589832 | tf_op jit(solution)/shard_map/ppermute | solution.py:301

commit v8 on v7

--- a/solution.py
+++ b/solution.py
@@ -39,10 +39,16 @@
     return copies
 
 
-def copy_kernel(from_ref, to_ref, sem):
-    copy = pltpu.make_async_copy(from_ref, to_ref, sem)
-    copy.start()
-    copy.wait()
+def early_kernel(x_hbm, w_hbm, dy_hbm, x_ref, own_hbm, w_ref, dy_ref, own_ref, sems):
+    copies = fetch((dy_hbm, w_hbm, x_hbm), (dy_ref, w_ref, x_ref), sems)
+    copies[0].wait()
+    dy_t = turned(dy_ref[...])
+    copies[1].wait()
+    own_ref[...] = dot(w_ref[...], dy_t).T
+    copies[2].wait()
+    out = pltpu.make_async_copy(own_ref, own_hbm, sems.at[3])
+    out.start()
+    out.wait()
 
 
 def pick_kernel(
@@ -194,17 +200,17 @@
 
 
 def input_kernel(
-    at_ref, side_ref, back_ref, fac0_ref, fac1_ref, fac2_ref, fac3_ref, dy_hbm, y2_hbm, y3_hbm, x2_hbm, x3_hbm, w0_hbm, w1_hbm,
-    out_ref, dy_ref, few_ref, w0_ref, w1_ref, buf, fetch_sems, sems,
+    at_ref, side_ref, back_ref, fac0_ref, fac1_ref, fac2_ref, fac3_ref, dy_hbm, y2_hbm, y3_hbm, x2_hbm, x3_hbm, own_hbm, w1_hbm,
+    out_ref, dy_ref, few_ref, own_ref, w1_ref, buf, fetch_sems, sems,
 ):
-    part = w0_ref.shape[0]
+    part = w1_ref.shape[0]
     fac_refs = (fac0_ref, fac1_ref, fac2_ref, fac3_ref)
     taken = few_ref.shape[1]
     side = side_ref[0] * taken
     few = [a.at[pl.ds(0, taken)] for a in (y2_hbm, y3_hbm, x2_hbm, x3_hbm)]
     fetches = fetch(
-        (*few, w0_hbm, w1_hbm, dy_hbm),
-        (*(few_ref.at[i] for i in range(4)), w0_ref, w1_ref, dy_ref),
+        (*few, own_hbm, w1_hbm, dy_hbm),
+        (*(few_ref.at[i] for i in range(4)), own_ref, w1_ref, dy_ref),
         fetch_sems,
     )
     fetches[6].wait()
@@ -216,7 +222,7 @@
             (3, few_ref.at[1], side, taken),
             (2, few_ref.at[2], taken - side, taken),
             (3, few_ref.at[3], taken - side, taken),
-            (0, w0_ref, 0, part),
+            (0, None, 0, part),
             (1, w1_ref, 0, part),
         )
     ):
@@ -224,7 +230,7 @@
         peer = lax.bitwise_xor(at_ref[0], k)
         start = pl.multiple_of(start, LANES)
         buf[i, :, :rows] = (
-            dot(w_ref[...], dy_t).T
+            (dot(w_ref[...], dy_t).T if k else own_ref[...])
             + dot(back_ref[...], fac_refs[k][:, pl.ds(start, rows)])
         ).astype(jnp.bfloat16)
         first = pl.multiple_of(peer * part + start, LANES)
@@ -335,15 +341,21 @@
         y2 = cross(some, 2)
         dy2 = cross(value_cotangent, 2)
         at_hand, _ = lax.optimization_barrier((projection_input, send))
-        at_hand = call(
-            copy_kernel,
-            shaped(tok_rows, width),
-            VMEM,
-            *in_hbm(at_hand),
-            specs=[ANY],
-            scratch=[pltpu.SemaphoreType.DMA],
-        )
-        owned, y2, at_hand = lax.optimization_barrier((owned, y2, at_hand))
+        at_hand, own = call(
+            early_kernel,
+            (shaped(tok_rows, width), shaped(tok_rows, down_part, dtype=jnp.float32)),
+            (VMEM, ANY),
+            *in_hbm(at_hand, value_weight, value_cotangent),
+            specs=[ANY] * 3,
+            vmem=16,
+            scratch=[
+                pltpu.VMEM(value_weight.shape, bf16),
+                pltpu.VMEM(value_cotangent.shape, bf16),
+                pltpu.VMEM((tok_rows, down_part), jnp.float32),
+                pltpu.SemaphoreType.DMA((4,)),
+            ],
+        )
+        owned, y2, at_hand, own = lax.optimization_barrier((owned, y2, at_hand, own))
     else:
         at_hand = projection_input
     share = call(
@@ -356,9 +368,11 @@
         smem=4,
     )
     if by_permute:
-        x2, share, dy2 = lax.optimization_barrier((y2, share, dy2))
+        x2 = y2
         x2 = cross(x2, 1, "dp")
     factors = exchange(share)
+    if by_permute:
+        factors, dy2 = lax.optimization_barrier((factors, dy2))
     *grads, back = call(
         functools.partial(block_kernel, by_permute, down_part, up_part, fsdp_count),
         [shaped(rank, wide + BLOCK)] * fsdp_count + [shaped(BLOCK, rank)],
@@ -424,14 +438,14 @@
             near[1],
             *in_hbm(x2),
             x3,
-            *in_hbm(value_weight, near[0]),
+            *in_hbm(own, near[0]),
             smem=2,
             specs=[VMEM] * 5 + [ANY] * 7,
             vmem=24,
             scratch=[
                 pltpu.VMEM(value_cotangent.shape, bf16),
                 pltpu.VMEM((4, side_rows, value_weight.shape[1]), bf16),
-                pltpu.VMEM(value_weight.shape, bf16),
+                pltpu.VMEM((tok_rows, down_part), jnp.float32),
                 pltpu.VMEM(value_weight.shape, bf16),
                 pltpu.VMEM((6, tok_rows, down_part), bf16),
                 pltpu.SemaphoreType.DMA((7,)),

time: 63.5 us -> 62.2 us (0.980)
  waiting for transfers between devices: 20.1 us -> 16.4 us
  starting transfers between devices: 21.9 us -> 23.8 us
  local copies, waits for them, and re-layouts: 0.02 us -> 0.95 us
    ppermute x15, waiting for transfers between devices: 20 us -> 16.1 us  [cross(): lax.ppermute(array, axis, [(i, i ^ bit) for i in range(lax.axis_size(axis...]
    ppermute x15, starting transfers between devices: 10.1 us -> 12.1 us  [cross(): lax.ppermute(array, axis, [(i, i ^ bit) for i in range(lax.axis_size(axis...]
    unnamed x8 -> x10, local copies, waits for them, and re-layouts: 0.02 us -> 0.95 us
where the time goes in v8:
time: 62.2 us; the launch traced here: 61.6 us
  starting transfers between devices  23.8 us (38%)
  Pallas kernels  19.7 us (32%)
  waiting for transfers between devices  16.4 us (26%)
  local copies, waits for them, and re-layouts  0.95 us (2%)
  between operations  0.77 us (1%)
    pallas_call x10, Pallas kernels, call(): pl.pallas_call(kernel, out_shape=out_shape, in_specs=[SMEM] * smem + (spe...  19.7 us
    ppermute x15, waiting for transfers between devices, cross(): lax.ppermute(array, axis, [(i, i ^ bit) for i in range(lax.axis_size(axis...  16.1 us
    ppermute x15, starting transfers between devices, cross(): lax.ppermute(array, axis, [(i, i ^ bit) for i in range(lax.axis_size(axis...  12.1 us
    all_to_all x1, starting transfers between devices, per_device(): owned = lax.all_to_all(send, 'dp', split_axis=0, concat_axis=0, tiled=True)  7.26 us
    all_to_all x1, starting transfers between devices, per_device(): lax.all_to_all(sums, 'dp', split_axis=0, concat_axis=0, tiled=True)  4.48 us
  transfers between devices with their start and end apart: 17, of which 7 were waited for; matrix products, arithmetic and copies ran while one was open for 0% of the time, Pallas kernels for 26%

profile of v8, /device:TPU:0, one launch (start us, length us, event | category | flops | bytes accessed | tf_op | source)
XLA Modules:
  0.0 61.6 jit_solution(4109775904375993994)
XLA Ops:
  0.6 2.0 %shard_map.94 = (bf16[8,16,1920]{2,1,0:T(8,128)(2,1)}, s32[8]{0:T(128)S(1)}, s32[5]{0:T(128)S(1)}, bf16[512,512]{1,0:T(8,128)(2,1)S(1)}) custom-call(s32[1]{0:T(128)} %bitcast.1.me_ref, s32[32]{0:T(128)} %apb_ref.3, s32[40]{0:T(128)} %row_ref.3, bf16[5,16,1792]{2,1,0:T(8,128)(2,1)} %down_hbm.1, bf16[5,16,128]{2,1,0:T(8,128)(2,1)} %up_hbm.1, ...), custom_call_target="tpu_custom_call" | custom-call | tf_op jit(solution)/shard_map/pallas_call | solution.py:267
  2.6 7.3 %all-to-all-start = ((bf16[8,16,1920]{2,1,0:T(8,128)(2,1)}), bf16[8,16,1920]{2,1,0:T(8,128)(2,1)S(1)}, u32[]{:S(2)}, u32[]{:S(2)}) async-start(bf16[8,16,1920]{2,1,0:T(8,128)(2,1)} %get-tuple-element.41), calls=%async_computation | async-start | bytes 983040 | tf_op jit(solution)/shard_map/all_to_all | solution.py:338
  9.9 0.0 copy-start
  9.9 0.0 copy-start.2
  9.9 0.0 copy-start.3
  9.9 1.6 %collective-permute-start = (bf16[512,512]{1,0:T(8,128)(2,1)S(1)}, bf16[512,512]{1,0:T(8,128)(2,1)S(1)}, u32[]{:S(2)}, u32[]{:S(2)}) collective-permute-start(bf16[512,512]{1,0:T(8,128)(2,1)S(1)} %get-tuple-element.42), channel_id=1, source_target_pairs={{0,2},{1,3},{2,0},{3,1},{4,6},{5,7},{6,4},{7,5},{8,10},{9,11},{10,... | collective-permute-start | bytes 1572872 | tf_op jit(solution)/shard_map/ppermute | solution.py:307
  11.5 2.5 %shard_map.95 = (bf16[128,7168]{1,0:T(8,128)(2,1)S(1)}, f32[128,1792]{1,0:T(8,128)S(1)}) custom-call(bf16[128,7168]{1,0:T(8,128)(2,1)} %x_hbm, bf16[1792,512]{1,0:T(8,128)(2,1)} %w_hbm.7, bf16[128,512]{1,0:T(8,128)(2,1)} %dy_hbm.3), custom_call_target="tpu_custom_call" | custom-call | tf_op jit(solution)/shard_map/pallas_call | solution.py:267
  14.1 0.0 copy-start.1
  14.1 0.9 %copy-done.1 = f32[128,1792]{1,0:T(8,128)} copy-done((f32[128,1792]{1,0:T(8,128)}, f32[128,1792]{1,0:T(8,128)S(1)}, u32[]{:S(2)}) %copy-start.1) | copy-done | bytes 917528
  15.0 8.4 %collective-permute-done.y2_hbm = bf16[512,512]{1,0:T(8,128)(2,1)S(1)} collective-permute-done((bf16[512,512]{1,0:T(8,128)(2,1)S(1)}, bf16[512,512]{1,0:T(8,128)(2,1)S(1)}, u32[]{:S(2)}, u32[]{:S(2)}) %collective-permute-start) | collective-permute-done | bytes 524320 | tf_op jit(solution)/shard_map/ppermute | solution.py:307
  23.4 0.0 copy-start.4
  23.4 0.3 all-to-all-done.got_ref
  23.7 1.5 %collective-permute-start.8 = (bf16[512,512]{1,0:T(8,128)(2,1)S(1)}, bf16[512,512]{1,0:T(8,128)(2,1)}, u32[]{:S(2)}, u32[]{:S(2)}) collective-permute-start(bf16[512,512]{1,0:T(8,128)(2,1)S(1)} %collective-permute-done.y2_hbm), channel_id=1, source_target_pairs={{0,4},{4,0},{8,12},{12,8},{16,20},{20,16},{24,28},{28,24},{1,5},{5... | collective-permute-start | bytes 1572872 | tf_op jit(solution)/shard_map/ppermute | solution.py:307
  25.1 0.0 copy-done
  25.1 1.5 %collective-permute-start.4 = (bf16[128,512]{1,0:T(8,128)(2,1)S(1)}, bf16[128,512]{1,0:T(8,128)(2,1)S(1)}, u32[]{:S(2)}, u32[]{:S(2)}) collective-permute-start(bf16[128,512]{1,0:T(8,128)(2,1)S(1)} %copy-done), channel_id=1, source_target_pairs={{0,2},{1,3},{2,0},{3,1},{4,6},{5,7},{6,4},{7,5},{8,10},{9,11},{10,... | collective-permute-start | bytes 393224 | tf_op jit(solution)/shard_map/ppermute | solution.py:307
  26.7 0.0 copy-done.2
  26.7 0.0 copy-done.3
  26.7 0.6 shard_map.96
  27.3 0.6 collective-permute-start.2
  27.8 0.0 collective-permute-start.3
  27.8 1.6 %collective-permute-start.1 = (bf16[16,1920]{1,0:T(8,128)(2,1)S(1)}, bf16[16,1920]{1,0:T(8,128)(2,1)S(1)}, u32[]{:S(2)}, u32[]{:S(2)}) collective-permute-start(bf16[16,1920]{1,0:T(8,128)(2,1)S(1)} %get-tuple-element.49), channel_id=1, source_target_pairs={{0,1},{1,0},{2,3},{3,2},{4,5},{5,4},{6,7},{7,6},{8,9},{9,8},{10,11... | collective-permute-start | bytes 184328 | tf_op jit(solution)/shard_map/ppermute | solution.py:307
  29.5 1.0 %collective-permute-done.4.dy_ref = bf16[128,512]{1,0:T(8,128)(2,1)S(1)} collective-permute-done((bf16[128,512]{1,0:T(8,128)(2,1)S(1)}, bf16[128,512]{1,0:T(8,128)(2,1)S(1)}, u32[]{:S(2)}, u32[]{:S(2)}) %collective-permute-start.4) | collective-permute-done | bytes 131104 | tf_op jit(solution)/shard_map/ppermute | solution.py:307
  30.5 1.7 %collective-permute-done.2.refs_2_.fac2_ref = bf16[16,1920]{1,0:T(8,128)(2,1)S(1)} collective-permute-done((bf16[16,1920]{1,0:T(8,128)(2,1)S(1)}, bf16[16,1920]{1,0:T(8,128)(2,1)S(1)}, u32[]{:S(2)}, u32[]{:S(2)}) %collective-permute-start.2) | collective-permute-done | bytes 61472 | tf_op jit(solution)/shard_map/ppermute | solution.py:307
  32.1 0.0 collective-permute-done.3.refs_3_.fac3_ref
  32.1 0.0 collective-permute-done.1.refs_1_.fac1_ref
  32.1 1.3 %shard_map.97 = (bf16[16,2048]{1,0:T(8,128)(2,1)S(1)}, bf16[16,2048]{1,0:T(8,128)(2,1)S(1)}, bf16[16,2048]{1,0:T(8,128)(2,1)S(1)}, bf16[16,2048]{1,0:T(8,128)(2,1)S(1)}, bf16[128,16]{1,0:T(8,128)(2,1)S(1)}) custom-call(s32[1]{0:T(128)} %bitcast.at_ref, bf16[128,7168]{1,0:T(8,128)(2,1)S(1)} %get-tuple-element.46.x_ref, bf16[128,512]{1,0:T(8,128)(2,1)S(1)} %copy-done, ...), custom_call_target="tpu_custom_call" | custom-call | tf_op jit(solution)/shard_map/pallas_call | solution.py:267
  33.5 0.9 %collective-permute-start.5 = (bf16[16,2048]{1,0:T(8,128)(2,1)S(1)}, bf16[16,2048]{1,0:T(8,128)(2,1)S(1)}, u32[]{:S(2)}, u32[]{:S(2)}) collective-permute-start(bf16[16,2048]{1,0:T(8,128)(2,1)S(1)} %get-tuple-element.57), channel_id=1, source_target_pairs={{0,1},{1,0},{2,3},{3,2},{4,5},{5,4},{6,7},{7,6},{8,9},{9,8},{10,11... | collective-permute-start | bytes 196616 | tf_op jit(solution)/shard_map/ppermute | solution.py:307
  34.4 0.7 %collective-permute-start.6 = (bf16[16,2048]{1,0:T(8,128)(2,1)S(1)}, bf16[16,2048]{1,0:T(8,128)(2,1)S(1)}, u32[]{:S(2)}, u32[]{:S(2)}) collective-permute-start(bf16[16,2048]{1,0:T(8,128)(2,1)S(1)} %get-tuple-element.58), channel_id=1, source_target_pairs={{0,2},{1,3},{2,0},{3,1},{4,6},{5,7},{6,4},{7,5},{8,10},{9,11},{10,... | collective-permute-start | bytes 196616 | tf_op jit(solution)/shard_map/ppermute | solution.py:307
  35.1 0.7 %collective-permute-start.7 = (bf16[16,2048]{1,0:T(8,128)(2,1)S(1)}, bf16[16,2048]{1,0:T(8,128)(2,1)S(1)}, u32[]{:S(2)}, u32[]{:S(2)}) collective-permute-start(bf16[16,2048]{1,0:T(8,128)(2,1)S(1)} %get-tuple-element.59), channel_id=1, source_target_pairs={{0,3},{1,2},{2,1},{3,0},{4,7},{5,6},{6,5},{7,4},{8,11},{9,10},{10,... | collective-permute-start | bytes 196616 | tf_op jit(solution)/shard_map/ppermute | solution.py:307
  35.8 0.0 collective-permute-done.5.refs_1_
  35.8 3.4 %collective-permute-done.6.refs_2_.got_ref = bf16[16,2048]{1,0:T(8,128)(2,1)S(1)} collective-permute-done((bf16[16,2048]{1,0:T(8,128)(2,1)S(1)}, bf16[16,2048]{1,0:T(8,128)(2,1)S(1)}, u32[]{:S(2)}, u32[]{:S(2)}) %collective-permute-start.6) | collective-permute-done | bytes 65568 | tf_op jit(solution)/shard_map/ppermute | solution.py:307
  39.2 0.3 collective-permute-done.7.refs_3_.got_ref
  39.5 1.5 %shard_map.98 = bf16[8,16,1920]{2,1,0:T(8,128)(2,1)} custom-call(s32[1]{0:T(128)} %bitcast.at_ref, s32[1]{0:T(128)} %bitcast.1.me_ref, s32[32]{0:T(128)S(1)} %copy-done.2, s32[40]{0:T(128)S(1)} %copy-done.3, bf16[16,2048]{1,0:T(8,128)(2,1)S(1)} %get-tuple-element.61.refs_0_, bf16[16,2048]{1,0:T(8,128)(2,1)S(1)} %collective-permute-done.5.refs_1_, ...), custom_call_target="tpu_custom_call" | custom-call | tf_op jit(solution)/shard_map/pallas_call | solution.py:267
  41.0 0.0 collective-permute-done.8.x2_hbm
  41.0 0.4 collective-permute-start.14
  41.4 4.5 %all-to-all-start.1 = ((bf16[8,16,1920]{2,1,0:T(8,128)(2,1)}), bf16[8,16,1920]{2,1,0:T(8,128)(2,1)S(1)}, u32[]{:S(2)}, u32[]{:S(2)}) async-start(bf16[8,16,1920]{2,1,0:T(8,128)(2,1)} %shard_map.98), calls=%async_computation.1 | async-start | bytes 983040 | tf_op jit(solution)/shard_map/all_to_all | solution.py:405
  45.9 0.0 copy-done.4
  45.9 0.1 collective-permute-start.12
  45.9 0.5 collective-permute-start.13
  46.4 0.1 collective-permute-start.10
  46.5 1.7 %shard_map.99 = bf16[128,768]{1,0:T(8,128)(2,1)S(1)} custom-call(bf16[1792,512]{1,0:T(8,128)(2,1)} %w_hbm.7, bf16[128,512]{1,0:T(8,128)(2,1)S(1)} %collective-permute-done.4.dy_ref, bf16[16,1920]{1,0:T(8,128)(2,1)S(1)} %get-tuple-element.50.share_ref, bf16[16,2048]{1,0:T(8,128)(2,1)S(1)} %collective-permute-done.6.refs_2_.got_ref), custom_call_target="tpu_custom_call" | custom-call | tf_op jit(solution)/shard_map/pallas_call | solution.py:267
  48.2 1.2 %collective-permute-start.9 = (bf16[128,768]{1,0:T(8,128)(2,1)S(1)}, bf16[128,768]{1,0:T(8,128)(2,1)S(1)}, u32[]{:S(2)}, u32[]{:S(2)}) collective-permute-start(bf16[128,768]{1,0:T(8,128)(2,1)S(1)} %shard_map.99), channel_id=1, source_target_pairs={{0,2},{1,3},{2,0},{3,1},{4,6},{5,7},{6,4},{7,5},{8,10},{9,11},{10,... | collective-permute-start | bytes 589832 | tf_op jit(solution)/shard_map/ppermute | solution.py:307
  49.4 0.0 collective-permute-done.10.dy_ref
  49.4 1.7 %shard_map.100 = bf16[128,768]{1,0:T(8,128)(2,1)S(1)} custom-call(bf16[1792,512]{1,0:T(8,128)(2,1)} %w_hbm.7, bf16[128,512]{1,0:T(8,128)(2,1)S(1)} %collective-permute-done.10.dy_ref, bf16[16,1920]{1,0:T(8,128)(2,1)S(1)} %get-tuple-element.51.share_ref, bf16[16,2048]{1,0:T(8,128)(2,1)S(1)} %collective-permute-done.7.refs_3_.got_ref), custom_call_target="tpu_custom_call" | custom-call | tf_op jit(solution)/shard_map/pallas_call | solution.py:267
  51.0 0.8 %collective-permute-start.11 = (bf16[128,768]{1,0:T(8,128)(2,1)S(1)}, bf16[128,768]{1,0:T(8,128)(2,1)S(1)}, u32[]{:S(2)}, u32[]{:S(2)}) collective-permute-start(bf16[128,768]{1,0:T(8,128)(2,1)S(1)} %shard_map.100), channel_id=1, source_target_pairs={{0,3},{1,2},{2,1},{3,0},{4,7},{5,6},{6,5},{7,4},{8,11},{9,10},{10,... | collective-permute-start | bytes 589832 | tf_op jit(solution)/shard_map/ppermute | solution.py:307
  51.8 0.0 collective-permute-done.12.y3_hbm
  51.8 0.0 collective-permute-done.13.x3_hbm
  51.8 0.0 collective-permute-done.14.w1_hbm
  51.8 6.1 %shard_map.101.in_ref = bf16[128,7168]{1,0:T(8,128)(2,1)} custom-call(s32[1]{0:T(128)} %bitcast.at_ref, s32[1]{0:T(128)S(6)} %and.5.side_ref, bf16[128,16]{1,0:T(8,128)(2,1)S(1)} %get-tuple-element.68.back_ref, bf16[16,1920]{1,0:T(8,128)(2,1)S(1)} %get-tuple-element.52.refs_0_.fac0_ref, bf16[16,1920]{1,0:T(8,128)(2,1)S(1)} %collective-permute-done.1.refs_1_.fac1_ref, ...), custom_call_target="tpu_custom_call" | custom-call | tf_op jit(solution)/shard_map/pallas_call | solution.py:267
  58.0 0.0 collective-permute-done.9.z2_ref
  58.0 1.3 %collective-permute-done.11.z3_ref = bf16[128,768]{1,0:T(8,128)(2,1)S(1)} collective-permute-done((bf16[128,768]{1,0:T(8,128)(2,1)S(1)}, bf16[128,768]{1,0:T(8,128)(2,1)S(1)}, u32[]{:S(2)}, u32[]{:S(2)}) %collective-permute-start.11) | collective-permute-done | bytes 196640 | tf_op jit(solution)/shard_map/ppermute | solution.py:307
  59.3 0.8 %shard_map.102 = bf16[128,7168]{1,0:T(8,128)(2,1)} custom-call(s32[1]{0:T(128)} %bitcast.at_ref, bf16[128,768]{1,0:T(8,128)(2,1)S(1)} %collective-permute-done.9.z2_ref, bf16[128,768]{1,0:T(8,128)(2,1)S(1)} %collective-permute-done.11.z3_ref, bf16[128,7168]{1,0:T(8,128)(2,1)} %shard_map.101.in_ref), custom_call_target="tpu_custom_call", output_to_operand_aliasing={{}: (3, {})} | custom-call | tf_op jit(solution)/shard_map/pallas_call | solution.py:267
  60.0 0.0 all-to-all-done.1.got_ref
  60.1 1.6 %shard_map.103 = (f32[5,16,1792]{2,1,0:T(8,128)}, f32[5,16,128]{2,1,0:T(8,128)}) custom-call(s32[8]{0:T(128)S(1)} %get-tuple-element.74.want_ref, s32[5]{0:T(128)S(1)} %get-tuple-element.75.count_ref, bf16[8,16,1920]{2,1,0:T(8,128)(2,1)S(1)} %all-to-all-done.1.got_ref), custom_call_target="tpu_custom_call" | custom-call | tf_op jit(solution)/shard_map/pallas_call | solution.py:267
Async XLA Ops:
  2.6 21.0 %all-to-all-start = ((bf16[8,16,1920]{2,1,0:T(8,128)(2,1)}), bf16[8,16,1920]{2,1,0:T(8,128)(2,1)S(1)}, u32[]{:S(2)}, u32[]{:S(2)}) async-start(bf16[8,16,1920]{2,1,0:T(8,128)(2,1)} %get-tuple-element.41), calls=%async_computation | async-start | bytes 983040 | tf_op jit(solution)/shard_map/all_to_all | solution.py:338
  9.9 15.3 %copy-start = (bf16[128,512]{1,0:T(8,128)(2,1)S(1)}, bf16[128,512]{1,0:T(8,128)(2,1)}, u32[]{:S(2)}) copy-start(bf16[128,512]{1,0:T(8,128)(2,1)} %dy_hbm.3) | copy-start | bytes 393220
  9.9 16.8 %copy-start.2 = (s32[32]{0:T(128)S(1)}, s32[32]{0:T(128)}, u32[]{:S(2)}) copy-start(s32[32]{0:T(128)} %apb_ref.3) | copy-start | bytes 388
  9.9 16.8 %copy-start.3 = (s32[40]{0:T(128)S(1)}, s32[40]{0:T(128)}, u32[]{:S(2)}) copy-start(s32[40]{0:T(128)} %row_ref.3) | copy-start | bytes 484
  9.9 13.4 %collective-permute-start = (bf16[512,512]{1,0:T(8,128)(2,1)S(1)}, bf16[512,512]{1,0:T(8,128)(2,1)S(1)}, u32[]{:S(2)}, u32[]{:S(2)}) collective-permute-start(bf16[512,512]{1,0:T(8,128)(2,1)S(1)} %get-tuple-element.42), channel_id=1, source_target_pairs={{0,2},{1,3},{2,0},{3,1},{4,6},{5,7},{6,4},{7,5},{8,10},{9,11},{10,... | collective-permute-start | bytes 1572872 | tf_op jit(solution)/shard_map/ppermute | solution.py:307
  14.1 0.9 %copy-start.1 = (f32[128,1792]{1,0:T(8,128)}, f32[128,1792]{1,0:T(8,128)S(1)}, u32[]{:S(2)}) copy-start(f32[128,1792]{1,0:T(8,128)S(1)} %get-tuple-element.71.own_hbm) | copy-start | bytes 2752516
  23.4 22.5 %copy-start.4 = (bf16[512,512]{1,0:T(8,128)(2,1)}, bf16[512,512]{1,0:T(8,128)(2,1)S(1)}, u32[]{:S(2)}) copy-start(bf16[512,512]{1,0:T(8,128)(2,1)S(1)} %collective-permute-done.y2_hbm) | copy-start | bytes 1572868
  23.7 17.3 %collective-permute-start.8 = (bf16[512,512]{1,0:T(8,128)(2,1)S(1)}, bf16[512,512]{1,0:T(8,128)(2,1)}, u32[]{:S(2)}, u32[]{:S(2)}) collective-permute-start(bf16[512,512]{1,0:T(8,128)(2,1)S(1)} %collective-permute-done.y2_hbm), channel_id=1, source_target_pairs={{0,4},{4,0},{8,12},{12,8},{16,20},{20,16},{24,28},{28,24},{1,5},{5... | collective-permute-start | bytes 1572872 | tf_op jit(solution)/shard_map/ppermute | solution.py:307
  25.1 5.3 %collective-permute-start.4 = (bf16[128,512]{1,0:T(8,128)(2,1)S(1)}, bf16[128,512]{1,0:T(8,128)(2,1)S(1)}, u32[]{:S(2)}, u32[]{:S(2)}) collective-permute-start(bf16[128,512]{1,0:T(8,128)(2,1)S(1)} %copy-done), channel_id=1, source_target_pairs={{0,2},{1,3},{2,0},{3,1},{4,6},{5,7},{6,4},{7,5},{8,10},{9,11},{10,... | collective-permute-start | bytes 393224 | tf_op jit(solution)/shard_map/ppermute | solution.py:307
  27.3 4.9 %collective-permute-start.2 = (bf16[16,1920]{1,0:T(8,128)(2,1)S(1)}, bf16[16,1920]{1,0:T(8,128)(2,1)S(1)}, u32[]{:S(2)}, u32[]{:S(2)}) collective-permute-start(bf16[16,1920]{1,0:T(8,128)(2,1)S(1)} %get-tuple-element.50.share_ref), channel_id=1, source_target_pairs={{0,2},{1,3},{2,0},{3,1},{4,6},{5,7},{6,4},{7,5},{8,10},{9,11},{10,... | collective-permute-start | bytes 184328 | tf_op jit(solution)/shard_map/ppermute | solution.py:307
  27.8 4.3 %collective-permute-start.3 = (bf16[16,1920]{1,0:T(8,128)(2,1)S(1)}, bf16[16,1920]{1,0:T(8,128)(2,1)S(1)}, u32[]{:S(2)}, u32[]{:S(2)}) collective-permute-start(bf16[16,1920]{1,0:T(8,128)(2,1)S(1)} %get-tuple-element.51.share_ref), channel_id=1, source_target_pairs={{0,3},{1,2},{2,1},{3,0},{4,7},{5,6},{6,5},{7,4},{8,11},{9,10},{10,... | collective-permute-start | bytes 184328 | tf_op jit(solution)/shard_map/ppermute | solution.py:307
  27.8 4.3 %collective-permute-start.1 = (bf16[16,1920]{1,0:T(8,128)(2,1)S(1)}, bf16[16,1920]{1,0:T(8,128)(2,1)S(1)}, u32[]{:S(2)}, u32[]{:S(2)}) collective-permute-start(bf16[16,1920]{1,0:T(8,128)(2,1)S(1)} %get-tuple-element.49), channel_id=1, source_target_pairs={{0,1},{1,0},{2,3},{3,2},{4,5},{5,4},{6,7},{7,6},{8,9},{9,8},{10,11... | collective-permute-start | bytes 184328 | tf_op jit(solution)/shard_map/ppermute | solution.py:307
  33.5 2.3 %collective-permute-start.5 = (bf16[16,2048]{1,0:T(8,128)(2,1)S(1)}, bf16[16,2048]{1,0:T(8,128)(2,1)S(1)}, u32[]{:S(2)}, u32[]{:S(2)}) collective-permute-start(bf16[16,2048]{1,0:T(8,128)(2,1)S(1)} %get-tuple-element.57), channel_id=1, source_target_pairs={{0,1},{1,0},{2,3},{3,2},{4,5},{5,4},{6,7},{7,6},{8,9},{9,8},{10,11... | collective-permute-start | bytes 196616 | tf_op jit(solution)/shard_map/ppermute | solution.py:307
  34.4 4.8 %collective-permute-start.6 = (bf16[16,2048]{1,0:T(8,128)(2,1)S(1)}, bf16[16,2048]{1,0:T(8,128)(2,1)S(1)}, u32[]{:S(2)}, u32[]{:S(2)}) collective-permute-start(bf16[16,2048]{1,0:T(8,128)(2,1)S(1)} %get-tuple-element.58), channel_id=1, source_target_pairs={{0,2},{1,3},{2,0},{3,1},{4,6},{5,7},{6,4},{7,5},{8,10},{9,11},{10,... | collective-permute-start | bytes 196616 | tf_op jit(solution)/shard_map/ppermute | solution.py:307
  35.1 4.4 %collective-permute-start.7 = (bf16[16,2048]{1,0:T(8,128)(2,1)S(1)}, bf16[16,2048]{1,0:T(8,128)(2,1)S(1)}, u32[]{:S(2)}, u32[]{:S(2)}) collective-permute-start(bf16[16,2048]{1,0:T(8,128)(2,1)S(1)} %get-tuple-element.59), channel_id=1, source_target_pairs={{0,3},{1,2},{2,1},{3,0},{4,7},{5,6},{6,5},{7,4},{8,11},{9,10},{10,... | collective-permute-start | bytes 196616 | tf_op jit(solution)/shard_map/ppermute | solution.py:307
  41.0 10.8 %collective-permute-start.14 = (bf16[1792,512]{1,0:T(8,128)(2,1)}, bf16[1792,512]{1,0:T(8,128)(2,1)}, u32[]{:S(2)}, u32[]{:S(2)}) collective-permute-start(bf16[1792,512]{1,0:T(8,128)(2,1)} %w_hbm.7), channel_id=1, source_target_pairs={{0,1},{1,0},{2,3},{3,2},{4,5},{5,4},{6,7},{7,6},{8,9},{9,8},{10,11... | collective-permute-start | bytes 5505032 | tf_op jit(solution)/shard_map/ppermute | solution.py:307
  41.4 18.7 %all-to-all-start.1 = ((bf16[8,16,1920]{2,1,0:T(8,128)(2,1)}), bf16[8,16,1920]{2,1,0:T(8,128)(2,1)S(1)}, u32[]{:S(2)}, u32[]{:S(2)}) async-start(bf16[8,16,1920]{2,1,0:T(8,128)(2,1)} %shard_map.98), calls=%async_computation.1 | async-start | bytes 983040 | tf_op jit(solution)/shard_map/all_to_all | solution.py:405
  45.9 6.0 %collective-permute-start.12 = (bf16[512,512]{1,0:T(8,128)(2,1)S(1)}, bf16[512,512]{1,0:T(8,128)(2,1)S(1)}, u32[]{:S(2)}, u32[]{:S(2)}) collective-permute-start(bf16[512,512]{1,0:T(8,128)(2,1)S(1)} %collective-permute-done.y2_hbm), channel_id=1, source_target_pairs={{0,1},{1,0},{2,3},{3,2},{4,5},{5,4},{6,7},{7,6},{8,9},{9,8},{10,11... | collective-permute-start | bytes 1572872 | tf_op jit(solution)/shard_map/ppermute | solution.py:307
  45.9 5.9 %collective-permute-start.13 = (bf16[512,512]{1,0:T(8,128)(2,1)}, bf16[512,512]{1,0:T(8,128)(2,1)S(1)}, u32[]{:S(2)}, u32[]{:S(2)}) collective-permute-start(bf16[512,512]{1,0:T(8,128)(2,1)} %collective-permute-done.8.x2_hbm), channel_id=1, source_target_pairs={{0,1},{1,0},{2,3},{3,2},{4,5},{5,4},{6,7},{7,6},{8,9},{9,8},{10,11... | collective-permute-start | bytes 1572872 | tf_op jit(solution)/shard_map/ppermute | solution.py:307
  46.4 2.9 %collective-permute-start.10 = (bf16[128,512]{1,0:T(8,128)(2,1)S(1)}, bf16[128,512]{1,0:T(8,128)(2,1)S(1)}, u32[]{:S(2)}, u32[]{:S(2)}) collective-permute-start(bf16[128,512]{1,0:T(8,128)(2,1)S(1)} %collective-permute-done.4.dy_ref), channel_id=1, source_target_pairs={{0,1},{1,0},{2,3},{3,2},{4,5},{5,4},{6,7},{7,6},{8,9},{9,8},{10,11... | collective-permute-start | bytes 393224 | tf_op jit(solution)/shard_map/ppermute | solution.py:307
  48.2 9.8 %collective-permute-start.9 = (bf16[128,768]{1,0:T(8,128)(2,1)S(1)}, bf16[128,768]{1,0:T(8,128)(2,1)S(1)}, u32[]{:S(2)}, u32[]{:S(2)}) collective-permute-start(bf16[128,768]{1,0:T(8,128)(2,1)S(1)} %shard_map.99), channel_id=1, source_target_pairs={{0,2},{1,3},{2,0},{3,1},{4,6},{5,7},{6,4},{7,5},{8,10},{9,11},{10,... | collective-permute-start | bytes 589832 | tf_op jit(solution)/shard_map/ppermute | solution.py:307
  51.0 8.2 %collective-permute-start.11 = (bf16[128,768]{1,0:T(8,128)(2,1)S(1)}, bf16[128,768]{1,0:T(8,128)(2,1)S(1)}, u32[]{:S(2)}, u32[]{:S(2)}) collective-permute-start(bf16[128,768]{1,0:T(8,128)(2,1)S(1)} %shard_map.100), channel_id=1, source_target_pairs={{0,3},{1,2},{2,1},{3,0},{4,7},{5,6},{6,5},{7,4},{8,11},{9,10},{10,... | collective-permute-start | bytes 589832 | tf_op jit(solution)/shard_map/ppermute | solution.py:307

commit v9 on v8

--- a/solution.py
+++ b/solution.py
@@ -79,18 +79,17 @@
     copies[1].wait()
 
     def group(g, carry):
-        want_ref[g] = 0
+        want = jnp.int32(0)
         for j in range(group_blocks):
             local = row_ref[apb_ref[g * group_blocks + j]] - first
-
-            @pl.when((local >= 0) & (local < slots))
-            def _():
-                want_ref[g] = local
-                count_ref[local] = count_ref[local] + 1
-
+            mine = (local >= 0) & (local < slots)
+            want = jnp.where(mine, local, want)
+            slot = jnp.where(mine, local, 0)
+            count_ref[slot] = count_ref[slot] + mine.astype(jnp.int32)
+        want_ref[g] = want
         return carry
 
-    lax.fori_loop(0, groups, group, 0)
+    lax.fori_loop(0, groups, group, 0, unroll=4)
     copies[2].wait()
     copies[3].wait()
 
@@ -243,7 +242,9 @@
         copy.wait()
 
 
-def place_kernel(at_ref, z2_ref, z3_ref, in_ref, out_ref, sems):
+def last_kernel(
+    want_ref, count_ref, at_ref, got_ref, z2_ref, z3_ref, in_ref, down_ref, up_ref, out_ref, sems
+):
     rows = z2_ref.shape[1]
     part = out_ref.shape[1] // 4
     copies = []
@@ -253,6 +254,7 @@
         copy = pltpu.make_async_copy(z_ref, out_ref.at[:, pl.ds(first, rows)], sems.at[i])
         copy.start()
         copies.append(copy)
+    total_kernel(want_ref, count_ref, got_ref, down_ref, up_ref)
     for copy in copies:
         copy.wait()
 
@@ -452,33 +454,39 @@
                 pltpu.SemaphoreType.DMA((6,)),
             ],
         )
-        grad_input = call(
-            place_kernel,
-            shaped(tok_rows, width),
-            pl.BlockSpec(memory_space=pl.ANY),
+        grad_down, grad_up, grad_input = call(
+            last_kernel,
+            (
+                shaped(slots, rank, down_part, dtype=jnp.float32),
+                shaped(slots, rank, up_part, dtype=jnp.float32),
+                shaped(tok_rows, width),
+            ),
+            (VMEM, VMEM, ANY),
+            want,
+            count,
             at,
+            arrived,
             z2,
             z3,
             grad_input,
-            smem=1,
-            specs=[VMEM, VMEM, pl.BlockSpec(memory_space=pl.ANY)],
+            smem=3,
+            specs=[VMEM, VMEM, VMEM, ANY],
             scratch=[pltpu.SemaphoreType.DMA((2,))],
-            aliases={3: 0},
-        )
-        arrived, grad_input = lax.optimization_barrier((arrived, grad_input))
-    grad_down, grad_up = call(
-        total_kernel,
-        (
-            shaped(slots, rank, down_part, dtype=jnp.float32),
-            shaped(slots, rank, up_part, dtype=jnp.float32),
-        ),
-        (VMEM, VMEM),
-        want,
-        count,
-        arrived,
-        smem=2,
-    )
-    if not by_permute:
+            aliases={6: 2},
+        )
+    else:
+        grad_down, grad_up = call(
+            total_kernel,
+            (
+                shaped(slots, rank, down_part, dtype=jnp.float32),
+                shaped(slots, rank, up_part, dtype=jnp.float32),
+            ),
+            (VMEM, VMEM),
+            want,
+            count,
+            arrived,
+            smem=2,
+        )
         weight = lax.all_gather(value_weight, "fsdp", axis=0, tiled=True)
         adapter_term = jnp.concatenate(
             [

time: 62.2 us -> 62.5 us (level)
    all_to_all x1, waiting for transfers between devices: 0.01 us -> 0.66 us  [per_device(): lax.all_to_all(sums, 'dp', split_axis=0, concat_axis=0, tiled=True)]
    pallas_call x10 -> x9, Pallas kernels: 19.7 us -> 19.5 us  [call(): pl.pallas_call(kernel, out_shape=out_shape, in_specs=[SMEM] * smem + (spe...]
  transfers between devices with their start and end apart: 17 -> 17, of which waited for: 7 -> 8; matrix products, arithmetic and copies ran while one was open for 0% -> 0% of each run, Pallas kernels for 26% -> 25%
where the time goes in v9:
time: 62.5 us; the launch traced here: 62.1 us
  starting transfers between devices  23.9 us (38%)
  Pallas kernels  19.5 us (31%)
  waiting for transfers between devices  17 us (27%)
  local copies, waits for them, and re-layouts  0.95 us (2%)
  between operations  0.75 us (1%)
    pallas_call x9, Pallas kernels, call(): pl.pallas_call(kernel, out_shape=out_shape, in_specs=[SMEM] * smem + (spe...  19.5 us
    ppermute x15, waiting for transfers between devices, cross(): lax.ppermute(array, axis, [(i, i ^ bit) for i in range(lax.axis_size(axis...  16.1 us
    ppermute x15, starting transfers between devices, cross(): lax.ppermute(array, axis, [(i, i ^ bit) for i in range(lax.axis_size(axis...  12.1 us
    all_to_all x1, starting transfers between devices, per_device(): owned = lax.all_to_all(send, 'dp', split_axis=0, concat_axis=0, tiled=True)  7.26 us
    all_to_all x1, starting transfers between devices, per_device(): lax.all_to_all(sums, 'dp', split_axis=0, concat_axis=0, tiled=True)  4.52 us
  transfers between devices with their start and end apart: 17, of which 8 were waited for; matrix products, arithmetic and copies ran while one was open for 0% of the time, Pallas kernels for 25%

profile of v9, /device:TPU:0, one launch (start us, length us, event | category | flops | bytes accessed | tf_op | source)
XLA Modules:
  0.0 62.1 jit_solution(3118763119723255217)
XLA Ops:
  0.6 2.0 %shard_map.94 = (bf16[8,16,1920]{2,1,0:T(8,128)(2,1)}, s32[8]{0:T(128)S(1)}, s32[5]{0:T(128)S(1)}, bf16[512,512]{1,0:T(8,128)(2,1)S(1)}) custom-call(s32[1]{0:T(128)} %bitcast.me_ref, s32[32]{0:T(128)} %apb_ref.3, s32[40]{0:T(128)} %row_ref.3, bf16[5,16,1792]{2,1,0:T(8,128)(2,1)} %down_hbm.1, bf16[5,16,128]{2,1,0:T(8,128)(2,1)} %up_hbm.1, ...), custom_call_target="tpu_custom_call" | custom-call | tf_op jit(solution)/shard_map/pallas_call | solution.py:269
  2.6 7.3 %all-to-all-start = ((bf16[8,16,1920]{2,1,0:T(8,128)(2,1)}), bf16[8,16,1920]{2,1,0:T(8,128)(2,1)S(1)}, u32[]{:S(2)}, u32[]{:S(2)}) async-start(bf16[8,16,1920]{2,1,0:T(8,128)(2,1)} %get-tuple-element.42), calls=%async_computation | async-start | bytes 983040 | tf_op jit(solution)/shard_map/all_to_all | solution.py:340
  9.9 0.0 copy-start
  9.9 0.0 copy-start.2
  9.9 0.0 copy-start.3
  9.9 1.6 %collective-permute-start = (bf16[512,512]{1,0:T(8,128)(2,1)S(1)}, bf16[512,512]{1,0:T(8,128)(2,1)S(1)}, u32[]{:S(2)}, u32[]{:S(2)}) collective-permute-start(bf16[512,512]{1,0:T(8,128)(2,1)S(1)} %get-tuple-element.43), channel_id=1, source_target_pairs={{0,2},{1,3},{2,0},{3,1},{4,6},{5,7},{6,4},{7,5},{8,10},{9,11},{10,... | collective-permute-start | bytes 1572872 | tf_op jit(solution)/shard_map/ppermute | solution.py:309
  11.5 2.5 %shard_map.95 = (bf16[128,7168]{1,0:T(8,128)(2,1)S(1)}, f32[128,1792]{1,0:T(8,128)S(1)}) custom-call(bf16[128,7168]{1,0:T(8,128)(2,1)} %x_hbm, bf16[1792,512]{1,0:T(8,128)(2,1)} %w_hbm.7, bf16[128,512]{1,0:T(8,128)(2,1)} %dy_hbm.3), custom_call_target="tpu_custom_call" | custom-call | tf_op jit(solution)/shard_map/pallas_call | solution.py:269
  14.1 0.0 copy-start.1
  14.1 0.9 %copy-done.1 = f32[128,1792]{1,0:T(8,128)} copy-done((f32[128,1792]{1,0:T(8,128)}, f32[128,1792]{1,0:T(8,128)S(1)}, u32[]{:S(2)}) %copy-start.1) | copy-done | bytes 917528
  15.0 8.4 %collective-permute-done.y2_hbm = bf16[512,512]{1,0:T(8,128)(2,1)S(1)} collective-permute-done((bf16[512,512]{1,0:T(8,128)(2,1)S(1)}, bf16[512,512]{1,0:T(8,128)(2,1)S(1)}, u32[]{:S(2)}, u32[]{:S(2)}) %collective-permute-start) | collective-permute-done | bytes 524320 | tf_op jit(solution)/shard_map/ppermute | solution.py:309
  23.4 0.0 copy-start.4
  23.4 0.3 all-to-all-done.got_ref
  23.7 1.5 %collective-permute-start.8 = (bf16[512,512]{1,0:T(8,128)(2,1)S(1)}, bf16[512,512]{1,0:T(8,128)(2,1)}, u32[]{:S(2)}, u32[]{:S(2)}) collective-permute-start(bf16[512,512]{1,0:T(8,128)(2,1)S(1)} %collective-permute-done.y2_hbm), channel_id=1, source_target_pairs={{0,4},{4,0},{8,12},{12,8},{16,20},{20,16},{24,28},{28,24},{1,5},{5... | collective-permute-start | bytes 1572872 | tf_op jit(solution)/shard_map/ppermute | solution.py:309
  25.1 0.0 copy-done
  25.1 1.5 %collective-permute-start.4 = (bf16[128,512]{1,0:T(8,128)(2,1)S(1)}, bf16[128,512]{1,0:T(8,128)(2,1)S(1)}, u32[]{:S(2)}, u32[]{:S(2)}) collective-permute-start(bf16[128,512]{1,0:T(8,128)(2,1)S(1)} %copy-done), channel_id=1, source_target_pairs={{0,2},{1,3},{2,0},{3,1},{4,6},{5,7},{6,4},{7,5},{8,10},{9,11},{10,... | collective-permute-start | bytes 393224 | tf_op jit(solution)/shard_map/ppermute | solution.py:309
  26.7 0.0 copy-done.2
  26.7 0.0 copy-done.3
  26.7 0.6 shard_map.96
  27.3 0.6 collective-permute-start.2
  27.8 0.0 collective-permute-start.3
  27.8 1.6 %collective-permute-start.1 = (bf16[16,1920]{1,0:T(8,128)(2,1)S(1)}, bf16[16,1920]{1,0:T(8,128)(2,1)S(1)}, u32[]{:S(2)}, u32[]{:S(2)}) collective-permute-start(bf16[16,1920]{1,0:T(8,128)(2,1)S(1)} %get-tuple-element.50), channel_id=1, source_target_pairs={{0,1},{1,0},{2,3},{3,2},{4,5},{5,4},{6,7},{7,6},{8,9},{9,8},{10,11... | collective-permute-start | bytes 184328 | tf_op jit(solution)/shard_map/ppermute | solution.py:309
  29.5 1.0 %collective-permute-done.4.dy_ref = bf16[128,512]{1,0:T(8,128)(2,1)S(1)} collective-permute-done((bf16[128,512]{1,0:T(8,128)(2,1)S(1)}, bf16[128,512]{1,0:T(8,128)(2,1)S(1)}, u32[]{:S(2)}, u32[]{:S(2)}) %collective-permute-start.4) | collective-permute-done | bytes 131104 | tf_op jit(solution)/shard_map/ppermute | solution.py:309
  30.5 1.7 %collective-permute-done.2.refs_2_.fac2_ref = bf16[16,1920]{1,0:T(8,128)(2,1)S(1)} collective-permute-done((bf16[16,1920]{1,0:T(8,128)(2,1)S(1)}, bf16[16,1920]{1,0:T(8,128)(2,1)S(1)}, u32[]{:S(2)}, u32[]{:S(2)}) %collective-permute-start.2) | collective-permute-done | bytes 61472 | tf_op jit(solution)/shard_map/ppermute | solution.py:309
  32.1 0.0 collective-permute-done.3.refs_3_.fac3_ref
  32.1 0.0 collective-permute-done.1.refs_1_.fac1_ref
  32.1 1.3 %shard_map.97 = (bf16[16,2048]{1,0:T(8,128)(2,1)S(1)}, bf16[16,2048]{1,0:T(8,128)(2,1)S(1)}, bf16[16,2048]{1,0:T(8,128)(2,1)S(1)}, bf16[16,2048]{1,0:T(8,128)(2,1)S(1)}, bf16[128,16]{1,0:T(8,128)(2,1)S(1)}) custom-call(s32[1]{0:T(128)} %bitcast.1.at_ref, bf16[128,7168]{1,0:T(8,128)(2,1)S(1)} %get-tuple-element.47.x_ref, bf16[128,512]{1,0:T(8,128)(2,1)S(1)} %copy-done, ...), custom_call_target="tpu_custom_call" | custom-call | tf_op jit(solution)/shard_map/pallas_call | solution.py:269
  33.5 0.9 %collective-permute-start.5 = (bf16[16,2048]{1,0:T(8,128)(2,1)S(1)}, bf16[16,2048]{1,0:T(8,128)(2,1)S(1)}, u32[]{:S(2)}, u32[]{:S(2)}) collective-permute-start(bf16[16,2048]{1,0:T(8,128)(2,1)S(1)} %get-tuple-element.58), channel_id=1, source_target_pairs={{0,1},{1,0},{2,3},{3,2},{4,5},{5,4},{6,7},{7,6},{8,9},{9,8},{10,11... | collective-permute-start | bytes 196616 | tf_op jit(solution)/shard_map/ppermute | solution.py:309
  34.4 0.7 %collective-permute-start.6 = (bf16[16,2048]{1,0:T(8,128)(2,1)S(1)}, bf16[16,2048]{1,0:T(8,128)(2,1)S(1)}, u32[]{:S(2)}, u32[]{:S(2)}) collective-permute-start(bf16[16,2048]{1,0:T(8,128)(2,1)S(1)} %get-tuple-element.59), channel_id=1, source_target_pairs={{0,2},{1,3},{2,0},{3,1},{4,6},{5,7},{6,4},{7,5},{8,10},{9,11},{10,... | collective-permute-start | bytes 196616 | tf_op jit(solution)/shard_map/ppermute | solution.py:309
  35.1 0.7 %collective-permute-start.7 = (bf16[16,2048]{1,0:T(8,128)(2,1)S(1)}, bf16[16,2048]{1,0:T(8,128)(2,1)S(1)}, u32[]{:S(2)}, u32[]{:S(2)}) collective-permute-start(bf16[16,2048]{1,0:T(8,128)(2,1)S(1)} %get-tuple-element.60), channel_id=1, source_target_pairs={{0,3},{1,2},{2,1},{3,0},{4,7},{5,6},{6,5},{7,4},{8,11},{9,10},{10,... | collective-permute-start | bytes 196616 | tf_op jit(solution)/shard_map/ppermute | solution.py:309
  35.8 0.0 collective-permute-done.5.refs_1_
  35.8 3.4 %collective-permute-done.6.refs_2_.got_ref = bf16[16,2048]{1,0:T(8,128)(2,1)S(1)} collective-permute-done((bf16[16,2048]{1,0:T(8,128)(2,1)S(1)}, bf16[16,2048]{1,0:T(8,128)(2,1)S(1)}, u32[]{:S(2)}, u32[]{:S(2)}) %collective-permute-start.6) | collective-permute-done | bytes 65568 | tf_op jit(solution)/shard_map/ppermute | solution.py:309
  39.2 0.3 collective-permute-done.7.refs_3_.got_ref
  39.5 1.5 %shard_map.98 = bf16[8,16,1920]{2,1,0:T(8,128)(2,1)} custom-call(s32[1]{0:T(128)} %bitcast.1.at_ref, s32[1]{0:T(128)} %bitcast.me_ref, s32[32]{0:T(128)S(1)} %copy-done.2, s32[40]{0:T(128)S(1)} %copy-done.3, bf16[16,2048]{1,0:T(8,128)(2,1)S(1)} %get-tuple-element.62.refs_0_, bf16[16,2048]{1,0:T(8,128)(2,1)S(1)} %collective-permute-done.5.refs_1_, ...), custom_call_target="tpu_custom_call" | custom-call | tf_op jit(solution)/shard_map/pallas_call | solution.py:269
  41.0 0.0 collective-permute-done.8.x2_hbm
  41.0 0.4 collective-permute-start.14
  41.3 4.5 %all-to-all-start.1 = ((bf16[8,16,1920]{2,1,0:T(8,128)(2,1)}), bf16[8,16,1920]{2,1,0:T(8,128)(2,1)S(1)}, u32[]{:S(2)}, u32[]{:S(2)}) async-start(bf16[8,16,1920]{2,1,0:T(8,128)(2,1)} %shard_map.98), calls=%async_computation.1 | async-start | bytes 983040 | tf_op jit(solution)/shard_map/all_to_all | solution.py:407
  45.9 0.0 copy-done.4
  45.9 0.1 collective-permute-start.12
  45.9 0.5 collective-permute-start.13
  46.4 0.1 collective-permute-start.10
  46.5 1.7 %shard_map.99 = bf16[128,768]{1,0:T(8,128)(2,1)S(1)} custom-call(bf16[1792,512]{1,0:T(8,128)(2,1)} %w_hbm.7, bf16[128,512]{1,0:T(8,128)(2,1)S(1)} %collective-permute-done.4.dy_ref, bf16[16,1920]{1,0:T(8,128)(2,1)S(1)} %get-tuple-element.51.share_ref, bf16[16,2048]{1,0:T(8,128)(2,1)S(1)} %collective-permute-done.6.refs_2_.got_ref), custom_call_target="tpu_custom_call" | custom-call | tf_op jit(solution)/shard_map/pallas_call | solution.py:269
  48.2 1.1 %collective-permute-start.9 = (bf16[128,768]{1,0:T(8,128)(2,1)S(1)}, bf16[128,768]{1,0:T(8,128)(2,1)S(1)}, u32[]{:S(2)}, u32[]{:S(2)}) collective-permute-start(bf16[128,768]{1,0:T(8,128)(2,1)S(1)} %shard_map.99), channel_id=1, source_target_pairs={{0,2},{1,3},{2,0},{3,1},{4,6},{5,7},{6,4},{7,5},{8,10},{9,11},{10,... | collective-permute-start | bytes 589832 | tf_op jit(solution)/shard_map/ppermute | solution.py:309
  49.3 0.0 collective-permute-done.10.dy_ref
  49.3 1.7 %shard_map.100 = bf16[128,768]{1,0:T(8,128)(2,1)S(1)} custom-call(bf16[1792,512]{1,0:T(8,128)(2,1)} %w_hbm.7, bf16[128,512]{1,0:T(8,128)(2,1)S(1)} %collective-permute-done.10.dy_ref, bf16[16,1920]{1,0:T(8,128)(2,1)S(1)} %get-tuple-element.52.share_ref, bf16[16,2048]{1,0:T(8,128)(2,1)S(1)} %collective-permute-done.7.refs_3_.got_ref), custom_call_target="tpu_custom_call" | custom-call | tf_op jit(solution)/shard_map/pallas_call | solution.py:269
  51.0 0.8 %collective-permute-start.11 = (bf16[128,768]{1,0:T(8,128)(2,1)S(1)}, bf16[128,768]{1,0:T(8,128)(2,1)S(1)}, u32[]{:S(2)}, u32[]{:S(2)}) collective-permute-start(bf16[128,768]{1,0:T(8,128)(2,1)S(1)} %shard_map.100), channel_id=1, source_target_pairs={{0,3},{1,2},{2,1},{3,0},{4,7},{5,6},{6,5},{7,4},{8,11},{9,10},{10,... | collective-permute-start | bytes 589832 | tf_op jit(solution)/shard_map/ppermute | solution.py:309
  51.8 0.0 collective-permute-done.12.y3_hbm
  51.8 0.0 collective-permute-done.13.x3_hbm
  51.8 0.0 collective-permute-done.14.w1_hbm
  51.8 6.1 %shard_map.101.in_ref = bf16[128,7168]{1,0:T(8,128)(2,1)} custom-call(s32[1]{0:T(128)} %bitcast.1.at_ref, s32[1]{0:T(128)S(6)} %and.5.side_ref, bf16[128,16]{1,0:T(8,128)(2,1)S(1)} %get-tuple-element.69.back_ref, bf16[16,1920]{1,0:T(8,128)(2,1)S(1)} %get-tuple-element.53.refs_0_.fac0_ref, bf16[16,1920]{1,0:T(8,128)(2,1)S(1)} %collective-permute-done.1.refs_1_.fac1_ref, ...), custom_call_target="tpu_custom_call" | custom-call | tf_op jit(solution)/shard_map/pallas_call | solution.py:269
  58.0 0.0 collective-permute-done.9.z2_ref
  58.0 1.3 %collective-permute-done.11.z3_ref = bf16[128,768]{1,0:T(8,128)(2,1)S(1)} collective-permute-done((bf16[128,768]{1,0:T(8,128)(2,1)S(1)}, bf16[128,768]{1,0:T(8,128)(2,1)S(1)}, u32[]{:S(2)}, u32[]{:S(2)}) %collective-permute-start.11) | collective-permute-done | bytes 196640 | tf_op jit(solution)/shard_map/ppermute | solution.py:309
  59.3 0.7 %all-to-all-done.1.got_ref = bf16[8,16,1920]{2,1,0:T(8,128)(2,1)S(1)} async-done(((bf16[8,16,1920]{2,1,0:T(8,128)(2,1)}), bf16[8,16,1920]{2,1,0:T(8,128)(2,1)S(1)}, u32[]{:S(2)}, u32[]{:S(2)}) %all-to-all-start.1) | async-done | bytes 491552 | tf_op jit(solution)/shard_map/all_to_all | solution.py:407
  59.9 2.1 %shard_map.102 = (f32[5,16,1792]{2,1,0:T(8,128)}, f32[5,16,128]{2,1,0:T(8,128)}, bf16[128,7168]{1,0:T(8,128)(2,1)}) custom-call(s32[8]{0:T(128)S(1)} %get-tuple-element.40.want_ref, s32[5]{0:T(128)S(1)} %get-tuple-element.41.count_ref, s32[1]{0:T(128)} %bitcast.1.at_ref, ...), custom_call_target="tpu_custom_call", output_to_operand_aliasing={{2}: (6, {})} | custom-call | tf_op jit(solution)/shard_map/pallas_call | solution.py:269
Async XLA Ops:
  2.6 21.0 %all-to-all-start = ((bf16[8,16,1920]{2,1,0:T(8,128)(2,1)}), bf16[8,16,1920]{2,1,0:T(8,128)(2,1)S(1)}, u32[]{:S(2)}, u32[]{:S(2)}) async-start(bf16[8,16,1920]{2,1,0:T(8,128)(2,1)} %get-tuple-element.42), calls=%async_computation | async-start | bytes 983040 | tf_op jit(solution)/shard_map/all_to_all | solution.py:340
  9.9 15.3 %copy-start = (bf16[128,512]{1,0:T(8,128)(2,1)S(1)}, bf16[128,512]{1,0:T(8,128)(2,1)}, u32[]{:S(2)}) copy-start(bf16[128,512]{1,0:T(8,128)(2,1)} %dy_hbm.3) | copy-start | bytes 393220
  9.9 16.8 %copy-start.2 = (s32[32]{0:T(128)S(1)}, s32[32]{0:T(128)}, u32[]{:S(2)}) copy-start(s32[32]{0:T(128)} %apb_ref.3) | copy-start | bytes 388
  9.9 16.8 %copy-start.3 = (s32[40]{0:T(128)S(1)}, s32[40]{0:T(128)}, u32[]{:S(2)}) copy-start(s32[40]{0:T(128)} %row_ref.3) | copy-start | bytes 484
  9.9 13.4 %collective-permute-start = (bf16[512,512]{1,0:T(8,128)(2,1)S(1)}, bf16[512,512]{1,0:T(8,128)(2,1)S(1)}, u32[]{:S(2)}, u32[]{:S(2)}) collective-permute-start(bf16[512,512]{1,0:T(8,128)(2,1)S(1)} %get-tuple-element.43), channel_id=1, source_target_pairs={{0,2},{1,3},{2,0},{3,1},{4,6},{5,7},{6,4},{7,5},{8,10},{9,11},{10,... | collective-permute-start | bytes 1572872 | tf_op jit(solution)/shard_map/ppermute | solution.py:309
  14.1 0.9 %copy-start.1 = (f32[128,1792]{1,0:T(8,128)}, f32[128,1792]{1,0:T(8,128)S(1)}, u32[]{:S(2)}) copy-start(f32[128,1792]{1,0:T(8,128)S(1)} %get-tuple-element.72.own_hbm) | copy-start | bytes 2752516
  23.4 22.5 %copy-start.4 = (bf16[512,512]{1,0:T(8,128)(2,1)}, bf16[512,512]{1,0:T(8,128)(2,1)S(1)}, u32[]{:S(2)}) copy-start(bf16[512,512]{1,0:T(8,128)(2,1)S(1)} %collective-permute-done.y2_hbm) | copy-start | bytes 1572868
  23.7 17.3 %collective-permute-start.8 = (bf16[512,512]{1,0:T(8,128)(2,1)S(1)}, bf16[512,512]{1,0:T(8,128)(2,1)}, u32[]{:S(2)}, u32[]{:S(2)}) collective-permute-start(bf16[512,512]{1,0:T(8,128)(2,1)S(1)} %collective-permute-done.y2_hbm), channel_id=1, source_target_pairs={{0,4},{4,0},{8,12},{12,8},{16,20},{20,16},{24,28},{28,24},{1,5},{5... | collective-permute-start | bytes 1572872 | tf_op jit(solution)/shard_map/ppermute | solution.py:309
  25.1 5.3 %collective-permute-start.4 = (bf16[128,512]{1,0:T(8,128)(2,1)S(1)}, bf16[128,512]{1,0:T(8,128)(2,1)S(1)}, u32[]{:S(2)}, u32[]{:S(2)}) collective-permute-start(bf16[128,512]{1,0:T(8,128)(2,1)S(1)} %copy-done), channel_id=1, source_target_pairs={{0,2},{1,3},{2,0},{3,1},{4,6},{5,7},{6,4},{7,5},{8,10},{9,11},{10,... | collective-permute-start | bytes 393224 | tf_op jit(solution)/shard_map/ppermute | solution.py:309
  27.3 4.9 %collective-permute-start.2 = (bf16[16,1920]{1,0:T(8,128)(2,1)S(1)}, bf16[16,1920]{1,0:T(8,128)(2,1)S(1)}, u32[]{:S(2)}, u32[]{:S(2)}) collective-permute-start(bf16[16,1920]{1,0:T(8,128)(2,1)S(1)} %get-tuple-element.51.share_ref), channel_id=1, source_target_pairs={{0,2},{1,3},{2,0},{3,1},{4,6},{5,7},{6,4},{7,5},{8,10},{9,11},{10,... | collective-permute-start | bytes 184328 | tf_op jit(solution)/shard_map/ppermute | solution.py:309
  27.8 4.3 %collective-permute-start.3 = (bf16[16,1920]{1,0:T(8,128)(2,1)S(1)}, bf16[16,1920]{1,0:T(8,128)(2,1)S(1)}, u32[]{:S(2)}, u32[]{:S(2)}) collective-permute-start(bf16[16,1920]{1,0:T(8,128)(2,1)S(1)} %get-tuple-element.52.share_ref), channel_id=1, source_target_pairs={{0,3},{1,2},{2,1},{3,0},{4,7},{5,6},{6,5},{7,4},{8,11},{9,10},{10,... | collective-permute-start | bytes 184328 | tf_op jit(solution)/shard_map/ppermute | solution.py:309
  27.8 4.3 %collective-permute-start.1 = (bf16[16,1920]{1,0:T(8,128)(2,1)S(1)}, bf16[16,1920]{1,0:T(8,128)(2,1)S(1)}, u32[]{:S(2)}, u32[]{:S(2)}) collective-permute-start(bf16[16,1920]{1,0:T(8,128)(2,1)S(1)} %get-tuple-element.50), channel_id=1, source_target_pairs={{0,1},{1,0},{2,3},{3,2},{4,5},{5,4},{6,7},{7,6},{8,9},{9,8},{10,11... | collective-permute-start | bytes 184328 | tf_op jit(solution)/shard_map/ppermute | solution.py:309
  33.5 2.3 %collective-permute-start.5 = (bf16[16,2048]{1,0:T(8,128)(2,1)S(1)}, bf16[16,2048]{1,0:T(8,128)(2,1)S(1)}, u32[]{:S(2)}, u32[]{:S(2)}) collective-permute-start(bf16[16,2048]{1,0:T(8,128)(2,1)S(1)} %get-tuple-element.58), channel_id=1, source_target_pairs={{0,1},{1,0},{2,3},{3,2},{4,5},{5,4},{6,7},{7,6},{8,9},{9,8},{10,11... | collective-permute-start | bytes 196616 | tf_op jit(solution)/shard_map/ppermute | solution.py:309
  34.4 4.8 %collective-permute-start.6 = (bf16[16,2048]{1,0:T(8,128)(2,1)S(1)}, bf16[16,2048]{1,0:T(8,128)(2,1)S(1)}, u32[]{:S(2)}, u32[]{:S(2)}) collective-permute-start(bf16[16,2048]{1,0:T(8,128)(2,1)S(1)} %get-tuple-element.59), channel_id=1, source_target_pairs={{0,2},{1,3},{2,0},{3,1},{4,6},{5,7},{6,4},{7,5},{8,10},{9,11},{10,... | collective-permute-start | bytes 196616 | tf_op jit(solution)/shard_map/ppermute | solution.py:309
  35.1 4.4 %collective-permute-start.7 = (bf16[16,2048]{1,0:T(8,128)(2,1)S(1)}, bf16[16,2048]{1,0:T(8,128)(2,1)S(1)}, u32[]{:S(2)}, u32[]{:S(2)}) collective-permute-start(bf16[16,2048]{1,0:T(8,128)(2,1)S(1)} %get-tuple-element.60), channel_id=1, source_target_pairs={{0,3},{1,2},{2,1},{3,0},{4,7},{5,6},{6,5},{7,4},{8,11},{9,10},{10,... | collective-permute-start | bytes 196616 | tf_op jit(solution)/shard_map/ppermute | solution.py:309
  41.0 10.9 %collective-permute-start.14 = (bf16[1792,512]{1,0:T(8,128)(2,1)}, bf16[1792,512]{1,0:T(8,128)(2,1)}, u32[]{:S(2)}, u32[]{:S(2)}) collective-permute-start(bf16[1792,512]{1,0:T(8,128)(2,1)} %w_hbm.7), channel_id=1, source_target_pairs={{0,1},{1,0},{2,3},{3,2},{4,5},{5,4},{6,7},{7,6},{8,9},{9,8},{10,11... | collective-permute-start | bytes 5505032 | tf_op jit(solution)/shard_map/ppermute | solution.py:309
  41.3 18.6 %all-to-all-start.1 = ((bf16[8,16,1920]{2,1,0:T(8,128)(2,1)}), bf16[8,16,1920]{2,1,0:T(8,128)(2,1)S(1)}, u32[]{:S(2)}, u32[]{:S(2)}) async-start(bf16[8,16,1920]{2,1,0:T(8,128)(2,1)} %shard_map.98), calls=%async_computation.1 | async-start | bytes 983040 | tf_op jit(solution)/shard_map/all_to_all | solution.py:407
  45.9 6.0 %collective-permute-start.12 = (bf16[512,512]{1,0:T(8,128)(2,1)S(1)}, bf16[512,512]{1,0:T(8,128)(2,1)S(1)}, u32[]{:S(2)}, u32[]{:S(2)}) collective-permute-start(bf16[512,512]{1,0:T(8,128)(2,1)S(1)} %collective-permute-done.y2_hbm), channel_id=1, source_target_pairs={{0,1},{1,0},{2,3},{3,2},{4,5},{5,4},{6,7},{7,6},{8,9},{9,8},{10,11... | collective-permute-start | bytes 1572872 | tf_op jit(solution)/shard_map/ppermute | solution.py:309
  45.9 5.9 %collective-permute-start.13 = (bf16[512,512]{1,0:T(8,128)(2,1)}, bf16[512,512]{1,0:T(8,128)(2,1)S(1)}, u32[]{:S(2)}, u32[]{:S(2)}) collective-permute-start(bf16[512,512]{1,0:T(8,128)(2,1)} %collective-permute-done.8.x2_hbm), channel_id=1, source_target_pairs={{0,1},{1,0},{2,3},{3,2},{4,5},{5,4},{6,7},{7,6},{8,9},{9,8},{10,11... | collective-permute-start | bytes 1572872 | tf_op jit(solution)/shard_map/ppermute | solution.py:309
  46.4 2.9 %collective-permute-start.10 = (bf16[128,512]{1,0:T(8,128)(2,1)S(1)}, bf16[128,512]{1,0:T(8,128)(2,1)S(1)}, u32[]{:S(2)}, u32[]{:S(2)}) collective-permute-start(bf16[128,512]{1,0:T(8,128)(2,1)S(1)} %collective-permute-done.4.dy_ref), channel_id=1, source_target_pairs={{0,1},{1,0},{2,3},{3,2},{4,5},{5,4},{6,7},{7,6},{8,9},{9,8},{10,11... | collective-permute-start | bytes 393224 | tf_op jit(solution)/shard_map/ppermute | solution.py:309
  48.2 9.8 %collective-permute-start.9 = (bf16[128,768]{1,0:T(8,128)(2,1)S(1)}, bf16[128,768]{1,0:T(8,128)(2,1)S(1)}, u32[]{:S(2)}, u32[]{:S(2)}) collective-permute-start(bf16[128,768]{1,0:T(8,128)(2,1)S(1)} %shard_map.99), channel_id=1, source_target_pairs={{0,2},{1,3},{2,0},{3,1},{4,6},{5,7},{6,4},{7,5},{8,10},{9,11},{10,... | collective-permute-start | bytes 589832 | tf_op jit(solution)/shard_map/ppermute | solution.py:309
  51.0 8.3 %collective-permute-start.11 = (bf16[128,768]{1,0:T(8,128)(2,1)S(1)}, bf16[128,768]{1,0:T(8,128)(2,1)S(1)}, u32[]{:S(2)}, u32[]{:S(2)}) collective-permute-start(bf16[128,768]{1,0:T(8,128)(2,1)S(1)} %shard_map.100), channel_id=1, source_target_pairs={{0,3},{1,2},{2,1},{3,0},{4,7},{5,6},{6,5},{7,4},{8,11},{9,10},{10,... | collective-permute-start | bytes 589832 | tf_op jit(solution)/shard_map/ppermute | solution.py:309
